TPU v7x, 32 devices: a whole 2x2x4 slice. The times are simulated.
32 devices in a mesh: dp: 8 (over z, y), mp: 4 (over x, core).
Axes of the slice: x: 2, y: 2, z: 4, core: 2. Of those that a mesh axis runs over, the one named last changes fastest.
Arguments:
- hidden_in: bfloat16 [32768, 768], P('dp'), may hold values from -6 to 6
- incoming: bfloat16 [32768, 768], P('dp'), may hold values from -6 to 6
- spans: int32 [64, 24, 2], P('dp'), may hold values from 0 to 508, as said below
- owners: int32 [12], replicated, may hold values from 0 to 7, as said below
- vectors: float32 [12, 768], replicated, may hold values from -2 to 2
- vec_one: float32 [12, 768], replicated, may hold values from -144.81548 to 144.81548
- vec_two: float32 [12, 768], replicated, may hold values from 1310.72 to 5242.88
- master_slots: float32 [32, 768, 768], P('dp', None, 'mp'), may hold values from -0.9021098 to 0.9021098
- slot_one: float32 [32, 768, 768], P('dp', None, 'mp'), may hold values from -144.81548 to 144.81548
- slot_two: float32 [32, 768, 768], P('dp', None, 'mp'), may hold values from 1310.72 to 5242.88
Outputs:
- layer_out: bfloat16 [32768, 768], P('dp')
- input_grad: bfloat16 [32768, 768], P('dp')
- new_vectors: float32 [12, 768], replicated
- new_vec_one: float32 [12, 768], replicated
- new_vec_two: float32 [12, 768], replicated
- new_slots: float32 [32, 768, 768], P('dp', None, 'mp')
- new_slot_one: float32 [32, 768, 768], P('dp', None, 'mp')
- new_slot_two: float32 [32, 768, 768], P('dp', None, 'mp')
Inputs may be any that keep to these rules, and one draw needn't show every extreme that they name: Each span lies within its sequence: length 1 to 4, start + length <= 512; spans may intersect. `owners`: no index of dp owns more than 4 pieces; one owns exactly 4.
All inputs are finite; a program needn't handle non-finite values.
Results may differ from a plain program's by a relative error of at most 0.02.
Values may be sent and summed in bfloat16 or wider, within the bound.
A program may use at most 384 MiB of HBM per device.

v0:
```python
import jax
import jax.numpy as jnp
from jax import lax
from jax.sharding import PartitionSpec as P

HDIM = 64
LEN = 512
STEP = 10


HI = lax.Precision.HIGHEST
LN_EPS = 1e-12
MATRIX_RATE = 0.03
VECTOR_RATE = 0.25
BETA_ONE = 0.5
BETA_TWO = 0.5
DECAY = 0.01
ADAM_EPS = 1e-08


def layer_norm(value, gain, shift):
    center = value - jnp.mean(value, axis=-1, keepdims=True)
    inverse = lax.rsqrt(jnp.mean(center * center, axis=-1, keepdims=True) + LN_EPS)
    normed = center * inverse
    return (normed * gain + shift, normed, inverse)


def norm_back(grad, normed, inverse, gain):
    scaled = grad * gain
    first = jnp.mean(scaled, axis=-1, keepdims=True)
    second = jnp.mean(scaled * normed, axis=-1, keepdims=True)
    return inverse * (scaled - first - normed * second)


def gelu_slope(value):
    cdf = 0.5 * (1.0 + lax.erf(value * 2.0 ** (-0.5)))
    pdf = jnp.exp(-0.5 * value * value) * (2.0 * jnp.pi) ** (-0.5)
    return cdf + value * pdf


def adamw(weight, moment_one, moment_two, grad, step_rate):
    new_one = BETA_ONE * moment_one + (1.0 - BETA_ONE) * grad
    new_two = BETA_TWO * moment_two + (1.0 - BETA_TWO) * grad * grad
    corr_one = 1.0 - BETA_ONE**STEP
    corr_two = 1.0 - BETA_TWO**STEP
    direction = new_one / corr_one / (jnp.sqrt(new_two / corr_two) + ADAM_EPS)
    return (weight - step_rate * (direction + DECAY * weight), new_one, new_two)


def on_device(
    hidden_in, incoming, spans, owners, vectors, vec_one, vec_two, master_slots, slot_one, slot_two
):
    bf16 = jnp.bfloat16
    f32 = jnp.float32
    cap, width, share = master_slots.shape
    nmat = owners.shape[0]
    ratio = (nmat - 4) // 2
    units = ratio * share
    scale = HDIM ** (-0.5)
    rank_dp = lax.axis_index("dp")
    rank_mp = lax.axis_index("mp")
    index = jnp.arange(nmat, dtype=jnp.int32)
    earlier = index[None, :] < index[:, None]
    same = owners[:, None] == owners[None, :]
    slot_of = jnp.sum((same & earlier).astype(jnp.int32), axis=1)
    select = (
        (owners == rank_dp)[:, None]
        & (slot_of[:, None] == jnp.arange(cap, dtype=jnp.int32)[None, :])
    ).astype(f32)
    local_share = jnp.einsum("ps,sij->pij", select, master_slots, precision=HI).astype(bf16)
    pieces = lax.psum(local_share, "dp").astype(jnp.float32)
    weights = pieces.astype(bf16)
    w_query, w_key, w_value, w_out_t = (weights[0], weights[1], weights[2], weights[3])
    w_up = weights[4 : 4 + ratio].transpose(1, 0, 2).reshape(width, units)
    w_down_t = weights[4 + ratio : 4 + 2 * ratio].transpose(1, 0, 2).reshape(width, units)
    b_query = lax.dynamic_slice_in_dim(vectors[0], rank_mp * share, share, 0)
    b_value = lax.dynamic_slice_in_dim(vectors[1], rank_mp * share, share, 0)
    b_out = vectors[2]
    b_up = lax.dynamic_slice_in_dim(vectors[3 : 3 + ratio].reshape(-1), rank_mp * units, units, 0)
    b_down = vectors[3 + ratio]
    gain_one, shift_one = (vectors[4 + ratio], vectors[5 + ratio])
    gain_two, shift_two = (vectors[6 + ratio], vectors[7 + ratio])
    tokens = hidden_in.shape[0]
    nseq = tokens // LEN
    heads_dev = share // HDIM
    query = (jnp.dot(hidden_in, w_query, preferred_element_type=f32) + b_query).astype(bf16)
    keys = jnp.dot(hidden_in, w_key, preferred_element_type=f32).astype(bf16)
    values = (jnp.dot(hidden_in, w_value, preferred_element_type=f32) + b_value).astype(bf16)
    shape = (nseq, LEN, heads_dev, HDIM)
    q_seq, k_seq, v_seq = (query.reshape(shape), keys.reshape(shape), values.reshape(shape))

    def attend(block):
        q_blk, k_blk, v_blk = block
        scores = jnp.einsum("qhd,khd->hqk", q_blk, k_blk, preferred_element_type=f32) * scale
        top = jnp.max(scores, axis=-1, keepdims=True)
        total = jnp.sum(jnp.exp(scores - top), axis=-1, keepdims=True)
        logsum = top + jnp.log(total)
        probs = jnp.exp(scores - logsum).astype(bf16)
        mixed = jnp.einsum("hqk,khd->qhd", probs, v_blk, preferred_element_type=f32)
        return (mixed.astype(bf16), logsum[..., 0])

    context, logsums = lax.map(attend, (q_seq, k_seq, v_seq))
    context = context.reshape(tokens, share)
    part_attn = jnp.einsum("ts,os->to", context, w_out_t, preferred_element_type=f32)
    attn = lax.psum(part_attn, "mp") + b_out
    first, normed_one, inverse_one = layer_norm(hidden_in.astype(f32) + attn, gain_one, shift_one)
    first_low = first.astype(bf16)
    upper = jnp.dot(first_low, w_up, preferred_element_type=f32) + b_up
    active = jax.nn.gelu(upper, approximate=False).astype(bf16)
    part_down = jnp.einsum("tf,of->to", active, w_down_t, preferred_element_type=f32)
    down = lax.psum(part_down.astype(jnp.bfloat16), "mp").astype(jnp.float32) + b_down
    layer, normed_two, inverse_two = layer_norm(first + down, gain_two, shift_two)
    position = jnp.arange(LEN, dtype=jnp.int32)
    starts = spans[:, :, 0][:, :, None]
    ends = starts + spans[:, :, 1][:, :, None]
    covered = jnp.any(
        (position[None, None, :] >= starts) & (position[None, None, :] < ends), axis=1
    )
    cotangent = incoming.astype(f32) * covered.reshape(-1).astype(f32)[:, None]
    grad_gain_two = jnp.sum(cotangent * normed_two, axis=0)
    grad_shift_two = jnp.sum(cotangent, axis=0)
    grad_second = norm_back(cotangent, normed_two, inverse_two, gain_two)
    grad_down = grad_second.astype(bf16)
    grad_b_down = jnp.sum(grad_down.astype(f32), axis=0)
    grad_w_down = jnp.einsum("to,tf->of", grad_down, active, preferred_element_type=f32)
    grad_active = jnp.einsum("to,of->tf", grad_down, w_down_t, preferred_element_type=f32)
    grad_upper = (grad_active * gelu_slope(upper)).astype(bf16)
    grad_b_up = jnp.sum(grad_upper.astype(f32), axis=0)
    grad_w_up = jnp.einsum("td,tf->df", first_low, grad_upper, preferred_element_type=f32)
    part_first = jnp.einsum("tf,df->td", grad_upper, w_up, preferred_element_type=f32)
    grad_first = grad_second + lax.psum(part_first.astype(jnp.bfloat16), "mp").astype(jnp.float32)
    grad_gain_one = jnp.sum(grad_first * normed_one, axis=0)
    grad_shift_one = jnp.sum(grad_first, axis=0)
    grad_base = norm_back(grad_first, normed_one, inverse_one, gain_one)
    grad_attn = grad_base.astype(bf16)
    grad_b_out = jnp.sum(grad_attn.astype(f32), axis=0)
    grad_w_out = jnp.einsum("to,ts->os", grad_attn, context, preferred_element_type=f32)
    grad_context = jnp.einsum("to,os->ts", grad_attn, w_out_t, preferred_element_type=f32).astype(
        bf16
    )

    def attend_back(block):
        q_blk, k_blk, v_blk, d_blk, logsum = block
        scores = jnp.einsum("qhd,khd->hqk", q_blk, k_blk, preferred_element_type=f32) * scale
        probs = jnp.exp(scores - logsum[..., None])
        grad_probs = jnp.einsum("qhd,khd->hqk", d_blk, v_blk, preferred_element_type=f32)
        row_total = jnp.sum(probs * grad_probs, axis=-1, keepdims=True)
        grad_scores = (probs * (grad_probs - row_total)).astype(bf16)
        grad_q = jnp.einsum("hqk,khd->qhd", grad_scores, k_blk, preferred_element_type=f32) * scale
        grad_k = jnp.einsum("hqk,qhd->khd", grad_scores, q_blk, preferred_element_type=f32) * scale
        grad_v = jnp.einsum("hqk,qhd->khd", probs.astype(bf16), d_blk, preferred_element_type=f32)
        return (grad_q.astype(bf16), grad_k.astype(bf16), grad_v.astype(bf16))

    grad_query, grad_keys, grad_values = lax.map(
        attend_back, (q_seq, k_seq, v_seq, grad_context.reshape(shape), logsums)
    )
    grad_query = grad_query.reshape(tokens, share)
    grad_keys = grad_keys.reshape(tokens, share)
    grad_values = grad_values.reshape(tokens, share)
    grad_w_query = jnp.einsum("td,ts->ds", hidden_in, grad_query, preferred_element_type=f32)
    grad_w_key = jnp.einsum("td,ts->ds", hidden_in, grad_keys, preferred_element_type=f32)
    grad_w_value = jnp.einsum("td,ts->ds", hidden_in, grad_values, preferred_element_type=f32)
    grad_b_query = jnp.sum(grad_query.astype(f32), axis=0)
    grad_b_value = jnp.sum(grad_values.astype(f32), axis=0)
    part_input = jnp.einsum("ts,ds->td", grad_query, w_query, preferred_element_type=f32)
    part_input = part_input + jnp.einsum("ts,ds->td", grad_keys, w_key, preferred_element_type=f32)
    part_input = part_input + jnp.einsum(
        "ts,ds->td", grad_values, w_value, preferred_element_type=f32
    )
    grad_input = grad_base + lax.psum(part_input.astype(jnp.bfloat16), "mp").astype(jnp.float32)
    leader = (rank_mp == 0).astype(f32)
    row_query = lax.dynamic_update_slice_in_dim(
        jnp.zeros((width,), f32), grad_b_query, rank_mp * share, 0
    )
    row_value = lax.dynamic_update_slice_in_dim(
        jnp.zeros((width,), f32), grad_b_value, rank_mp * share, 0
    )
    rows_up = lax.dynamic_update_slice_in_dim(
        jnp.zeros((ratio * width,), f32), grad_b_up, rank_mp * units, 0
    )
    vec_grad = jnp.concatenate(
        [
            jnp.stack([row_query, row_value, leader * grad_b_out]),
            rows_up.reshape(ratio, width),
            leader
            * jnp.stack(
                [grad_b_down, grad_gain_one, grad_shift_one, grad_gain_two, grad_shift_two]
            ),
        ],
        axis=0,
    )
    vec_total = lax.psum(vec_grad, ("dp", "mp"))
    new_vectors, new_vec_one, new_vec_two = adamw(vectors, vec_one, vec_two, vec_total, VECTOR_RATE)
    grads = jnp.concatenate(
        [
            jnp.stack([grad_w_query, grad_w_key, grad_w_value, grad_w_out]),
            grad_w_up.reshape(width, ratio, share).transpose(1, 0, 2),
            grad_w_down.reshape(width, ratio, share).transpose(1, 0, 2),
        ],
        axis=0,
    )
    target = owners * cap + slot_of
    rows = jnp.arange(cap * lax.axis_size("dp"), dtype=jnp.int32)
    pick = (rows[:, None] == target[None, :]).astype(f32)
    slot_grad = lax.psum_scatter(
        jnp.einsum("rp,pij->rij", pick, grads, precision=HI).astype(jnp.bfloat16),
        "dp",
        scatter_dimension=0,
        tiled=True,
    ).astype(jnp.float32)
    occupied = jnp.sum(select, axis=0)[:, None, None]
    new_slots, new_slot_one, new_slot_two = adamw(
        master_slots, slot_one, slot_two, slot_grad, MATRIX_RATE
    )
    return (
        layer.astype(bf16),
        grad_input.astype(bf16),
        new_vectors,
        new_vec_one,
        new_vec_two,
        new_slots * occupied,
        new_slot_one * occupied,
        new_slot_two * occupied,
    )


def solution(mesh):
    placed = (
        P("dp", None),
        P("dp", None),
        P("dp", None, None),
        P(),
        P(),
        P(),
        P(),
        P("dp", None, "mp"),
        P("dp", None, "mp"),
        P("dp", None, "mp"),
    )
    return jax.shard_map(
        on_device,
        mesh=mesh,
        in_specs=placed,
        out_specs=(
            P("dp", None),
            P("dp", None),
            P(),
            P(),
            P(),
            P("dp", None, "mp"),
            P("dp", None, "mp"),
            P("dp", None, "mp"),
        ),
        check_vma=False,
    )
```

profile of v0, /device:TPU:0, one launch (start us, length us, event | category | flops | bytes accessed | tf_op | source)
XLA Modules:
  0.0 1277.3 jit_solution(18019133437601693149)
XLA Ops:
  9.4 8.4 convolution_convert_fusion.5
  19.2 171.2 %all-reduce.6.cloned.1.call-done = bf16[12,768,192]{1,0,2:T(8,128)(2,1)} async-done(((bf16[12,768,192]{1,0,2:T(8,128)(2,1)}), bf16[12,768,192]{1,0,2:T(8,128)(2,1)}) %all-reduce.6.cloned.1.call-update) | async-done | bytes 3538960 | tf_op jit(solution)/shard_map/psum | solution.py:71
  190.4 6.5 fusion.124
  196.9 5.6 fusion.78
  212.9 32.6 %while.26 = (s32[]{:T(128)}, bf16[8,512,3,64]{1,3,2,0:T(8,128)(2,1)}, f32[8,3,512]{2,1,0:T(4,128)}, bf16[8,512,3,64]{1,3,2,0:T(8,128)(2,1)}, bf16[8,512,3,64]{1,...) while((s32[]{:T(128)}, bf16[8,512,3,64]{1,3,2,0:T(8,128)(2,1)}, ...), condition=%wide.region_5.6_spmd, body=%wide.region_2.5_spmd.sunk | while | flops 207714816 | bytes 10277453 | solution.py:102
  218.7 2.3 fusion.169
  222.8 2.3 fusion.169
  226.8 2.3 fusion.169
  230.9 2.3 fusion.169
  239.0 2.3 fusion.169
  243.1 2.3 fusion.169
  245.5 3.4 copy.107
  250.7 6.3 fusion.87
  257.3 3.3 slice_bitcast_fusion
  261.8 215.1 %all-reduce.8.cloned.1.call-done = f32[4096,768]{1,0:T(8,128)} async-done(((f32[4096,768]{1,0:T(8,128)}), f32[4096,768]{1,0:T(8,128)}) %all-reduce.8.cloned.1.call-update) | async-done | bytes 12582928 | tf_op jit(solution)/shard_map/psum | solution.py:105
  476.9 7.4 fusion.123
  485.8 3.1 copy-done
  488.9 2.5 fusion.77
  491.4 32.8 %fusion.60 = (bf16[4096,768]{1,0:T(8,128)(2,1)S(1)}, f32[4096,768]{1,0:T(8,128)}) fusion(f32[768]{0:T(1024)S(1)} %dynamic_slice.37, bf16[4096,768]{1,0:T(8,128)(2,1)S(1)} %fusion.77, bf16[768,768]{0,1:T(8,128)(2,1)S(1)} %bitcast.258), kind=kOutput, calls=%fused_computation.66 | convolution fusion | flops 5039456256 | bytes 26348544 | tf_op jit(solution)/shard_map/dot_general | solution.py:108
  524.3 2.6 copy-done.44
  526.8 6.9 convolution_convert_fusion.2
  534.7 119.1 %all-reduce.10.cloned.1.call-done = bf16[4096,768]{1,0:T(8,128)(2,1)} async-done(((bf16[4096,768]{1,0:T(8,128)(2,1)}), bf16[4096,768]{1,0:T(8,128)(2,1)}) %all-reduce.10.cloned.1.call-update) | async-done | bytes 6291472 | tf_op jit(solution)/shard_map/psum | solution.py:111
  653.8 8.7 fusion.122
  664.0 8.2 multiply_reduce_fusion.2
  672.2 9.2 subtract_multiply_fusion.1
  681.4 13.6 %convert_reduce_fusion.1 = (f32[768]{0:T(1024)}, bf16[4096,768]{1,0:T(8,128)(2,1)S(1)}) fusion(f32[4096,768]{1,0:T(8,128)} %get-tuple-element.247, f32[768]{0:T(1024)S(1)} %dynamic_slice.37, bf16[768,768]{0,1:T(8,128)(2,1)S(1)} %bitcast.261, f32[4096,768]{1,0:T(8,128)} %get-tuple-element.231), kind=kOutput, calls=%fused_computation.76 | convolution fusion | flops 4875877376 | bytes 32643072 | tf_op jit(solution)/shard_map/to,of->tf/dot_general | solution.py:126
  695.0 2.6 copy-done.45
  697.5 6.9 convolution_convert_fusion.1
  705.1 13.1 %fusion.117 = f32[768,768]{0,1:T(8,128)} fusion(bf16[4096,768]{1,0:T(8,128)(2,1)} %copy-done.44, f32[4096,768]{1,0:T(8,128)} %get-tuple-element.231), kind=kOutput, calls=%fused_computation.204 | convolution fusion | flops 4834983936 | bytes 21233664 | tf_op jit(solution)/shard_map/to,tf->of/dot_general | solution.py:125
  718.2 106.2 %all-reduce.12.cloned.1.call-done = bf16[4096,768]{1,0:T(8,128)(2,1)} async-done(((bf16[4096,768]{1,0:T(8,128)(2,1)}), bf16[4096,768]{1,0:T(8,128)(2,1)}) %all-reduce.12.cloned.1.call-update) | async-done | bytes 6291472 | tf_op jit(solution)/shard_map/psum | solution.py:131
  824.4 18.1 %multiply_reduce_fusion.3 = (f32[768]{0:T(1024)S(1)}, f32[4096]{0:T(1024)S(1)}, f32[4096]{0:T(1024)S(1)}, f32[768]{0:T(1024)S(1)}, f32[768]{0:T(1024)S(1)}) fusion(f32[4096,768]{1,0:T(8,128)} %copy-done, f32[4096]{0:T(1024)S(1)} %add_rsqrt_fusion.1, f32[4096]{0:T(1024)S(1)} %broadcast_multiply_fusion.6, f32[4096,768]{1,0:T(8,128)} %get-tuple-element.231, ...), kind=kLoop, calls=%fused_computation.74 | loop fusion | flops 44029696 | bytes 31535104 | tf_op jit(solution)/shard_map/reduce_sum | solution.py:132
  842.6 10.9 convert_reduce_fusion.2
  855.7 2.4 copy-done.1
  862.0 81.6 %while.27 = (s32[]{:T(128)}, bf16[8,512,3,64]{1,3,2,0:T(8,128)(2,1)S(1)}, bf16[8,512,3,64]{1,3,2,0:T(8,128)(2,1)}, bf16[8,512,3,64]{1,3,2,0:T(8,128)(2,1)S(1)}, ...) while((s32[]{:T(128)}, ...), condition=%wide.region_20.21_spmd, body=%wide.region_18.20_spmd.sunk | while | flops 513243648 | bytes 25609320 | solution.py:154
  948.2 6.3 fusion.89
  954.6 6.5 fusion.92
  961.0 12.9 %add_convert_fusion.1 = bf16[4096,768]{1,0:T(8,128)(2,1)} fusion(f32[4096,768]{1,0:T(8,128)} %fusion.92, f32[4096,768]{1,0:T(8,128)} %fusion.89, bf16[4096,192]{0,1:T(8,128)(2,1)S(1)} %bitcast.243, bf16[1,768,192]{1,0,2:T(2,128)(2,1)S(1)} %copy-done.22), kind=kOutput, calls=%fused_computation.79 | convolution fusion | flops 1217396736 | bytes 33325056 | tf_op jit(solution)/shard_map/ts,ds->td/dot_general | solution.py:167
  974.1 9.4 fusion.126
  983.5 2.9 copy.177
  986.4 2.9 copy.178
  989.4 6.3 convolution_bitcast_fusion
  1005.7 24.6 %concatenate.7 = f32[12,768,192]{1,0,2:T(8,128)} concatenate(f32[1,768,192]{1,0,2:T(1,128)} %copy.119, f32[1,768,192]{1,0,2:T(1,128)} %copy.120, f32[1,768,192]{1,0,2:T(1,128)} %copy.121, f32[1,768,192]{1,0,2:T(1,128)} %copy.122, f32[4,768,192]{1,0,2:T(4,128)} %bitcast.238, f32[4,768,192]{1,0,2:T(4,128)} %bitcast.237), dimensions={0} | concatenate | bytes 14155776 | tf_op jit(solution)/shard_map/concatenate | solution.py:194
  1030.2 12.6 convolution_convert_fusion
  1042.9 12.8 %copy.123 = bf16[32,768,192]{1,2,0:T(8,128)(2,1)} copy(bf16[32,768,192]{1,0,2:T(8,128)(2,1)} %convolution_convert_fusion) | data formatting | bytes 18874368 | tf_op jit(solution)/shard_map/convert_element_type | solution.py:206
  1058.3 40.8 %psum.47 = f32[12,768]{1,0:T(8,128)S(1)} all-reduce(f32[12,768]{1,0:T(8,128)S(1)} %concatenate.6), channel_id=1, replica_groups=mesh['dp'=8,'mp'=4] {'dp','mp'}, use_global_device_ids=true, to_apply=%region_31.32 | all-reduce | flops 9216 | bytes 73728 | tf_op jit(solution)/shard_map/psum | solution.py:192
  1099.8 11.2 add_convert_fusion
  1111.0 151.0 %reduce-scatter.2.cloned.1.call-done = bf16[4,768,192]{1,2,0:T(8,128)(2,1)} async-done(((bf16[32,768,192]{1,2,0:T(8,128)(2,1)}), bf16[4,768,192]{1,2,0:T(8,128)(2,1)}) %reduce-scatter.2.cloned.1.call-update) | async-done | bytes 1179664 | tf_op jit(solution)/shard_map/reduce_scatter | solution.py:205
  1262.0 8.3 fusion.83
  (270 shorter events, 145.2 us)
Async XLA Ops:
  7.2 11.3 copy-start.27
  7.2 183.2 %all-reduce.6.cloned.1.call-start = ((), (), s32[]{:S(2)}) async-start(), calls=%async_computation.1 | async-start | bytes 9437184 | tf_op jit(solution)/shard_map/psum | solution.py:71
  17.9 459.1 %all-reduce.8.cloned.1.call-start = ((), (), s32[]{:S(2)}) async-start(), calls=%async_computation.2 | async-start | bytes 25165824 | tf_op jit(solution)/shard_map/psum | solution.py:105
  196.9 8.0 copy-start.21
  196.9 8.0 copy-start.23
  196.9 11.4 copy-start.17
  196.9 8.0 slice-start
  196.9 8.0 slice-start.1
  245.5 11.6 copy-start.5
  245.5 11.6 copy-start.6
  245.5 5.2 copy-start.19
  249.6 1.1 copy-start.3
  257.1 396.6 %all-reduce.10.cloned.1.call-start = ((), (), s32[]{:S(2)}) async-start(), calls=%async_computation.3 | async-start | bytes 12582912 | tf_op jit(solution)/shard_map/psum | solution.py:111
  484.3 4.6 copy-start
  491.4 32.8 %copy-start.15 = (bf16[4096,768]{1,0:T(8,128)(2,1)}, bf16[4096,768]{1,0:T(8,128)(2,1)S(1)}, u32[]{:S(2)}) copy-start(bf16[4096,768]{1,0:T(8,128)(2,1)S(1)} %fusion.77) | copy-start | bytes 18874372
  491.4 35.4 %copy-start.25 = (bf16[768,4,192]{0,2,1:T(8,128)(2,1)S(1)}, bf16[768,4,192]{0,2,1:T(8,128)(2,1)}, u32[]{:S(2)}) copy-start(bf16[768,4,192]{0,2,1:T(8,128)(2,1)} %copy.109) | copy-start | bytes 3538948
  524.3 2.6 copy-start.44
  533.8 120.0 %copy-start.33 = (f32[768]{0:T(1024)S(1)}, f32[768]{0:T(1024)}, u32[]{:S(2)}) copy-start(f32[768]{0:T(1024)} %get-tuple-element.181) | copy-start | bytes 9220
  533.8 290.6 %all-reduce.12.cloned.1.call-start = ((), (), s32[]{:S(2)}) async-start(), calls=%async_computation.4 | async-start | bytes 12582912 | tf_op jit(solution)/shard_map/psum | solution.py:131
  662.5 1.5 copy-start.31
  663.9 8.2 copy-start.32
  672.1 9.2 copy-start.26
  695.0 2.6 copy-start.45
  704.5 395.3 %all-reduce.14.cloned.1.call-start = ((), (), s32[]{:S(2)}) async-start(), calls=%async_computation.5 | async-start | bytes 12582912 | tf_op jit(solution)/shard_map/psum | solution.py:170
  824.4 18.1 %copy-start.2 = (bf16[4096,768]{1,0:T(8,128)(2,1)S(1)}, bf16[4096,768]{1,0:T(8,128)(2,1)}, u32[]{:S(2)}) copy-start(bf16[4096,768]{1,0:T(8,128)(2,1)} %all-reduce.12.cloned.1.call-done) | copy-start | bytes 18874372
  842.6 10.9 copy-start.20
  853.4 4.6 copy-start.1
  943.5 1.6 copy-start.14
  945.1 9.5 copy-start.8
  945.1 3.1 copy-start.18
  946.6 7.9 copy-start.10
  948.2 12.9 %copy-start.12 = (bf16[24,8,8,512]{3,1,2,0:T(8,128)(2,1)}, bf16[24,8,8,512]{3,1,2,0:T(8,128)(2,1)S(1)}, u32[]{:S(2)}) copy-start(bf16[24,8,8,512]{3,1,2,0:T(8,128)(2,1)S(1)} %copy.140) | copy-start | bytes 4718596
  948.2 6.4 copy-start.24
  954.6 6.5 copy-start.22
  974.0 288.0 %reduce-scatter.2.cloned.1.call-start = ((), (), s32[]{:S(2)}) async-start(), calls=%async_computation.6 | async-start | bytes 10616832 | tf_op jit(solution)/shard_map/reduce_scatter | solution.py:205
  974.0 9.4 copy-start.16
  983.5 5.9 copy-start.4
  983.5 13.6 %slice-start.2 = ((s8[6291456]{0:T(1024)(128)(4,1)}), s8[4194304]{0:T(1024)(128)(4,1)S(1)}, s32[]{:S(2)}) async-start(s8[6291456]{0:T(1024)(128)(4,1)} %bitcast.232), calls=%async_computation.9 | async-start | bytes 8388608
  989.4 7.8 slice-start.3
  989.4 7.8 copy-start.9
  997.1 2.9 copy-start.11
  1000.0 2.8 copy-start.13
  1055.7 0.8 copy-start.34
  1055.7 0.8 copy-start.37
  1055.7 43.3 %copy-start.28 = (f32[12,768]{1,0:T(8,128)S(1)}, f32[12,768]{1,0:T(8,128)}, u32[]{:S(2)}) copy-start(f32[12,768]{1,0:T(8,128)} %param.18) | copy-start | bytes 110596
  1055.8 43.3 %copy-start.29 = (f32[12,768]{1,0:T(8,128)S(1)}, f32[12,768]{1,0:T(8,128)}, u32[]{:S(2)}) copy-start(f32[12,768]{1,0:T(8,128)} %param.19) | copy-start | bytes 110596
  1055.8 43.3 %copy-start.30 = (f32[12,768]{1,0:T(8,128)S(1)}, f32[12,768]{1,0:T(8,128)}, u32[]{:S(2)}) copy-start(f32[12,768]{1,0:T(8,128)} %param.20) | copy-start | bytes 110596
  1099.8 162.2 %copy-start.7 = (f32[4,768,192]{1,2,0:T(8,128)S(1)}, f32[4,768,192]{1,2,0:T(8,128)}, u32[]{:S(2)}) copy-start(f32[4,768,192]{1,2,0:T(8,128)} %param.21) | copy-start | bytes 7077892
  (8 other events, 5.3 us)
Sparse Core Ops, SparseCore 0:
  18.0 172.3 all-reduce.5
  257.2 219.6 all-reduce.7
  533.9 119.7 all-reduce.9
  704.6 119.7 all-reduce.11
  974.1 120.6 all-reduce.13
  1098.3 163.6 reduce-scatter.1
where the time goes:
time: 1280 us
  waiting for transfers between devices  763 us (60%)
  matrix products  250 us (20%)
  other arithmetic  107 us (8%)
  local copies, waits for them, and re-layouts  100 us (8%)
  blocking collectives  40.8 us (3%)
  between operations  15.1 us (1%)
    psum x1, waiting for transfers between devices, on_device(): attn = lax.psum(part_attn, 'mp') + b_out  215 us
    psum x1, waiting for transfers between devices, on_device(): pieces = lax.psum(local_share, 'dp').astype(jnp.float32)  171 us
    reduce_scatter x1, waiting for transfers between devices, on_device(): lax.psum_scatter(jnp.einsum('rp,pij->rij', pick, grads, precision=HI).ast...  151 us
    psum x1, waiting for transfers between devices, on_device(): lax.psum(part_down.astype(jnp.bfloat16), 'mp').astype(jnp.float32) + b_down  119 us
    psum x1, waiting for transfers between devices, on_device(): lax.psum(part_first.astype(jnp.bfloat16), 'mp').astype(jnp.float32)  106 us
    psum x1, blocking collectives, on_device(): vec_total = lax.psum(vec_grad, ('dp', 'mp'))  40.8 us
    dot_general x1, matrix products, on_device(): upper = jnp.dot(first_low, w_up, preferred_element_type=f32) + b_up  32.8 us
  transfers between devices with their start and end apart: 6, of which 5 were waited for; matrix products, arithmetic and copies ran while one was open for 9% of the time, Pallas kernels for 0%

commit v1 on v0

v1 whole, which is shorter than its diff:
```python
import functools
import jax
import jax.numpy as jnp
from jax import lax
from jax.sharding import PartitionSpec as P
from jax.experimental import pallas as pl
from jax.experimental.pallas import tpu as pltpu

MESH = pl.DeviceIdType.MESH


def place():
    dp, mp = lax.axis_index("dp"), lax.axis_index("mp")
    return dp // 2, dp % 2, mp // 2, mp % 2


def device(z, y, x, c):
    return (z * 2 + y, x * 2 + c)


def greet(line):
    z, y, x, c = place()
    bar = pltpu.get_barrier_semaphore()
    for who in (device(z, 1 - y, x, c), device(z, y, 1 - x, c), device(z, y, x, 1 - c)):
        pl.semaphore_signal(bar, inc=1, device_id=who, device_id_type=MESH)

    @pl.when(z > 0)
    def _():
        pl.semaphore_signal(bar, inc=1, device_id=device(z - 1, y, x, c), device_id_type=MESH)

    @pl.when(z < line - 1)
    def _():
        pl.semaphore_signal(bar, inc=1, device_id=device(z + 1, y, x, c), device_id_type=MESH)

    peers = 3 + jnp.where(z > 0, 1, 0) + jnp.where(z < line - 1, 1, 0)
    pl.semaphore_wait(bar, peers.astype(jnp.int32))


def rcopy(src, dst, send, recv, who):
    return pltpu.make_async_remote_copy(
        src_ref=src, dst_ref=dst, send_sem=send, recv_sem=recv, device_id=who, device_id_type=MESH
    )


def gather_kernel(line, nmat, cap, owners, slots, out, full, ys, fr, fl, zo, idx, slot_sem,
                  sr, rl, sl, rr, xs, xr, ysd, yr, ds, dr, cs, cr, loc):
    share = slots.shape[1]
    quarter = share // 2
    half = quarter // 2
    nchunk = 2 * nmat
    z, y, x, c = place()
    me = 2 * x + c
    over = 2 * (1 - x) + c
    to_y, to_x, to_c = device(z, 1 - y, x, c), device(z, y, 1 - x, c), device(z, y, x, 1 - c)
    greet(line)
    slot_copy = rcopy(
        slots.at[:, pl.ds(pl.multiple_of((1 - y) * quarter, 16), quarter), :],
        ys.at[pl.ds(y * cap, cap)], slot_sem.at[0], slot_sem.at[1], to_y)
    slot_copy.start()
    for p in range(nmat):
        mine = owners[p]
        place_of = jnp.int32(0)
        for q in range(p):
            place_of += jnp.where(owners[q] == mine, 1, 0).astype(jnp.int32)
        zo[p] = mine // 2
        idx[p] = (mine % 2) * cap + jnp.minimum(place_of, cap - 1)
    ys[pl.ds(y * cap, cap)] = slots[:, pl.ds(pl.multiple_of(y * quarter, 16), quarter), :]
    slot_copy.wait()

    def rows(block, yy, h):
        return pl.ds(pl.multiple_of(block * share + yy * quarter + h * half, 16), half)

    def own(r):
        return ys[idx[r // 2], pl.ds(pl.multiple_of((r % 2) * half, 16), half), :]

    def right(r):
        return rcopy(fr.at[r], fr.at[r], sr.at[r], rl.at[r], device(z + 1, y, x, c))

    def left(r):
        return rcopy(fl.at[r], fl.at[r], sl.at[r], rr.at[r], device(z - 1, y, x, c))

    def x_copy(f):
        at = full.at[f // 2, rows(me, y, f % 2), :]
        return rcopy(at, at, xs.at[f], xr.at[f], to_x)

    def x_came(f):
        at = full.at[f // 2, rows(over, y, f % 2), :]
        return rcopy(at, at, xs.at[f], xr.at[f], to_x)

    def y_copy(f):
        at = full.at[f // 2, rows(me, y, f % 2), :]
        return rcopy(at, at, ysd.at[f], yr.at[f], to_y)

    def y_came(f):
        at = full.at[f // 2, rows(me, 1 - y, f % 2), :]
        return rcopy(at, at, ysd.at[f], yr.at[f], to_y)

    def diag_x(f):
        at = full.at[f // 2, rows(me, 1 - y, f % 2), :]
        return rcopy(at, at, ds.at[f], dr.at[f], to_x)

    def diag_y(f):
        at = full.at[f // 2, rows(over, y, f % 2), :]
        return rcopy(at, at, ds.at[f], dr.at[f], to_y)

    def diag_came(f):
        at = full.at[f // 2, rows(over, 1 - y, f % 2), :]
        return rcopy(at, at, ds.at[f], dr.at[f], to_x)

    def core_copy(p, k):
        block = jnp.where(k == 0, me, over) if not isinstance(k, int) else (me, over)[k]
        at = full.at[p, pl.ds(pl.multiple_of(block * share, 16), share), :]
        return rcopy(at, at, cs.at[p, k], cr.at[p, k], to_c)

    def core_came(p, k):
        block = (2 * x + 1 - c, 2 * (1 - x) + 1 - c)[k]
        at = full.at[p, pl.ds(pl.multiple_of(block * share, 16), share), :]
        return rcopy(at, at, cs.at[p, k], cr.at[p, k], to_c)

    def keep(p):
        return pltpu.make_async_copy(full.at[p], out.at[p], loc.at[p])

    lag0 = 2 * (line - 1)
    lag1 = lag0 + 2
    lag2 = lag1 + 3
    lag3 = lag2 + 1

    def tick(t):
        r = t - 2 * z

        @pl.when((r >= 0) & (r < nchunk))
        def _():
            @pl.when(z == 0)
            def _():
                fr[r] = own(r)

            @pl.when(z > 0)
            def _():
                right(r).wait_recv()
                fr[r] = jnp.where(zo[r // 2] == z, own(r), fr[r])

            @pl.when(z < line - 1)
            def _():
                right(r).start()

        l = t - 2 * (line - 1 - z)

        @pl.when((l >= 0) & (l < nchunk))
        def _():
            @pl.when(z == line - 1)
            def _():
                fl[l] = own(l)

            @pl.when(z < line - 1)
            def _():
                left(l).wait_recv()
                fl[l] = jnp.where(zo[l // 2] == z, own(l), fl[l])

            @pl.when(z > 0)
            def _():
                left(l).start()

        f = t - lag0

        @pl.when((f >= 0) & (f < nchunk))
        def _():
            full[f // 2, rows(me, y, f % 2), :] = jnp.where(zo[f // 2] <= z, fr[f], fl[f])
            x_copy(f).start()
            y_copy(f).start()

        g = t - lag1

        @pl.when((g >= 0) & (g < nchunk))
        def _():
            x_came(g).wait_recv()
            y_came(g).wait_recv()

            @pl.when(g % 2 == 0)
            def _():
                diag_x(g).start()

            @pl.when(g % 2 == 1)
            def _():
                diag_y(g).start()

        e = t - lag2

        @pl.when((e >= 0) & (e < nchunk))
        def _():
            diag_came(e).wait_recv()

            @pl.when(e % 2 == 1)
            def _():
                for k in range(2):
                    core_copy(e // 2, k).start()

        w = t - lag3

        @pl.when((w >= 0) & (w < nchunk) & (w % 2 == 1))
        def _():
            for k in range(2):
                core_came(w // 2, k).wait_recv()
            keep(w // 2).start()

    def body(t, carry):
        tick(t)
        return carry

    lax.fori_loop(0, nchunk + lag3, body, 0)

    def finish(r, carry):
        @pl.when(z < line - 1)
        def _():
            right(r).wait_send()

        @pl.when(z > 0)
        def _():
            left(r).wait_send()

        x_copy(r).wait_send()
        y_copy(r).wait_send()
        diag_came(r).wait_send()
        return carry

    lax.fori_loop(0, nchunk, finish, 0)

    def last(p, carry):
        for k in range(2):
            core_copy(p, k).wait_send()
        keep(p).wait()
        return carry

    lax.fori_loop(0, nmat, last, 0)


def gather_weights(owners, slots, line):
    cap, share, width = slots.shape
    nmat = owners.shape[0]
    quarter, half = share // 2, share // 4
    n = 2 * nmat
    bf16 = jnp.bfloat16
    dma = pltpu.SemaphoreType.DMA
    return pl.pallas_call(
        functools.partial(gather_kernel, line, nmat, cap),
        out_shape=jax.ShapeDtypeStruct((nmat, 4 * share, width), bf16),
        in_specs=[pl.BlockSpec(memory_space=pltpu.SMEM), pl.BlockSpec(memory_space=pltpu.VMEM)],
        out_specs=pl.BlockSpec(memory_space=pl.ANY),
        scratch_shapes=[
            pltpu.VMEM((nmat, 4 * share, width), bf16),
            pltpu.VMEM((2 * cap, quarter, width), bf16),
            pltpu.VMEM((n, half, width), bf16),
            pltpu.VMEM((n, half, width), bf16),
            pltpu.SMEM((nmat,), jnp.int32),
            pltpu.SMEM((nmat,), jnp.int32),
            dma((2,)),
        ] + [dma((n,))] * 10 + [dma((nmat, 2)), dma((nmat, 2)), dma((nmat,))],
        name="gather_weights",
        compiler_params=pltpu.CompilerParams(
            collective_id=1, has_side_effects=True, vmem_limit_bytes=56 * 1024 * 1024),
    )(owners, slots)


def reduce_kernel(line, order, cap, owners, grads, out, cin, hold, yo, yi, fr, fl, to, do, di,
                  who, pick, cs, cr, ysd, yr, sr, rl, sl, rr, dsem):
    nmat = len(order)
    share = grads.shape[1] // 2
    quarter = share // 2
    f32, bf16 = jnp.float32, jnp.bfloat16
    z, y, x, c = place()
    to_y, to_c = device(z, 1 - y, x, c), device(z, y, x, 1 - c)
    greet(line)

    for s in range(2 * cap):
        pick[s] = 0
    for j, p in enumerate(order):
        mine = owners[p]
        place_of = jnp.int32(0)
        for q in range(p):
            place_of += jnp.where(owners[q] == mine, 1, 0).astype(jnp.int32)
        who[j] = mine // 2
        slot = (mine % 2) * cap + jnp.minimum(place_of, cap - 1)
        for s in range(2 * cap):
            pick[s] = jnp.where((mine // 2 == z) & (slot == s), j, pick[s])

    def rows(start, size):
        return pl.ds(pl.multiple_of(start, 16), size)

    def core_copy(j):
        return rcopy(grads.at[j, rows((1 - c) * share, share), :], cin.at[j], cs.at[j], cr.at[j], to_c)

    def y_copy(j):
        return rcopy(yo.at[j], yi.at[j], ysd.at[j], yr.at[j], to_y)

    def right(j):
        return rcopy(to.at[0, j], fr.at[j], sr.at[j], rl.at[j], device(z + 1, y, x, c))

    def left(j):
        return rcopy(to.at[1, j], fl.at[j], sl.at[j], rr.at[j], device(z - 1, y, x, c))

    def stage0(j):
        core_copy(j).start()

    def stage1(j):
        core_copy(j).wait_recv()
        for part in range(2):
            at = y if part == 0 else 1 - y
            total = (grads[j, rows(c * share + at * quarter, quarter), :].astype(f32)
                     + cin[j, rows(at * quarter, quarter), :].astype(f32))
            if part == 0:
                hold[j] = total
            else:
                yo[j] = total.astype(bf16)
        y_copy(j).start()

    def stage2(j):
        y_copy(j).wait_recv()
        hold[j] = hold[j] + yi[j].astype(f32)

    def flow_right(j):
        @pl.when(z == 0)
        def _():
            to[0, j] = hold[j].astype(bf16)

        @pl.when(z > 0)
        def _():
            right(j).wait_recv()
            to[0, j] = (hold[j] + fr[j].astype(f32)).astype(bf16)

        @pl.when(z < line - 1)
        def _():
            right(j).start()

    def flow_left(j):
        @pl.when(z == line - 1)
        def _():
            to[1, j] = hold[j].astype(bf16)

        @pl.when(z < line - 1)
        def _():
            left(j).wait_recv()
            to[1, j] = (hold[j] + fl[j].astype(f32)).astype(bf16)

        @pl.when(z > 0)
        def _():
            left(j).start()

    def total(j):
        value = hold[j]
        value = value + jnp.where(z > 0, fr[j].astype(f32), 0.0)
        return value + jnp.where(z < line - 1, fl[j].astype(f32), 0.0)

    def ranged(j, do_it):
        pl.when((j >= 0) & (j < nmat))(functools.partial(do_it, j))

    def tick(t):
        ranged(t, stage0)
        ranged(t - 1, stage1)
        ranged(t - 3, stage2)
        ranged(t - 4 - 2 * z, flow_right)
        ranged(t - 4 - 2 * (line - 1 - z), flow_left)

    def body(t, carry):
        tick(t)
        return carry

    lax.fori_loop(0, nmat + 4 + 2 * (line - 1), body, 0)

    for s in range(cap):
        do[s] = total(pick[(1 - y) * cap + s]).astype(bf16)
    deliver = rcopy(do, di, dsem.at[0], dsem.at[1], to_y)
    deliver.start()
    for s in range(cap):
        out[s, rows(y * quarter, quarter), :] = total(pick[y * cap + s])
    deliver.wait_recv()
    for s in range(cap):
        out[s, rows((1 - y) * quarter, quarter), :] = di[s].astype(f32)
    deliver.wait_send()

    def finish(j, carry):
        core_copy(j).wait_send()
        y_copy(j).wait_send()

        @pl.when(z < line - 1)
        def _():
            right(j).wait_send()

        @pl.when(z > 0)
        def _():
            left(j).wait_send()

        return carry

    lax.fori_loop(0, nmat, finish, 0)


def reduce_grads(owners, grads, line, order, cap):
    nmat, both, width = grads.shape
    share = both // 2
    quarter = share // 2
    bf16, f32 = jnp.bfloat16, jnp.float32
    dma = pltpu.SemaphoreType.DMA
    return pl.pallas_call(
        functools.partial(reduce_kernel, line, order, cap),
        out_shape=jax.ShapeDtypeStruct((cap, share, width), f32),
        in_specs=[pl.BlockSpec(memory_space=pltpu.SMEM), pl.BlockSpec(memory_space=pltpu.VMEM)],
        out_specs=pl.BlockSpec(memory_space=pltpu.VMEM),
        scratch_shapes=[
            pltpu.VMEM((nmat, share, width), bf16),
            pltpu.VMEM((nmat, quarter, width), f32),
            pltpu.VMEM((nmat, quarter, width), bf16),
            pltpu.VMEM((nmat, quarter, width), bf16),
            pltpu.VMEM((nmat, quarter, width), bf16),
            pltpu.VMEM((nmat, quarter, width), bf16),
            pltpu.VMEM((2, nmat, quarter, width), bf16),
            pltpu.VMEM((cap, quarter, width), bf16),
            pltpu.VMEM((cap, quarter, width), bf16),
            pltpu.SMEM((nmat,), jnp.int32),
            pltpu.SMEM((2 * cap,), jnp.int32),
        ] + [dma((nmat,))] * 8 + [dma((2,))],
        name="reduce_grads",
        compiler_params=pltpu.CompilerParams(
            collective_id=2, has_side_effects=True, vmem_limit_bytes=56 * 1024 * 1024),
    )(owners, grads)
HDIM = 64
LEN = 512
STEP = 10
SPAN_ROWS = 96
LN_EPS = 1e-12
MATRIX_RATE = 0.03
VECTOR_RATE = 0.25
BETA_ONE = 0.5
BETA_TWO = 0.5
DECAY = 0.01
ADAM_EPS = 1e-08
BF16 = jnp.bfloat16
F32 = jnp.float32


def layer_norm(value, gain, shift):
    center = value - jnp.mean(value, axis=-1, keepdims=True)
    inverse = lax.rsqrt(jnp.mean(center * center, axis=-1, keepdims=True) + LN_EPS)
    normed = center * inverse
    return (normed * gain + shift, normed, inverse)


def norm_back(grad, normed, inverse, gain):
    scaled = grad * gain
    first = jnp.mean(scaled, axis=-1, keepdims=True)
    second = jnp.mean(scaled * normed, axis=-1, keepdims=True)
    return inverse * (scaled - first - normed * second)


def gelu_slope(value):
    cdf = 0.5 * (1.0 + lax.erf(value * 2.0 ** (-0.5)))
    pdf = jnp.exp(-0.5 * value * value) * (2.0 * jnp.pi) ** (-0.5)
    return cdf + value * pdf


def adamw(weight, moment_one, moment_two, grad, step_rate):
    new_one = BETA_ONE * moment_one + (1.0 - BETA_ONE) * grad
    new_two = BETA_TWO * moment_two + (1.0 - BETA_TWO) * grad * grad
    corr_one = 1.0 - BETA_ONE**STEP
    corr_two = 1.0 - BETA_TWO**STEP
    direction = new_one / corr_one / (jnp.sqrt(new_two / corr_two) + ADAM_EPS)
    return (weight - step_rate * (direction + DECAY * weight), new_one, new_two)


def dot(eq, a, b):
    return jnp.einsum(eq, a, b, preferred_element_type=F32)


def on_device(line, hidden_in, incoming, spans, owners, vectors, vec_one, vec_two, master_slots, slot_one, slot_two):
    cap, width, share = master_slots.shape
    nmat = owners.shape[0]
    ratio = (nmat - 4) // 2
    scale = HDIM ** (-0.5)
    heads = width // HDIM
    rank_mp = lax.axis_index("mp")
    rx, rc = rank_mp // 2, rank_mp % 2
    tokens = hidden_in.shape[0]
    own = tokens // 4
    nseq = own // LEN
    pieces = gather_weights(owners, jnp.transpose(master_slots, (0, 2, 1)).astype(BF16), line)
    wq, wk, wv, wo = pieces[0], pieces[1], pieces[2], pieces[3]
    b_up = vectors[3:3 + ratio].reshape(4, ratio, share).transpose(1, 0, 2).reshape(ratio, width)
    b_q, b_v, b_o, b_down = vectors[0], vectors[1], vectors[2], vectors[3 + ratio]
    gain_one, shift_one, gain_two, shift_two = (vectors[4 + ratio + i] for i in range(4))

    def split(v):
        return v.reshape(-1, LEN, heads, HDIM)

    def attend(block):
        q_blk, k_blk, v_blk = block
        scores = dot("qhd,khd->hqk", q_blk, k_blk) * scale
        probs = jax.nn.softmax(scores, axis=-1)
        return dot("hqk,khd->qhd", probs.astype(BF16), v_blk).astype(BF16)

    mine = lax.dynamic_slice_in_dim(hidden_in, rank_mp * own, own, 0)
    q = (dot("td,sd->ts", mine, wq) + b_q).astype(BF16)
    k = dot("td,sd->ts", mine, wk).astype(BF16)
    v = (dot("td,sd->ts", mine, wv) + b_v).astype(BF16)
    ctx = lax.map(attend, (split(q), split(k), split(v))).reshape(own, width)
    first, _, _ = layer_norm(mine.astype(F32) + dot("ts,so->to", ctx, wo) + b_o, gain_one, shift_one)
    low = first.astype(BF16)
    second = first + b_down
    for i in range(ratio):
        act = jax.nn.gelu(dot("td,fd->tf", low, pieces[4 + i]) + b_up[i], approximate=False).astype(BF16)
        second = second + dot("tf,fo->to", act, pieces[4 + ratio + i])
    layer = layer_norm(second, gain_two, shift_two)[0].astype(BF16)
    layer = lax.all_gather(layer, "mp", axis=0, tiled=True)

    def ours(v):
        v = v.reshape((2, 2, v.shape[0] // 4) + v.shape[1:])
        v = lax.dynamic_index_in_dim(v, rc, 1, keepdims=False)
        return v.reshape((-1,) + v.shape[2:])
    hid = ours(hidden_in)
    inc = ours(incoming)
    spn = ours(spans)
    position = jnp.arange(LEN, dtype=jnp.int32)
    starts = spn[:, :, 0][:, :, None]
    ends = starts + spn[:, :, 1][:, :, None]
    covered = jnp.any((position >= starts) & (position < ends), axis=1)
    rank = jnp.cumsum(covered.astype(jnp.int32), axis=1) - 1
    pick = ((rank[:, None, :] == jnp.arange(SPAN_ROWS)[None, :, None]) & covered[:, None, :]).astype(BF16)
    hid_s = hid.reshape(-1, LEN, width)
    ns = hid_s.shape[0]
    hm = dot("sit,std->sid", pick, hid_s).astype(BF16).reshape(-1, width)
    gm = dot("sit,std->sid", pick, inc.reshape(-1, LEN, width)).reshape(-1, width)
    q = (dot("td,sd->ts", hm, wq) + b_q).astype(BF16)
    k = dot("td,sd->ts", hid, wk).astype(BF16)
    v = (dot("td,sd->ts", hid, wv) + b_v).astype(BF16)
    q_s, k_s, v_s = q.reshape(ns, SPAN_ROWS, heads, HDIM), split(k), split(v)
    probs = jax.nn.softmax(dot("sqhd,skhd->shqk", q_s, k_s) * scale, axis=-1)
    pr = probs.astype(BF16)
    ctx = dot("shqk,skhd->sqhd", pr, v_s).astype(BF16).reshape(-1, width)
    y1, n1, i1 = layer_norm(hm.astype(F32) + dot("ts,so->to", ctx, wo) + b_o, gain_one, shift_one)
    low = y1.astype(BF16)
    second = y1 + b_down
    acts, ups = [], []
    for i in range(ratio):
        up = dot("td,fd->tf", low, pieces[4 + i]) + b_up[i]
        act = jax.nn.gelu(up, approximate=False).astype(BF16)
        second = second + dot("tf,fo->to", act, pieces[4 + ratio + i])
        ups.append(up)
        acts.append(act)
    _, n2, i2 = layer_norm(second, gain_two, shift_two)
    grad_g2 = jnp.sum(gm * n2, axis=0)
    grad_e2 = jnp.sum(gm, axis=0)
    dh2 = norm_back(gm, n2, i2, gain_two)
    df = dh2.astype(BF16)
    grad_b2 = jnp.sum(df.astype(F32), axis=0)

    def half(v):
        return lax.dynamic_slice_in_dim(v, rx * 2 * share, 2 * share, 1)
    grads = [None] * nmat
    dy1 = dh2
    b_rows = []
    for i in range(ratio):
        du = (dot("to,fo->tf", df, pieces[4 + ratio + i]) * gelu_slope(ups[i])).astype(BF16)
        dy1 = dy1 + dot("tf,fd->td", du, pieces[4 + i])
        b_rows.append(jnp.sum(du.astype(F32), axis=0))
        grads[4 + i] = dot("tf,td->fd", half(du), low)
        grads[4 + ratio + i] = dot("tf,to->fo", half(acts[i]), df)
    grad_b1 = jnp.stack(b_rows).reshape(ratio, 4, share).transpose(1, 0, 2).reshape(ratio, width)
    grad_g1 = jnp.sum(dy1 * n1, axis=0)
    grad_e1 = jnp.sum(dy1, axis=0)
    dh1 = norm_back(dy1, n1, i1, gain_one)
    da = dh1.astype(BF16)
    grad_bo = jnp.sum(da.astype(F32), axis=0)
    grads[3] = dot("ts,to->so", half(ctx), da)
    dctx = dot("to,so->ts", da, wo).astype(BF16).reshape(ns, SPAN_ROWS, heads, HDIM)
    dp = dot("sqhd,skhd->shqk", dctx, v_s)
    ds = (probs * (dp - jnp.sum(probs * dp, axis=-1, keepdims=True))).astype(BF16)
    dq = (dot("shqk,skhd->sqhd", ds, k_s) * scale).astype(BF16).reshape(-1, width)
    dk = (dot("shqk,sqhd->skhd", ds, q_s) * scale).astype(BF16).reshape(-1, width)
    dv = dot("shqk,sqhd->skhd", pr, dctx).astype(BF16).reshape(-1, width)
    grads[0] = dot("ts,td->sd", half(dq), hm)
    grads[1] = dot("ts,td->sd", half(dk), hid)
    grads[2] = dot("ts,td->sd", half(dv), hid)
    grad_bq = jnp.sum(dq.astype(F32), axis=0)
    grad_bv = jnp.sum(dv.astype(F32), axis=0)
    back = (dh1 + dot("ts,sd->td", dq, wq)).astype(BF16).reshape(ns, SPAN_ROWS, width)
    dx = dot("ts,sd->td", dk, wk) + dot("ts,sd->td", dv, wv) + dot("sit,sid->std", pick, back).reshape(-1, width)
    dx = lax.dynamic_slice_in_dim(dx.astype(BF16), rx * own, own, 0)
    grad_in = lax.all_gather(dx, "mp", axis=0, tiled=True)

    vec_grad = jnp.concatenate([
        jnp.stack([grad_bq, grad_bv, grad_bo]), grad_b1,
        jnp.stack([grad_b2, grad_g1, grad_e1, grad_g2, grad_e2])], axis=0)
    vec_total = lax.psum(vec_grad, ("dp", "mp")) * 0.5
    new_vec = adamw(vectors, vec_one, vec_two, vec_total, VECTOR_RATE)

    order = tuple(p for i in range(ratio) for p in (4 + ratio + i, 4 + i)) + (3, 0, 1, 2)
    slot_grad = reduce_grads(owners, jnp.stack([grads[p] for p in order]).astype(BF16), line, order, cap)
    slot_grad = jnp.transpose(slot_grad, (0, 2, 1))
    held = jnp.sum((owners == lax.axis_index("dp")).astype(jnp.int32))
    occupied = (jnp.arange(cap) < held).astype(F32)[:, None, None]
    new_slots = adamw(master_slots, slot_one, slot_two, slot_grad, MATRIX_RATE)
    return (layer, grad_in) + new_vec + tuple(v * occupied for v in new_slots)


def solution(mesh):
    line = mesh.shape["dp"] // 2
    rows, slots = P("dp", None), P("dp", None, "mp")
    return jax.shard_map(
        functools.partial(on_device, line),
        mesh=mesh,
        in_specs=(rows, rows, P("dp", None, None), P(), P(), P(), P(), slots, slots, slots),
        out_specs=(rows, rows, P(), P(), P(), slots, slots, slots),
        check_vma=False,
    )
```

time: 1280 us -> 623 us (0.49)
  waiting for transfers between devices: 763 us -> 0.04 us
  Pallas kernels: 0 us -> 179 us
  other arithmetic: 107 us -> 31.5 us
    psum x5 -> x0, waiting for transfers between devices: 612 us -> none  [the longest x1 215 us: on_device(): attn = lax.psum(part_attn, 'mp') + b_out]
    pallas_call x0 -> x2, Pallas kernels: none -> 179 us  [the longest x1 95.6 us: gather_weights(): pl.pallas_call(functools.partial(gather_kernel, line, nmat, cap), out_sha...]
    reduce_scatter x1 -> x0, waiting for transfers between devices: 151 us -> none  [on_device(): lax.psum_scatter(jnp.einsum('rp,pij->rij', pick, grads, precision=HI).ast...]
    reduce_sum x17 -> x4, other arithmetic: 59.1 us -> 3.68 us  [the longest x1 1.05 us: on_device(): grad_g2 = jnp.sum(gm * n2, axis=0)]
    concatenate x2 -> x1, local copies, waits for them, and re-layouts: 24.7 us -> 0.07 us  [on_device(): jnp.concatenate([jnp.stack([grad_bq, grad_bv, grad_bo]), grad_b1, jnp.sta...]
    dot_general x76 -> x55, matrix products: 250 us -> 227 us  [dot(): return jnp.einsum(eq, a, b, preferred_element_type=F32)]
    sub x0 -> x2, matrix products: none -> 20.4 us  [attend(): probs = jax.nn.softmax(scores, axis=-1)]
    reshape x4 -> x13, local copies, waits for them, and re-layouts: 5.87 us -> 21.8 us  [the longest x5 11.4 us: split(): return v.reshape(-1, LEN, heads, HDIM)]
  transfers between devices with their start and end apart: 6 -> 2, of which waited for: 5 -> 0; matrix products, arithmetic and copies ran while one was open for 9% -> 39% of each run, Pallas kernels for 0% -> 14%
where the time goes in v1:
time: 623 us; the launch traced here: 610 us
  matrix products  248 us (40%)
  Pallas kernels  179 us (29%)
  local copies, waits for them, and re-layouts  98.6 us (16%)
  blocking collectives  37.5 us (6%)
  other arithmetic  31.5 us (5%)
  between operations  15.4 us (2%)
    dot_general x55, matrix products, dot(): return jnp.einsum(eq, a, b, preferred_element_type=F32)  227 us
    pallas_call x1, Pallas kernels, gather_weights(): pl.pallas_call(functools.partial(gather_kernel, line, nmat, cap), out_sha...  95.6 us
    pallas_call x1, Pallas kernels, reduce_grads(): pl.pallas_call(functools.partial(reduce_kernel, line, order, cap), out_sh...  83.5 us
    psum x1, blocking collectives, on_device(): vec_total = lax.psum(vec_grad, ('dp', 'mp')) * 0.5  37.5 us
    unnamed x188, local copies, waits for them, and re-layouts  31.5 us
    sub x2, matrix products, attend(): probs = jax.nn.softmax(scores, axis=-1)  20.4 us
  transfers between devices with their start and end apart: 2, of which 0 were waited for; matrix products, arithmetic and copies ran while one was open for 39% of the time, Pallas kernels for 14%

profile of v1, /device:TPU:0, one launch (start us, length us, event | category | flops | bytes accessed | tf_op | source)
XLA Modules:
  0.0 610.5 jit_solution(14076138125154395797)
XLA Ops:
  11.2 2.8 convert_bitcast_fusion.1.slots
  17.2 95.6 %gather_weights.1 = bf16[12,768,768]{2,1,0:T(8,128)(2,1)} custom-call(s32[12]{0:T(128)} %owners.3, bf16[4,192,768]{2,1,0:T(8,128)(2,1)} %convert_bitcast_fusion.1.slots), custom_call_target="tpu_custom_call" | custom-call | tf_op jit(solution)/shard_map/gather_weights/pallas_call | solution.py:243
  112.9 3.8 convolution_convert_fusion.1
  116.7 2.7 add_convert_fusion.2
  123.1 2.7 add_convert_fusion.3
  133.8 32.5 %while.10 = (s32[]{:T(128)}, bf16[2,512,12,64]{1,3,2,0:T(8,128)(2,1)S(1)}, bf16[2,512,12,64]{1,3,2,0:T(8,128)(2,1)}, bf16[2,512,12,64]{1,3,2,0:T(8,128)(2,1)}, bf16[2,512,12,64]{1,3,2,0:T(8,128)(2,1)}, /*index=5*/s32[]{:T(128)}) while((s32[]{:T(128)}, bf16[2,512,12,64]{1,3,2,0:T(8,128)(2,1)S(1)}, bf16[2,512,12,64]{1,3,2,0:T(8,128)(2,1)}, ...), condition=%wide.region_3.4_spmd, body=%wide.region_0.3_spmd.sunk | while | flops 821428736 | bytes 34662504 | solution.py:502
  133.8 10.2 %fusion.591 = (f32[12,512]{1,0:T(8,128)S(1)}, f32[12,512,512]{1,2,0:T(8,128)}) fusion(bf16[2,512,12,64]{1,3,2,0:T(8,128)(2,1)} %get-tuple-element.207, s32[]{:T(128)S(6)} %copy.130, bf16[2,512,12,64]{1,3,2,0:T(8,128)(2,1)} %get-tuple-element.206), kind=kOutput, calls=%fused_computation.647.clone.1 | convolution fusion | flops 412090880 | bytes 14181376 | tf_op jit(solution)/shard_map/while/body/eval_jaxpr/sub | solution.py:495
  144.0 5.8 fusion.592
  149.9 10.2 %fusion.591 = (f32[12,512]{1,0:T(8,128)S(1)}, f32[12,512,512]{1,2,0:T(8,128)}) fusion(bf16[2,512,12,64]{1,3,2,0:T(8,128)(2,1)} %get-tuple-element.207, s32[]{:T(128)S(6)} %copy.130, bf16[2,512,12,64]{1,3,2,0:T(8,128)(2,1)} %get-tuple-element.206), kind=kOutput, calls=%fused_computation.647.clone.1 | convolution fusion | flops 412090880 | bytes 14181376 | tf_op jit(solution)/shard_map/while/body/eval_jaxpr/sub | solution.py:495
  160.1 5.8 fusion.592
  169.4 2.9 fusion.525
  172.8 13.7 %fusion.164 = f32[1024,768]{0,1:T(8,128)} fusion(f32[768]{0:T(1024)S(1)} %add.377, bf16[12,768,768]{2,1,0:T(8,128)(2,1)} %gather_weights.1, f32[1024,768]{0,1:T(8,128)S(1)} %get-tuple-element.121, f32[768]{0:T(1024)S(1)} %get-tuple-element.85, f32[768]{0:T(1024)S(1)} %get-tuple-element.86, f32[1024]{0:T(1024)S(1)} %add_rsqrt_fusion.1, ...), kind=kOutput, calls=%fused_computation.233 | convolution fusion | flops 2471755776 | bytes 8668160 | tf_op jit(solution)/shard_map/tf,fo->to/dot_general | solution.py:469
  186.5 12.9 %fusion.163 = f32[1024,768]{0,1:T(8,128)} fusion(f32[768]{0:T(1024)S(1)} %add.381, bf16[12,768,768]{2,1,0:T(8,128)(2,1)} %gather_weights.1, f32[1024,768]{0,1:T(8,128)S(1)} %get-tuple-element.121, f32[768]{0:T(1024)S(1)} %get-tuple-element.85, f32[768]{0:T(1024)S(1)} %get-tuple-element.86, f32[1024]{0:T(1024)S(1)} %add_rsqrt_fusion.1, ...), kind=kOutput, calls=%fused_computation.232 | convolution fusion | flops 2471755776 | bytes 8668160 | tf_op jit(solution)/shard_map/tf,fo->to/dot_general | solution.py:469
  199.4 13.1 %fusion.165 = f32[1024,768]{0,1:T(8,128)} fusion(f32[768]{0:T(1024)S(1)} %copy-done.73, bf16[12,768,768]{2,1,0:T(8,128)(2,1)} %gather_weights.1, f32[1024,768]{0,1:T(8,128)S(1)} %get-tuple-element.121, f32[768]{0:T(1024)S(1)} %get-tuple-element.85, f32[768]{0:T(1024)S(1)} %get-tuple-element.86, f32[1024]{0:T(1024)S(1)} %add_rsqrt_fusion.1, ...), kind=kOutput, calls=%fused_computation.234 | convolution fusion | flops 2471755776 | bytes 8668160 | tf_op jit(solution)/shard_map/tf,fo->to/dot_general | solution.py:469
  212.5 17.2 %fusion.526 = (f32[1024]{0:T(1024)S(1)}, f32[1024,768]{0,1:T(8,128)S(1)}) fusion(bf16[12,768,768]{2,1,0:T(8,128)(2,1)} %gather_weights.1, f32[768]{0:T(1024)S(1)} %copy-done.79, f32[1024,768]{0,1:T(8,128)} %copy-done.16, f32[768]{0:T(1024)S(1)} %get-tuple-element.85, f32[768]{0:T(1024)S(1)} %get-tuple-element.86, f32[1024]{0:T(1024)S(1)} %add_rsqrt_fusion.1, ...), kind=kOutput, calls=%fused_computation.649 | convolution fusion | flops 2479619072 | bytes 21278720 | tf_op jit(solution)/shard_map/tf,fo->to/dot_general | solution.py:469
  232.2 4.9 constant_dynamic-slice_fusion
  237.2 6.5 %add_convert_fusion = bf16[2048,768]{1,0:T(8,128)(2,1)} fusion(bf16[2048,768]{1,0:T(8,128)(2,1)S(1)} %bitcast.346, f32[768]{0:T(1024)S(1)} %copy-done.72, bf16[12,768,768]{2,1,0:T(8,128)(2,1)} %gather_weights.1), kind=kOutput, calls=%fused_computation.34 | convolution fusion | flops 2419064832 | bytes 7474176 | tf_op jit(solution)/shard_map/td,sd->ts/dot_general | solution.py:469
  243.7 5.3 convolution_convert_fusion
  257.1 3.2 copy.79
  260.3 3.9 reshape.233
  264.2 3.2 copy.76
  267.4 4.0 reshape.232
  271.4 3.7 fusion.91
  275.0 4.6 fusion.531
  279.7 2.5 copy-done.2
  282.1 15.7 %fusion.155 = bf16[4,96,12,64]{1,3,2,0:T(8,128)(2,1)} fusion(bf16[4,512,12,64]{1,0,3,2:T(4,128)(2,1)S(1)} %copy-done.11, f32[4,12,96]{2,1,0:T(8,128)S(1)} %get-tuple-element.124, f32[4,12,96,512]{3,2,1,0:T(8,128)} %copy-done.2), kind=kOutput, calls=%fused_computation.230 | convolution fusion | flops 314086400 | bytes 13191168 | tf_op jit(solution)/shard_map/shqk,skhd->sqhd/dot_general | solution.py:469
  303.0 5.6 fusion.209
  308.5 5.3 fusion.206
  313.9 5.4 fusion.203
  319.3 5.9 fusion.200
  339.1 2.7 convert_reduce_fusion.6
  344.6 3.2 convert_reduce_fusion.5
  350.0 2.7 convert_reduce_fusion.4
  354.9 2.7 convert_reduce_fusion.3
  357.7 3.1 multiply_reduce_fusion.5
  368.0 14.4 %convert_reduce_fusion = (f32[12,64]{1,0:T(8,128)}, bf16[4,512,12,64]{1,3,2,0:T(8,128)(2,1)}) fusion(bf16[4,96,12,64]{1,3,2,0:T(8,128)(2,1)S(1)} %copy.84, f32[4,12,96]{2,1,0:T(8,128)S(1)} %copy-done.41, f32[4,12,96,512]{3,2,1,0:T(8,128)} %copy-done.2), kind=kOutput, calls=%fused_computation.32 | convolution fusion | flops 318509312 | bytes 13194240 | tf_op jit(solution)/shard_map/shqk,sqhd->skhd/dot_general | solution.py:469
  382.4 4.3 copy.89
  386.7 2.7 copy.104
  389.4 6.7 %multiply_reduce_fusion.1 = (f32[4,12,96]{2,1,0:T(8,128)S(1)}, f32[4,12,96,512]{3,2,1,0:T(8,128)S(1)}) fusion(f32[4,12,96,512]{3,2,1,0:T(8,128)} %get-tuple-element.125, f32[4,12,96]{2,1,0:T(8,128)S(1)} %copy-done.41, bf16[4,96,12,64]{1,3,2,0:T(8,128)(2,1)S(1)} %copy.84, bf16[4,512,12,64]{1,0,3,2:T(4,128)(2,1)} %reshape.233), kind=kOutput, calls=%fused_computation.28 | convolution fusion | flops 309063168 | bytes 22646784 | tf_op jit(solution)/shard_map/sqhd,skhd->shqk/dot_general | solution.py:469
  402.0 2.7 copy.103
  404.7 2.5 convert_reduce_fusion.1
  413.2 4.1 fusion.258
  417.3 4.4 fusion.265
  457.1 83.5 %reduce_grads.1 = f32[4,192,768]{2,1,0:T(8,128)} custom-call(s32[12]{0:T(128)} %owners.3, bf16[12,384,768]{2,1,0:T(8,128)(2,1)} %fusion.169.grads), custom_call_target="tpu_custom_call" | custom-call | tf_op jit(solution)/shard_map/reduce_grads/pallas_call | solution.py:402
  540.7 37.5 %psum.7 = f32[12,768]{1,0:T(8,128)S(1)} all-reduce(f32[12,768]{1,0:T(8,128)S(1)} %concatenate.4), channel_id=1, replica_groups=mesh['dp'=8,'mp'=4] {'dp','mp'}, use_global_device_ids=true, to_apply=%region_34.35 | all-reduce | flops 9216 | bytes 73728 | tf_op jit(solution)/shard_map/psum | solution.py:590
  580.2 8.7 %broadcast_multiply_fusion = (f32[4,768,192]{1,2,0:T(8,128)}, f32[4,768,192]{1,2,0:T(8,128)}, f32[4,768,192]{1,2,0:T(8,128)}) fusion(f32[4]{0:T(128)S(1)} %compare_convert_fusion, f32[4,192,768]{2,1,0:T(8,128)} %reduce_grads.1, f32[4,768,192]{1,2,0:T(8,128)} %param.21, f32[4,768,192]{1,2,0:T(8,128)S(1)} %copy-done.7, f32[4,768,192]{1,2,0:T(8,128)} %param.20), kind=kLoop, calls=%fused_computation.328 | loop fusion | flops 10027008 | bytes 16515088 | tf_op jit(solution)/shard_map/mul | solution.py:599
  588.9 8.6 %copy.92 = bf16[4096,768]{1,0:T(8,128)(2,1)} copy(bf16[4096,768]{0,1:T(8,128)(2,1)} %all-gather.3.cloned.1.call-done) | data formatting | bytes 12582912
  597.5 5.9 copy.146
  (301 shorter events, 115.1 us)
Async XLA Ops:
  7.2 241.8 %copy-start = (s32[8,24,2]{1,2,0:T(2,128)S(1)}, s32[8,24,2]{1,2,0:T(2,128)}, u32[]{:S(2)}) copy-start(s32[8,24,2]{1,2,0:T(2,128)} %param.14) | copy-start | bytes 4612
  7.2 581.8 %all-gather.3.cloned.1.call-start = ((), (), s32[]{:S(2)}) async-start(), calls=%async_computation | async-start | bytes 7864320 | tf_op jit(solution)/shard_map/all_gather | solution.py:510
  9.6 107.1 %copy-start.69 = (f32[768]{0:T(1024)}, f32[768]{0:T(1024)S(1)}, u32[]{:S(2)}) copy-start(f32[768]{0:T(1024)S(1)} %get-tuple-element.88) | copy-start | bytes 9220
  9.6 113.3 %copy-start.71 = (f32[768]{0:T(1024)}, f32[768]{0:T(1024)S(1)}, u32[]{:S(2)}) copy-start(f32[768]{0:T(1024)S(1)} %get-tuple-element.89) | copy-start | bytes 9220
  9.6 158.9 %copy-start.67 = (f32[768]{0:T(1024)}, f32[768]{0:T(1024)S(1)}, u32[]{:S(2)}) copy-start(f32[768]{0:T(1024)S(1)} %get-tuple-element.87) | copy-start | bytes 9220
  9.6 202.9 %copy-start.46 = (f32[768]{0:T(1024)}, f32[768]{0:T(1024)S(1)}, u32[]{:S(2)}) copy-start(f32[768]{0:T(1024)S(1)} %get-tuple-element.86) | copy-start | bytes 9220
  9.6 202.9 %copy-start.53 = (f32[768]{0:T(1024)}, f32[768]{0:T(1024)S(1)}, u32[]{:S(2)}) copy-start(f32[768]{0:T(1024)S(1)} %get-tuple-element.85) | copy-start | bytes 9220
  10.5 176.0 %copy-start.77 = (f32[768]{0:T(1024)}, f32[768]{0:T(1024)S(1)}, u32[]{:S(2)}) copy-start(f32[768]{0:T(1024)S(1)} %add.381) | copy-start | bytes 9220
  10.6 162.2 %copy-start.75 = (f32[768]{0:T(1024)}, f32[768]{0:T(1024)S(1)}, u32[]{:S(2)}) copy-start(f32[768]{0:T(1024)S(1)} %add.377) | copy-start | bytes 9220
  15.5 101.2 %copy-start.9 = (bf16[1024,768]{1,0:T(8,128)(2,1)}, bf16[1024,768]{1,0:T(8,128)(2,1)S(1)}, u32[]{:S(2)}) copy-start(bf16[1024,768]{1,0:T(8,128)(2,1)S(1)} %constant_dynamic-slice_fusion.3) | copy-start | bytes 4718596
  133.8 10.2 %copy-start.21 = (bf16[2,512,12,64]{1,3,2,0:T(8,128)(2,1)S(1)}, bf16[2,512,12,64]{1,3,2,0:T(8,128)(2,1)}, u32[]{:S(2)}) copy-start(bf16[2,512,12,64]{1,3,2,0:T(8,128)(2,1)} %get-tuple-element.205) | copy-start | bytes 4718596 | tf_op jit(solution)/shard_map/while
  149.9 10.2 %copy-start.21 = (bf16[2,512,12,64]{1,3,2,0:T(8,128)(2,1)S(1)}, bf16[2,512,12,64]{1,3,2,0:T(8,128)(2,1)}, u32[]{:S(2)}) copy-start(bf16[2,512,12,64]{1,3,2,0:T(8,128)(2,1)} %get-tuple-element.205) | copy-start | bytes 4718596 | tf_op jit(solution)/shard_map/while
  172.3 27.1 %copy-start.16 = (f32[1024,768]{0,1:T(8,128)}, f32[1024,768]{0,1:T(8,128)S(1)}, u32[]{:S(2)}) copy-start(f32[1024,768]{0,1:T(8,128)S(1)} %get-tuple-element.121) | copy-start | bytes 9437188
  186.5 12.9 %copy-start.73 = (f32[768]{0:T(1024)S(1)}, f32[768]{0:T(1024)}, u32[]{:S(2)}) copy-start(f32[768]{0:T(1024)} %add.373) | copy-start | bytes 9220
  199.4 13.1 %copy-start.66 = (f32[768]{0:T(1024)S(1)}, f32[768]{0:T(1024)}, u32[]{:S(2)}) copy-start(f32[768]{0:T(1024)} %get-tuple-element.84) | copy-start | bytes 9220
  199.4 13.1 %copy-start.79 = (f32[768]{0:T(1024)S(1)}, f32[768]{0:T(1024)}, u32[]{:S(2)}) copy-start(f32[768]{0:T(1024)} %add.385) | copy-start | bytes 9220
  232.2 365.4 %all-gather.5.cloned.1.call-start = ((), (), s32[]{:S(2)}) async-start(), calls=%async_computation.1 | async-start | bytes 7864320 | tf_op jit(solution)/shard_map/all_gather | solution.py:585
  237.2 13.7 %copy-start.3 = (bf16[2,1,1024,768]{3,2,1,0:T(8,128)(2,1)}, bf16[2,1,1024,768]{3,2,1,0:T(8,128)(2,1)S(1)}, u32[]{:S(2)}) copy-start(bf16[2,1,1024,768]{3,2,1,0:T(8,128)(2,1)S(1)} %get-tuple-element.155) | copy-start | bytes 9437188
  275.0 7.1 %copy-start.2 = (f32[4,12,96,512]{3,2,1,0:T(8,128)}, f32[4,12,96,512]{3,2,1,0:T(8,128)S(1)}, u32[]{:S(2)}) copy-start(f32[4,12,96,512]{3,2,1,0:T(8,128)S(1)} %fusion.91) | copy-start | bytes 28311556
  275.0 7.1 %copy-start.11 = (bf16[4,512,12,64]{1,0,3,2:T(4,128)(2,1)S(1)}, bf16[4,512,12,64]{1,0,3,2:T(4,128)(2,1)}, u32[]{:S(2)}) copy-start(bf16[4,512,12,64]{1,0,3,2:T(4,128)(2,1)} %reshape.233) | copy-start | bytes 9437188
  282.1 15.7 %copy-start.40 = (f32[4,12,96]{2,1,0:T(8,128)}, f32[4,12,96]{2,1,0:T(8,128)S(1)}, u32[]{:S(2)}) copy-start(f32[4,12,96]{2,1,0:T(8,128)S(1)} %get-tuple-element.124) | copy-start | bytes 55300
  302.3 6.2 %copy-start.49 = (f32[384]{0:T(512)}, f32[384]{0:T(512)S(1)}, u32[]{:S(2)}) copy-start(f32[384]{0:T(512)S(1)} %broadcast_multiply_fusion.9) | copy-start | bytes 4612
  302.6 5.9 copy-start.51
  303.0 16.3 %copy-start.25 = (bf16[384,768]{1,0:T(8,128)(2,1)}, bf16[384,768]{1,0:T(8,128)(2,1)S(1)}, u32[]{:S(2)}) copy-start(bf16[384,768]{1,0:T(8,128)(2,1)S(1)} %fusion.297) | copy-start | bytes 1769476
  303.0 5.6 copy-start.78
  308.5 5.4 copy-start.76
  319.3 5.9 copy-start.6
  389.4 6.7 %slice-start = ((s8[9437184]{0:T(1024)(128)(4,1)}), s8[4194304]{0:T(1024)(128)(4,1)S(1)}, s32[]{:S(2)}) async-start(s8[9437184]{0:T(1024)(128)(4,1)} %bitcast.341), calls=%async_computation.2 | async-start | bytes 8388608
  389.4 7.1 %slice-start.1 = ((s8[9437184]{0:T(1024)(128)(4,1)}), s8[4194304]{0:T(1024)(128)(4,1)S(1)}, s32[]{:S(2)}) async-start(s8[9437184]{0:T(1024)(128)(4,1)} %bitcast.341), calls=%async_computation.3 | async-start | bytes 8388608
  389.4 7.3 %slice-start.2 = ((s8[9437184]{0:T(1024)(128)(4,1)}), s8[1048576]{0:T(1024)(128)(4,1)S(1)}, s32[]{:S(2)}) async-start(s8[9437184]{0:T(1024)(128)(4,1)} %bitcast.341), calls=%async_computation.4 | async-start | bytes 2097152
  421.7 10.5 %copy-start.58 = (f32[768]{0:T(1024)S(1)}, f32[768]{0:T(1024)}, u32[]{:S(2)}) copy-start(f32[768]{0:T(1024)} %get-tuple-element.111) | copy-start | bytes 9220
  421.7 14.5 %copy-start.32 = (bf16[384,768]{1,0:T(8,128)(2,1)S(1)}, bf16[384,768]{1,0:T(8,128)(2,1)}, u32[]{:S(2)}) copy-start(bf16[384,768]{1,0:T(8,128)(2,1)} %copy-done.30) | copy-start | bytes 1769476
  423.4 15.2 %copy-start.26 = (bf16[384,768]{1,0:T(8,128)(2,1)S(1)}, bf16[384,768]{1,0:T(8,128)(2,1)}, u32[]{:S(2)}) copy-start(bf16[384,768]{1,0:T(8,128)(2,1)} %copy-done.25) | copy-start | bytes 1769476
  436.2 7.1 %copy-start.36 = (bf16[384,768]{1,0:T(8,128)(2,1)S(1)}, bf16[384,768]{1,0:T(8,128)(2,1)}, u32[]{:S(2)}) copy-start(bf16[384,768]{1,0:T(8,128)(2,1)} %copy-done.35) | copy-start | bytes 1769476
  438.6 6.1 copy-start.28
  457.0 83.6 %copy-start.43 = (f32[4,768]{1,0:T(4,128)S(1)}, f32[4,768]{1,0:T(4,128)}, u32[]{:S(2)}) copy-start(f32[4,768]{1,0:T(4,128)} %reshape.243) | copy-start | bytes 36868
  457.0 83.6 %copy-start.59 = (f32[1,768]{1,0:T(1,128)S(1)}, f32[1,768]{1,0:T(1,128)}, u32[]{:S(2)}) copy-start(f32[1,768]{1,0:T(1,128)} %stack.103) | copy-start | bytes 9220
  457.0 83.6 %copy-start.60 = (f32[1,768]{1,0:T(1,128)S(1)}, f32[1,768]{1,0:T(1,128)}, u32[]{:S(2)}) copy-start(f32[1,768]{1,0:T(1,128)} %stack.102) | copy-start | bytes 9220
  457.0 83.6 %copy-start.61 = (f32[1,768]{1,0:T(1,128)S(1)}, f32[1,768]{1,0:T(1,128)}, u32[]{:S(2)}) copy-start(f32[1,768]{1,0:T(1,128)} %stack.100) | copy-start | bytes 9220
  457.0 83.6 %copy-start.62 = (f32[1,768]{1,0:T(1,128)S(1)}, f32[1,768]{1,0:T(1,128)}, u32[]{:S(2)}) copy-start(f32[1,768]{1,0:T(1,128)} %stack.93) | copy-start | bytes 9220
  457.0 83.6 %copy-start.63 = (f32[1,768]{1,0:T(1,128)S(1)}, f32[1,768]{1,0:T(1,128)}, u32[]{:S(2)}) copy-start(f32[1,768]{1,0:T(1,128)} %stack.92) | copy-start | bytes 9220
  457.0 83.6 %copy-start.64 = (f32[1,768]{1,0:T(1,128)S(1)}, f32[1,768]{1,0:T(1,128)}, u32[]{:S(2)}) copy-start(f32[1,768]{1,0:T(1,128)} %stack.91) | copy-start | bytes 9220
  457.1 121.2 %copy-start.82 = (s32[12]{0:T(128)S(1)}, s32[12]{0:T(128)}, u32[]{:S(2)}) copy-start(s32[12]{0:T(128)} %owners.3) | copy-start | bytes 148
  457.1 122.5 %copy-start.39 = (f32[12,768]{1,0:T(8,128)S(1)}, f32[12,768]{1,0:T(8,128)}, u32[]{:S(2)}) copy-start(f32[12,768]{1,0:T(8,128)} %param.16) | copy-start | bytes 110596
  457.1 122.5 %copy-start.44 = (f32[12,768]{1,0:T(8,128)S(1)}, f32[12,768]{1,0:T(8,128)}, u32[]{:S(2)}) copy-start(f32[12,768]{1,0:T(8,128)} %param.17) | copy-start | bytes 110596
  457.1 122.5 %copy-start.45 = (f32[12,768]{1,0:T(8,128)S(1)}, f32[12,768]{1,0:T(8,128)}, u32[]{:S(2)}) copy-start(f32[12,768]{1,0:T(8,128)} %param.18) | copy-start | bytes 110596
  457.1 123.1 %copy-start.7 = (f32[4,768,192]{1,2,0:T(8,128)S(1)}, f32[4,768,192]{1,2,0:T(8,128)}, u32[]{:S(2)}) copy-start(f32[4,768,192]{1,2,0:T(8,128)} %param.19) | copy-start | bytes 7077892
  597.5 5.9 copy-start.1
  (46 other events, 128.3 us)
Sparse Core Ops, SparseCore 0:
  232.3 45.1 all-gather.2
  423.5 45.1 all-gather.4

commit v2 on v1

--- a/solution.py
+++ b/solution.py
@@ -7,6 +7,34 @@
 from jax.experimental.pallas import tpu as pltpu
 
 MESH = pl.DeviceIdType.MESH
+BF16 = jnp.bfloat16
+F32 = jnp.float32
+LN_EPS = 1e-12
+HDIM = 64
+LEN = 512
+NT = (((1,), (1,)), ((), ()))
+NN = (((1,), (0,)), ((), ()))
+TN = (((0,), (0,)), ((), ()))
+
+
+def dg(left, right, dims):
+    return lax.dot_general(left, right, dims, preferred_element_type=F32)
+
+
+def flow_order(nmat):
+    ratio = (nmat - 4) // 2
+    return (0, 1, 2, 3) + tuple(p for k in range(ratio) for p in (4 + k, 4 + ratio + k))
+
+
+def layer_norm(value, gain, shift):
+    center = value - jnp.mean(value, axis=-1, keepdims=True)
+    inverse = lax.rsqrt(jnp.mean(center * center, axis=-1, keepdims=True) + LN_EPS)
+    normed = center * inverse
+    return normed * gain + shift, normed, inverse
+
+
+def gelu(value):
+    return 0.5 * value * (1.0 + lax.erf(value * 2.0 ** (-0.5)))
 
 
 def place():
@@ -42,8 +70,9 @@
     )
 
 
-def gather_kernel(line, nmat, cap, owners, slots, out, full, ys, fr, fl, zo, idx, slot_sem,
-                  sr, rl, sl, rr, xs, xr, ysd, yr, ds, dr, cs, cr, loc):
+def forward_kernel(line, nmat, cap, owners, slots_in, hidden, vecs, out, layer, k_ref, v_ref,
+                   full, slots, ys, stage, fr, fl, hid, q_ref, ctx, y1, low, acc, zo, idx,
+                   hid_sem, slot_send, slot_recv, sr, rl, sl, rr, xs, xr, ysd, yr, ds, dr, cs, cr, loc):
     share = slots.shape[1]
     quarter = share // 2
     half = quarter // 2
@@ -53,25 +82,43 @@
     over = 2 * (1 - x) + c
     to_y, to_x, to_c = device(z, 1 - y, x, c), device(z, y, 1 - x, c), device(z, y, x, 1 - c)
     greet(line)
-    slot_copy = rcopy(
-        slots.at[:, pl.ds(pl.multiple_of((1 - y) * quarter, 16), quarter), :],
-        ys.at[pl.ds(y * cap, cap)], slot_sem.at[0], slot_sem.at[1], to_y)
-    slot_copy.start()
-    for p in range(nmat):
+    ratio = (nmat - 4) // 2
+    order = flow_order(nmat)
+    own_rows = q_ref.shape[0]
+    hid_copy = pltpu.make_async_copy(
+        hidden.at[pl.ds(pl.multiple_of(me * own_rows, 16), own_rows)], hid, hid_sem)
+    hid_copy.start()
+
+    def slot_copy(s):
+        return rcopy(
+            slots.at[s, pl.ds(pl.multiple_of((1 - y) * quarter, 16), quarter), :],
+            ys[s].at[y], slot_send.at[s], slot_recv.at[s], to_y)
+
+    for s in range(cap):
+        slots[s] = slots_in[s].astype(BF16)
+        slot_copy(s).start()
+        ys[s][y] = slots[s, pl.ds(pl.multiple_of(y * quarter, 16), quarter), :]
+    for j, p in enumerate(order):
         mine = owners[p]
         place_of = jnp.int32(0)
         for q in range(p):
             place_of += jnp.where(owners[q] == mine, 1, 0).astype(jnp.int32)
-        zo[p] = mine // 2
-        idx[p] = (mine % 2) * cap + jnp.minimum(place_of, cap - 1)
-    ys[pl.ds(y * cap, cap)] = slots[:, pl.ds(pl.multiple_of(y * quarter, 16), quarter), :]
-    slot_copy.wait()
+        zo[j] = mine // 2
+        idx[j] = (mine % 2) * cap + jnp.minimum(place_of, cap - 1)
 
     def rows(block, yy, h):
         return pl.ds(pl.multiple_of(block * share + yy * quarter + h * half, 16), half)
 
     def own(r):
-        return ys[idx[r // 2], pl.ds(pl.multiple_of((r % 2) * half, 16), half), :]
+        at = pl.ds(pl.multiple_of((r % 2) * half, 16), half)
+        slot, half_of = idx[r // 2] % cap, idx[r // 2] // cap
+        stage[...] = ys[0][half_of, at, :]
+        for s in range(1, cap):
+            @pl.when(r // 2 >= s)
+            def _():
+                stage[...] = jnp.where(slot == s, ys[s][half_of, at, :], stage[...])
+
+        return stage[...]
 
     def right(r):
         return rcopy(fr.at[r], fr.at[r], sr.at[r], rl.at[r], device(z + 1, y, x, c))
@@ -125,7 +172,14 @@
     lag2 = lag1 + 3
     lag3 = lag2 + 1
 
+    def slot_came(s):
+        rcopy(slots.at[s, pl.ds(pl.multiple_of((1 - y) * quarter, 16), quarter), :],
+              ys[s].at[1 - y], slot_send.at[s], slot_recv.at[s], to_y).wait_recv()
+
     def tick(t):
+        for s in range(cap):
+            pl.when(t == 2 * s)(functools.partial(slot_came, s))
+
         r = t - 2 * z
 
         @pl.when((r >= 0) & (r < nchunk))
@@ -202,11 +256,92 @@
                 core_came(w // 2, k).wait_recv()
             keep(w // 2).start()
 
-    def body(t, carry):
-        tick(t)
-        return carry
-
-    lax.fori_loop(0, nchunk + lag3, body, 0)
+    ticks = nchunk + lag3
+    first = lag3 + 6
+
+    def ticking(start, count):
+        def body(i, carry):
+            tick(start + i)
+            return carry
+
+        lax.fori_loop(0, count, body, 0)
+
+    ticking(0, first)
+    hid_copy.wait()
+    tile = min(512, own_rows)
+    tiles = own_rows // tile
+
+    def at_rows(i):
+        return pl.ds(pl.multiple_of(i * tile, 16), tile)
+
+    def project(i, carry):
+        block = hid[at_rows(i), :]
+        q_ref[at_rows(i), :] = (
+            (dg(block, full[0], NT) + vecs[0:1, :]).astype(BF16) * jnp.asarray(HDIM ** -0.5, BF16))
+        k_ref[at_rows(i), :] = dg(block, full[1], NT).astype(BF16)
+        v_ref[at_rows(i), :] = (dg(block, full[2], NT) + vecs[1:2, :]).astype(BF16)
+        return carry
+
+    lax.fori_loop(0, tiles, project, 0)
+    pairs = hid.shape[1] // (2 * HDIM)
+    blocks = own_rows // LEN * pairs
+    lane = lax.broadcasted_iota(jnp.int32, (LEN, 2 * HDIM), 1)
+    left_half = lane < HDIM
+    ones = jnp.ones((LEN, 2 * HDIM), BF16)
+
+    def attend(i):
+        at = pl.ds(pl.multiple_of((i // pairs) * LEN, 16), LEN)
+        lanes = pl.ds(pl.multiple_of((i % pairs) * (2 * HDIM), 2 * HDIM), 2 * HDIM)
+        q_blk, k_blk = q_ref[at, lanes], k_ref[at, lanes]
+        v_blk = jnp.concatenate([v_ref[at, lanes], ones], axis=1)
+        mixed = []
+        for h in range(2):
+            q_one = jnp.where(left_half if h == 0 else ~left_half, q_blk, jnp.zeros_like(q_blk))
+            scores = dg(q_one, k_blk, NT)
+            raised = jnp.exp(scores - jnp.max(scores, axis=-1, keepdims=True)).astype(BF16)
+            both = dg(raised, v_blk, NN)
+            mixed.append(both[:, :2 * HDIM] / both[:, 2 * HDIM:])
+        ctx[at, lanes] = jnp.where(left_half, mixed[0], mixed[1]).astype(BF16)
+
+    def attend_step(i, carry):
+        tick(first + i)
+        attend(i)
+        return carry
+
+    lax.fori_loop(0, blocks, attend_step, 0)
+    after = first + blocks
+    ticking(after, max(0, ticks - after - 2 * tiles * 2))
+    after = max(after, ticks - 2 * tiles * 2)
+
+    def mix(i, carry):
+        h1 = hid[at_rows(i), :].astype(F32) + dg(ctx[at_rows(i), :], full[3], NN) + vecs[2:3, :]
+        value = layer_norm(h1, vecs[4 + ratio:5 + ratio, :], vecs[5 + ratio:6 + ratio, :])[0]
+        y1[at_rows(i), :] = value
+        low[at_rows(i), :] = value.astype(BF16)
+        acc[at_rows(i), :] = value + vecs[3 + ratio:4 + ratio, :]
+        return carry
+
+    lax.fori_loop(0, tiles, mix, 0)
+
+    def feed(i, carry):
+        k, at = i // tiles, at_rows(i % tiles)
+
+        @pl.when(after + i < ticks)
+        def _():
+            tick(after + i)
+
+        up = dg(low[at, :], full[4 + 2 * k], NT) + vecs[pl.ds(3 + k, 1), :]
+        acc[at, :] = acc[at, :] + dg(gelu(up).astype(BF16), full[5 + 2 * k], NN)
+        return carry
+
+    lax.fori_loop(0, ratio * tiles, feed, 0)
+
+    def close(i, carry):
+        layer[at_rows(i), :] = layer_norm(
+            acc[at_rows(i), :], vecs[6 + ratio:7 + ratio, :], vecs[7 + ratio:8 + ratio, :])[0].astype(BF16)
+        return carry
+
+    lax.fori_loop(0, tiles, close, 0)
 
     def finish(r, carry):
         @pl.when(z < line - 1)
@@ -231,33 +366,46 @@
         return carry
 
     lax.fori_loop(0, nmat, last, 0)
-
-
-def gather_weights(owners, slots, line):
+    for s in range(cap):
+        slot_copy(s).wait_send()
+
+
+def forward(owners, slots, hidden, vecs, line):
     cap, share, width = slots.shape
     nmat = owners.shape[0]
+    own_rows = hidden.shape[0] // 4
     quarter, half = share // 2, share // 4
     n = 2 * nmat
-    bf16 = jnp.bfloat16
     dma = pltpu.SemaphoreType.DMA
+    vmem = pl.BlockSpec(memory_space=pltpu.VMEM)
+    hbm = pl.BlockSpec(memory_space=pl.ANY)
+    rows = jax.ShapeDtypeStruct((own_rows, width), BF16)
     return pl.pallas_call(
-        functools.partial(gather_kernel, line, nmat, cap),
-        out_shape=jax.ShapeDtypeStruct((nmat, 4 * share, width), bf16),
-        in_specs=[pl.BlockSpec(memory_space=pltpu.SMEM), pl.BlockSpec(memory_space=pltpu.VMEM)],
-        out_specs=pl.BlockSpec(memory_space=pl.ANY),
+        functools.partial(forward_kernel, line, nmat, cap),
+        out_shape=(jax.ShapeDtypeStruct((nmat, 4 * share, width), BF16), rows, rows, rows),
+        in_specs=[pl.BlockSpec(memory_space=pltpu.SMEM), vmem, hbm, vmem],
+        out_specs=(hbm, vmem, vmem, vmem),
         scratch_shapes=[
-            pltpu.VMEM((nmat, 4 * share, width), bf16),
-            pltpu.VMEM((2 * cap, quarter, width), bf16),
-            pltpu.VMEM((n, half, width), bf16),
-            pltpu.VMEM((n, half, width), bf16),
+            pltpu.VMEM((nmat, 4 * share, width), BF16),
+            pltpu.VMEM((cap, share, width), BF16),
+            [pltpu.VMEM((2, quarter, width), BF16)] * cap,
+            pltpu.VMEM((half, width), BF16),
+            pltpu.VMEM((n, half, width), BF16),
+            pltpu.VMEM((n, half, width), BF16),
+            pltpu.VMEM((own_rows, width), BF16),
+            pltpu.VMEM((own_rows, width), BF16),
+            pltpu.VMEM((own_rows, width), BF16),
+            pltpu.VMEM((own_rows, width), F32),
+            pltpu.VMEM((own_rows, width), BF16),
+            pltpu.VMEM((own_rows, width), F32),
             pltpu.SMEM((nmat,), jnp.int32),
             pltpu.SMEM((nmat,), jnp.int32),
-            dma((2,)),
+            dma(()), dma((cap,)), dma((cap,)),
         ] + [dma((n,))] * 10 + [dma((nmat, 2)), dma((nmat, 2)), dma((nmat,))],
-        name="gather_weights",
+        name="forward",
         compiler_params=pltpu.CompilerParams(
-            collective_id=1, has_side_effects=True, vmem_limit_bytes=56 * 1024 * 1024),
-    )(owners, slots)
+            collective_id=1, has_side_effects=True, vmem_limit_bytes=58 * 1024 * 1024),
+    )(owners, slots, hidden, vecs)
 
 
 def reduce_kernel(line, order, cap, owners, grads, out, cin, hold, yo, yi, fr, fl, to, do, di,
@@ -421,26 +569,16 @@
         compiler_params=pltpu.CompilerParams(
             collective_id=2, has_side_effects=True, vmem_limit_bytes=56 * 1024 * 1024),
     )(owners, grads)
-HDIM = 64
-LEN = 512
+
+
 STEP = 10
 SPAN_ROWS = 96
-LN_EPS = 1e-12
 MATRIX_RATE = 0.03
 VECTOR_RATE = 0.25
 BETA_ONE = 0.5
 BETA_TWO = 0.5
 DECAY = 0.01
 ADAM_EPS = 1e-08
-BF16 = jnp.bfloat16
-F32 = jnp.float32
-
-
-def layer_norm(value, gain, shift):
-    center = value - jnp.mean(value, axis=-1, keepdims=True)
-    inverse = lax.rsqrt(jnp.mean(center * center, axis=-1, keepdims=True) + LN_EPS)
-    normed = center * inverse
-    return (normed * gain + shift, normed, inverse)
 
 
 def norm_back(grad, normed, inverse, gain):
@@ -480,8 +618,6 @@
     tokens = hidden_in.shape[0]
     own = tokens // 4
     nseq = own // LEN
-    pieces = gather_weights(owners, jnp.transpose(master_slots, (0, 2, 1)).astype(BF16), line)
-    wq, wk, wv, wo = pieces[0], pieces[1], pieces[2], pieces[3]
     b_up = vectors[3:3 + ratio].reshape(4, ratio, share).transpose(1, 0, 2).reshape(ratio, width)
     b_q, b_v, b_o, b_down = vectors[0], vectors[1], vectors[2], vectors[3 + ratio]
     gain_one, shift_one, gain_two, shift_two = (vectors[4 + ratio + i] for i in range(4))
@@ -495,19 +631,12 @@
         probs = jax.nn.softmax(scores, axis=-1)
         return dot("hqk,khd->qhd", probs.astype(BF16), v_blk).astype(BF16)
 
-    mine = lax.dynamic_slice_in_dim(hidden_in, rank_mp * own, own, 0)
-    q = (dot("td,sd->ts", mine, wq) + b_q).astype(BF16)
-    k = dot("td,sd->ts", mine, wk).astype(BF16)
-    v = (dot("td,sd->ts", mine, wv) + b_v).astype(BF16)
-    ctx = lax.map(attend, (split(q), split(k), split(v))).reshape(own, width)
-    first, _, _ = layer_norm(mine.astype(F32) + dot("ts,so->to", ctx, wo) + b_o, gain_one, shift_one)
-    low = first.astype(BF16)
-    second = first + b_down
-    for i in range(ratio):
-        act = jax.nn.gelu(dot("td,fd->tf", low, pieces[4 + i]) + b_up[i], approximate=False).astype(BF16)
-        second = second + dot("tf,fo->to", act, pieces[4 + ratio + i])
-    layer = layer_norm(second, gain_two, shift_two)[0].astype(BF16)
+    vecs = jnp.concatenate([vectors[:3], b_up, vectors[3 + ratio:]], axis=0)
+    flow, layer, k_own, v_own = forward(owners, jnp.transpose(master_slots, (0, 2, 1)), hidden_in, vecs, line)
     layer = lax.all_gather(layer, "mp", axis=0, tiled=True)
+    where = flow_order(nmat)
+    pieces = [flow[where.index(p)] for p in range(nmat)]
+    wq, wk, wv, wo = pieces[:4]
 
     def ours(v):
         v = v.reshape((2, 2, v.shape[0] // 4) + v.shape[1:])

time: 623 us -> 454 us (0.73)
  matrix products: 248 us -> 120 us
  local copies, waits for them, and re-layouts: 98.6 us -> 65.6 us
  other arithmetic: 31.5 us -> 23.2 us
    dot_general x55 -> x45, matrix products: 227 us -> 120 us  [dot(): return jnp.einsum(eq, a, b, preferred_element_type=F32)]
    sub x2 -> x0, matrix products: 20.4 us -> none  [attend(): probs = jax.nn.softmax(scores, axis=-1)]
    unnamed x188 -> x115, local copies, waits for them, and re-layouts: 31.5 us -> 24.1 us
  transfers between devices with their start and end apart: 2 -> 2, of which waited for: 0 -> 0; matrix products, arithmetic and copies ran while one was open for 39% -> 42% of each run, Pallas kernels for 14% -> 19%
where the time goes in v2:
time: 454 us; the launch traced here: 446 us
  Pallas kernels  184 us (41%)
  matrix products  120 us (26%)
  local copies, waits for them, and re-layouts  65.6 us (14%)
  blocking collectives  37.8 us (8%)
  other arithmetic  23.2 us (5%)
  between operations  15 us (3%)
    dot_general x45, matrix products, dot(): return jnp.einsum(eq, a, b, preferred_element_type=F32)  120 us
    pallas_call x1, Pallas kernels, forward(): pl.pallas_call(functools.partial(forward_kernel, line, nmat, cap), out_sh...  101 us
    pallas_call x1, Pallas kernels, reduce_grads(): pl.pallas_call(functools.partial(reduce_kernel, line, order, cap), out_sh...  83.5 us
    psum x1, blocking collectives, on_device(): vec_total = lax.psum(vec_grad, ('dp', 'mp')) * 0.5  37.8 us
    unnamed x115, local copies, waits for them, and re-layouts  24.1 us
  transfers between devices with their start and end apart: 2, of which 0 were waited for; matrix products, arithmetic and copies ran while one was open for 42% of the time, Pallas kernels for 19%

profile of v2, /device:TPU:0, one launch (start us, length us, event | category | flops | bytes accessed | tf_op | source)
XLA Modules:
  0.0 446.4 jit_solution(980723468671851613)
XLA Ops:
  10.3 100.9 %forward.1 = (bf16[12,768,768]{2,1,0:T(8,128)(2,1)}, bf16[1024,768]{1,0:T(8,128)(2,1)}, bf16[1024,768]{1,0:T(8,128)(2,1)}, bf16[1024,768]{1,0:T(8,128)(2,1)}) custom-call(s32[12]{0:T(128)} %owners.3, f32[4,192,768]{2,1,0:T(8,128)} %bitcast.264, bf16[4096,768]{1,0:T(8,128)(2,1)} %hidden.1, f32[12,768]{1,0:T(8,128)} %pad_maximum_fusion.vecs), custom_call_target="tpu_custom_call" | custom-call | tf_op jit(solution)/shard_map/forward/pallas_call | solution.py:383
  114.7 2.6 constant_dynamic-slice_fusion.1
  117.4 3.4 copy-done.16
  121.0 1.4 convolution_convert_fusion.12
  122.5 2.2 fusion.242
  124.8 3.0 fusion.33
  127.8 2.8 reshape.206
  130.6 2.8 copy.64
  133.4 5.3 %convolution_convert_fusion = bf16[2048,768]{1,0:T(8,128)(2,1)} fusion(bf16[2048,768]{1,0:T(8,128)(2,1)S(1)} %bitcast.257, bf16[12,768,768]{2,1,0:T(8,128)(2,1)} %get-tuple-element.11), kind=kOutput, calls=%fused_computation.13 | convolution fusion | flops 2417491968 | bytes 7471104 | tf_op jit(solution)/shard_map/td,sd->ts/dot_general | solution.py:607
  138.7 5.3 %add_convert_fusion = bf16[2048,768]{1,0:T(8,128)(2,1)} fusion(bf16[2048,768]{1,0:T(8,128)(2,1)S(1)} %bitcast.258, f32[768]{0:T(1024)S(1)} %get-tuple-element.25, bf16[12,768,768]{2,1,0:T(8,128)(2,1)} %get-tuple-element.11), kind=kOutput, calls=%fused_computation.8 | convolution fusion | flops 2419064832 | bytes 7474176 | tf_op jit(solution)/shard_map/td,sd->ts/dot_general | solution.py:607
  144.0 3.2 copy.57
  147.2 3.9 reshape.194
  151.1 3.2 copy.54
  154.3 3.9 reshape.193
  158.2 3.6 fusion.13
  161.8 4.6 %fusion.244 = (f32[4,12,96]{2,1,0:T(8,128)S(1)}, f32[4,12,96,512]{3,2,1,0:T(8,128)}) fusion(f32[4,12,96,512]{3,2,1,0:T(8,128)S(1)} %fusion.13), kind=kOutput, calls=%fused_computation.349 | output fusion | flops 9437695 | bytes 18892800 | tf_op jit(solution)/shard_map/sub | solution.py:662
  166.5 2.5 copy-done.2
  168.9 15.7 %fusion.45 = bf16[4,96,12,64]{1,3,2,0:T(8,128)(2,1)} fusion(bf16[4,512,12,64]{1,0,3,2:T(4,128)(2,1)S(1)} %copy-done.12, f32[4,12,96]{2,1,0:T(8,128)S(1)} %get-tuple-element.44, f32[4,12,96,512]{3,2,1,0:T(8,128)} %copy-done.2), kind=kOutput, calls=%fused_computation.87 | convolution fusion | flops 314086400 | bytes 13191168 | tf_op jit(solution)/shard_map/shqk,skhd->sqhd/dot_general | solution.py:607
  184.6 1.8 copy.59
  187.0 2.2 fusion.245
  189.8 5.0 %fusion.96 = (bf16[384,768]{1,0:T(8,128)(2,1)S(1)}, f32[384,768]{1,0:T(8,128)S(1)}) fusion(f32[768]{0:T(1024)S(1)} %add.268, bf16[384,768]{1,0:T(8,128)(2,1)S(1)} %fusion.168, bf16[12,768,768]{2,1,0:T(8,128)(2,1)} %get-tuple-element.11), kind=kOutput, calls=%fused_computation.124 | convolution fusion | flops 472449024 | bytes 3542016 | tf_op jit(solution)/shard_map/td,fd->tf/dot_general | solution.py:607
  195.0 3.6 fusion.93
  198.6 3.6 fusion.90
  202.3 4.0 fusion.87
  218.6 1.5 convolution_convert_fusion.11
  220.1 1.9 reshape.207
  222.1 1.8 copy.62
  223.9 14.1 %convert_reduce_fusion = (f32[12,64]{1,0:T(8,128)S(1)}, bf16[4,512,12,64]{1,3,2,0:T(8,128)(2,1)}) fusion(bf16[4,96,12,64]{1,3,2,0:T(8,128)(2,1)} %copy.62, f32[4,12,96]{2,1,0:T(8,128)S(1)} %get-tuple-element.44, f32[4,12,96,512]{3,2,1,0:T(8,128)} %copy-done.2), kind=kOutput, calls=%fused_computation.6 | convolution fusion | flops 318509312 | bytes 13194240 | tf_op jit(solution)/shard_map/shqk,sqhd->skhd/dot_general | solution.py:607
  238.0 4.3 copy.67
  242.3 2.7 copy.78
  245.1 6.7 %multiply_reduce_fusion = (f32[4,12,96]{2,1,0:T(8,128)S(1)}, f32[4,12,96,512]{3,2,1,0:T(8,128)S(1)}) fusion(f32[4,12,96,512]{3,2,1,0:T(8,128)} %get-tuple-element.45, f32[4,12,96]{2,1,0:T(8,128)S(1)} %get-tuple-element.44, bf16[4,96,12,64]{1,3,2,0:T(8,128)(2,1)S(1)} %copy-done.19, bf16[4,512,12,64]{1,0,3,2:T(4,128)(2,1)} %reshape.194), kind=kOutput, calls=%fused_computation.2 | convolution fusion | flops 309063168 | bytes 22646784 | tf_op jit(solution)/shard_map/sqhd,skhd->shqk/dot_general | solution.py:607
  252.4 1.9 multiply_convert_fusion
  255.3 2.4 copy.65
  257.7 2.7 copy.77
  260.4 1.9 convert_reduce_fusion.1
  263.5 2.0 fusion.38
  267.4 4.1 fusion.135
  271.5 4.2 fusion.132
  275.7 1.6 fusion.6
  278.6 2.5 fusion.66
  281.1 2.4 fusion.68
  294.1 2.2 fusion.62
  296.3 2.2 fusion.56.grads
  298.6 83.5 %reduce_grads.1 = f32[4,192,768]{2,1,0:T(8,128)} custom-call(s32[12]{0:T(128)} %owners.3, bf16[12,384,768]{2,1,0:T(8,128)(2,1)} %fusion.56.grads), custom_call_target="tpu_custom_call" | custom-call | tf_op jit(solution)/shard_map/reduce_grads/pallas_call | solution.py:550
  382.2 37.8 %psum.7 = f32[12,768]{1,0:T(8,128)S(1)} all-reduce(f32[12,768]{1,0:T(8,128)S(1)} %concatenate.8), channel_id=1, replica_groups=mesh['dp'=8,'mp'=4] {'dp','mp'}, use_global_device_ids=true, to_apply=%region_26.27 | all-reduce | flops 9216 | bytes 73728 | tf_op jit(solution)/shard_map/psum | solution.py:719
  421.9 8.7 %broadcast_multiply_fusion = (f32[4,768,192]{1,2,0:T(8,128)}, f32[4,768,192]{1,2,0:T(8,128)}, f32[4,768,192]{1,2,0:T(8,128)}) fusion(f32[4]{0:T(128)S(1)} %compare_convert_fusion, f32[4,192,768]{2,1,0:T(8,128)} %reduce_grads.1, f32[4,768,192]{1,2,0:T(8,128)} %param.19, f32[4,768,192]{1,2,0:T(8,128)S(1)} %copy-done.7, f32[4,768,192]{1,2,0:T(8,128)} %param.18), kind=kLoop, calls=%fused_computation.170 | loop fusion | flops 10027008 | bytes 16515088 | tf_op jit(solution)/shard_map/mul | solution.py:728
  430.6 6.0 %copy.116 = bf16[4096,768]{1,0:T(8,128)(2,1)} copy(bf16[4096,768]{1,0:T(8,128)(2,1)} %all-gather.3.cloned.1.call-done) | data formatting | bytes 12582912
  436.7 2.7 copy.117
  (198 shorter events, 38.8 us)
Async XLA Ops:
  7.2 105.3 %copy-start = (s32[8,24,2]{1,2,0:T(2,128)S(1)}, s32[8,24,2]{1,2,0:T(2,128)}, u32[]{:S(2)}) copy-start(s32[8,24,2]{1,2,0:T(2,128)} %param.12) | copy-start | bytes 4612
  7.2 423.5 %all-gather.3.cloned.1.call-start = ((), (), s32[]{:S(2)}) async-start(), calls=%async_computation | async-start | bytes 7864320 | tf_op jit(solution)/shard_map/all_gather | solution.py:636
  111.2 319.4 %all-gather.5.cloned.1.call-start = ((), (), s32[]{:S(2)}) async-start(), calls=%async_computation.1 | async-start | bytes 7864320 | tf_op jit(solution)/shard_map/all_gather | solution.py:714
  112.7 9.8 %copy-start.39 = (pred[4,512]{1,0:T(4,128)(4,1)}, pred[4,512]{1,0:T(4,128)(4,1)S(1)}, u32[]{:S(2)}) copy-start(pred[4,512]{1,0:T(4,128)(4,1)S(1)} %fusion.216) | copy-start | bytes 6148
  114.4 8.0 %copy-start.37 = (s32[1,4,4,128]{3,1,2,0:T(4,128)}, s32[1,4,4,128]{3,1,2,0:T(4,128)S(1)}, u32[]{:S(2)}) copy-start(s32[1,4,4,128]{3,1,2,0:T(4,128)S(1)} %copy.102) | copy-start | bytes 24580
  114.7 6.1 %copy-start.16 = (bf16[4096,768]{1,0:T(8,128)(2,1)S(1)}, bf16[4096,768]{1,0:T(8,128)(2,1)}, u32[]{:S(2)}) copy-start(bf16[4096,768]{1,0:T(8,128)(2,1)} %param.11) | copy-start | bytes 18874372
  117.4 21.3 %copy-start.3 = (bf16[2,1,1024,768]{3,2,1,0:T(8,128)(2,1)}, bf16[2,1,1024,768]{3,2,1,0:T(8,128)(2,1)S(1)}, u32[]{:S(2)}) copy-start(bf16[2,1,1024,768]{3,2,1,0:T(8,128)(2,1)S(1)} %constant_dynamic-slice_fusion.1) | copy-start | bytes 9437188
  161.8 7.1 %copy-start.2 = (f32[4,12,96,512]{3,2,1,0:T(8,128)}, f32[4,12,96,512]{3,2,1,0:T(8,128)S(1)}, u32[]{:S(2)}) copy-start(f32[4,12,96,512]{3,2,1,0:T(8,128)S(1)} %fusion.13) | copy-start | bytes 28311556
  161.8 7.1 %copy-start.12 = (bf16[4,512,12,64]{1,0,3,2:T(4,128)(2,1)S(1)}, bf16[4,512,12,64]{1,0,3,2:T(4,128)(2,1)}, u32[]{:S(2)}) copy-start(bf16[4,512,12,64]{1,0,3,2:T(4,128)(2,1)} %reshape.194) | copy-start | bytes 9437188
  184.6 2.3 copy-start.15
  187.0 2.3 copy-start.17
  189.3 5.6 %slice-start.3 = ((s8[14155776]{0:T(1024)(128)(4,1)}), s8[4194304]{0:T(1024)(128)(4,1)S(1)}, s32[]{:S(2)}) async-start(s8[14155776]{0:T(1024)(128)(4,1)} %bitcast.265), calls=%async_computation.5 | async-start | bytes 8388608
  189.8 12.4 %copy-start.22 = (bf16[384,768]{1,0:T(8,128)(2,1)}, bf16[384,768]{1,0:T(8,128)(2,1)S(1)}, u32[]{:S(2)}) copy-start(bf16[384,768]{1,0:T(8,128)(2,1)S(1)} %fusion.168) | copy-start | bytes 1769476
  189.8 5.0 %slice-start.4 = ((s8[14155776]{0:T(1024)(128)(4,1)}), s8[4194304]{0:T(1024)(128)(4,1)S(1)}, s32[]{:S(2)}) async-start(s8[14155776]{0:T(1024)(128)(4,1)} %bitcast.265), calls=%async_computation.6 | async-start | bytes 8388608
  189.8 5.0 %slice-start.5 = ((s8[14155776]{0:T(1024)(128)(4,1)}), s8[4194304]{0:T(1024)(128)(4,1)S(1)}, s32[]{:S(2)}) async-start(s8[14155776]{0:T(1024)(128)(4,1)} %bitcast.265), calls=%async_computation.7 | async-start | bytes 8388608
  189.8 5.1 %slice-start.6 = ((s8[14155776]{0:T(1024)(128)(4,1)}), s8[1572864]{0:T(1024)(128)(4,1)S(1)}, s32[]{:S(2)}) async-start(s8[14155776]{0:T(1024)(128)(4,1)} %bitcast.265), calls=%async_computation.8 | async-start | bytes 3145728
  195.0 13.5 %copy-start.20 = (bf16[384,768]{1,0:T(8,128)(2,1)}, bf16[384,768]{1,0:T(8,128)(2,1)S(1)}, u32[]{:S(2)}) copy-start(bf16[384,768]{1,0:T(8,128)(2,1)S(1)} %get-tuple-element.54) | copy-start | bytes 1769476
  198.6 9.2 %copy-start.25 = (bf16[384,768]{1,0:T(8,128)(2,1)}, bf16[384,768]{1,0:T(8,128)(2,1)S(1)}, u32[]{:S(2)}) copy-start(bf16[384,768]{1,0:T(8,128)(2,1)S(1)} %get-tuple-element.52) | copy-start | bytes 1769476
  202.2 4.9 %copy-start.27 = (bf16[384,768]{1,0:T(8,128)(2,1)}, bf16[384,768]{1,0:T(8,128)(2,1)S(1)}, u32[]{:S(2)}) copy-start(bf16[384,768]{1,0:T(8,128)(2,1)S(1)} %get-tuple-element.50) | copy-start | bytes 1769476
  211.4 5.0 %copy-start.29 = (bf16[384,768]{1,0:T(8,128)(2,1)}, bf16[384,768]{1,0:T(8,128)(2,1)S(1)}, u32[]{:S(2)}) copy-start(bf16[384,768]{1,0:T(8,128)(2,1)S(1)} %get-tuple-element.31) | copy-start | bytes 1769476
  242.3 2.7 copy-start.19
  245.1 6.7 %slice-start = ((s8[9437184]{0:T(1024)(128)(4,1)}), s8[4194304]{0:T(1024)(128)(4,1)S(1)}, s32[]{:S(2)}) async-start(s8[9437184]{0:T(1024)(128)(4,1)} %bitcast.252), calls=%async_computation.2 | async-start | bytes 8388608
  245.1 7.1 %slice-start.1 = ((s8[9437184]{0:T(1024)(128)(4,1)}), s8[4194304]{0:T(1024)(128)(4,1)S(1)}, s32[]{:S(2)}) async-start(s8[9437184]{0:T(1024)(128)(4,1)} %bitcast.252), calls=%async_computation.3 | async-start | bytes 8388608
  245.1 7.3 %slice-start.2 = ((s8[9437184]{0:T(1024)(128)(4,1)}), s8[1048576]{0:T(1024)(128)(4,1)S(1)}, s32[]{:S(2)}) async-start(s8[9437184]{0:T(1024)(128)(4,1)} %bitcast.252), calls=%async_computation.4 | async-start | bytes 2097152
  252.4 1.9 copy-start.8
  257.7 2.7 copy-start.5
  263.4 2.0 copy-start.38
  263.5 2.0 copy-start.40
  265.5 1.9 copy-start.13
  267.4 4.1 copy-start.10
  277.3 3.7 copy-start.23
  281.1 2.4 copy-start.28
  281.1 2.4 copy-start.30
  283.5 1.4 copy-start.33
  284.9 1.3 copy-start.26
  287.5 1.3 copy-start.21
  287.5 2.7 copy-start.46
  287.5 4.0 copy-start.18
  288.9 5.3 %copy-start.4 = (bf16[2,1,1024,768]{3,2,1,0:T(8,128)(2,1)S(1)}, bf16[2,1,1024,768]{3,2,1,0:T(8,128)(2,1)}, u32[]{:S(2)}) copy-start(bf16[2,1,1024,768]{3,2,1,0:T(8,128)(2,1)} %copy-done.3) | copy-start | bytes 9437188
  291.5 2.6 copy-start.14
  294.1 2.2 copy-start.11
  298.6 121.3 %copy-start.44 = (s32[12]{0:T(128)S(1)}, s32[12]{0:T(128)}, u32[]{:S(2)}) copy-start(s32[12]{0:T(128)} %owners.3) | copy-start | bytes 148
  298.6 122.6 %copy-start.36 = (f32[12,768]{1,0:T(8,128)S(1)}, f32[12,768]{1,0:T(8,128)}, u32[]{:S(2)}) copy-start(f32[12,768]{1,0:T(8,128)} %param.14) | copy-start | bytes 110596
  298.6 122.7 %copy-start.41 = (f32[12,768]{1,0:T(8,128)S(1)}, f32[12,768]{1,0:T(8,128)}, u32[]{:S(2)}) copy-start(f32[12,768]{1,0:T(8,128)} %param.15) | copy-start | bytes 110596
  298.6 122.7 %copy-start.42 = (f32[12,768]{1,0:T(8,128)S(1)}, f32[12,768]{1,0:T(8,128)}, u32[]{:S(2)}) copy-start(f32[12,768]{1,0:T(8,128)} %param.16) | copy-start | bytes 110596
  298.6 123.3 %copy-start.7 = (f32[4,768,192]{1,2,0:T(8,128)S(1)}, f32[4,768,192]{1,2,0:T(8,128)}, u32[]{:S(2)}) copy-start(f32[4,768,192]{1,2,0:T(8,128)} %param.17) | copy-start | bytes 7077892
  430.6 6.0 %copy-start.9 = (bf16[4096,768]{1,0:T(8,128)(2,1)S(1)}, bf16[4096,768]{1,0:T(8,128)(2,1)}, u32[]{:S(2)}) copy-start(bf16[4096,768]{1,0:T(8,128)(2,1)} %all-gather.5.cloned.1.call-done) | copy-start | bytes 18874372
  436.7 2.7 copy-start.1
  (9 other events, 8.9 us)
Sparse Core Ops, SparseCore 0:
  111.4 43.8 all-gather.2
  277.5 43.4 all-gather.4

commit v3 on v2

--- a/solution.py
+++ b/solution.py
@@ -408,190 +408,516 @@
     )(owners, slots, hidden, vecs)
 
 
-def reduce_kernel(line, order, cap, owners, grads, out, cin, hold, yo, yi, fr, fl, to, do, di,
-                  who, pick, cs, cr, ysd, yr, sr, rl, sl, rr, dsem):
-    nmat = len(order)
-    share = grads.shape[1] // 2
-    quarter = share // 2
-    f32, bf16 = jnp.float32, jnp.bfloat16
+SPAN_ROWS = 96
+
+
+def norm_back(grad, normed, inverse, gain):
+    scaled = grad * gain
+    first = jnp.mean(scaled, axis=-1, keepdims=True)
+    second = jnp.mean(scaled * normed, axis=-1, keepdims=True)
+    return inverse * (scaled - first - normed * second)
+
+
+def column_sum(value):
+    return jnp.sum(value, axis=0, keepdims=True)
+
+
+def backward_kernel(line, nmat, cap, owners, spans, vecs, flow, hidden, incoming, layer, k_own, v_own,
+                    sg, vec_out, lay, gin,
+                    full, hid, k_ref, v_ref, pick, probs, hm, gm, qm, ctx, n1, inv1, low, acc,
+                    slope, act, df, dq, gqkv, gvec, vin, vz,
+                    cin, hold, yi, fr, fl, do, di, slot_pick,
+                    w_sem, in_sem, lsem_s, lsem_r, gsem_s, gsem_r, loc_sem,
+                    cs, cr, ysd, yr, sr, rl, sl, rr, dsem, vs, vr, vzs, vzr):
+    ratio = (nmat - 4) // 2
+    width = vecs.shape[1]
+    share = cin.shape[1]
+    quarter, half = share // 2, share // 4
+    nchunk = 2 * nmat
     z, y, x, c = place()
-    to_y, to_c = device(z, 1 - y, x, c), device(z, y, x, 1 - c)
+    me, over = 2 * x + c, 2 * (1 - x) + c
+    to_y, to_x, to_c = device(z, 1 - y, x, c), device(z, y, 1 - x, c), device(z, y, x, 1 - c)
+    own_rows = layer.shape[0]
+    nseq = 2 * own_rows // LEN
+    per = own_rows // LEN
     greet(line)
 
+    def rows(start, size):
+        return pl.ds(pl.multiple_of(start, 16), size)
+
+    def block_copy(src, dst, b, sem):
+        return pltpu.make_async_copy(
+            src.at[rows((2 * b + c) * own_rows, own_rows)], dst.at[pl.ds(b * own_rows, own_rows)], sem)
+
+    loads = [block_copy(hidden, hid, b, in_sem.at[b]) for b in range(2)]
+    loads += [block_copy(incoming, v_ref, b, in_sem.at[2 + b]) for b in range(2)]
+    loads += [pltpu.make_async_copy(src, dst.at[rows(x * own_rows, own_rows)], in_sem.at[4 + i])
+              for i, (src, dst) in enumerate(((k_own, k_ref), (v_own, v_ref)))]
+    for copy in loads[:4]:
+        copy.start()
+    for j in range(nmat):
+        pltpu.make_async_copy(flow.at[j], full.at[j], w_sem.at[j]).start()
+
+    def lay_rows(b):
+        return lay.at[rows(b * own_rows, own_rows)]
+
+    lay_x = rcopy(layer, lay_rows(me), lsem_s.at[0], lsem_r.at[0], to_x)
+    lay_x_came = rcopy(layer, lay_rows(over), lsem_s.at[0], lsem_r.at[0], to_x)
+    lay_c = rcopy(layer, lay_rows(me), lsem_s.at[1], lsem_r.at[1], to_c)
+    lay_c_came = rcopy(layer, lay_rows(2 * x + 1 - c), lsem_s.at[1], lsem_r.at[1], to_c)
+    lay_d = rcopy(lay_rows(over), lay_rows(over), lsem_s.at[2], lsem_r.at[2], to_c)
+    lay_d_came = rcopy(layer, lay_rows(2 * (1 - x) + 1 - c), lsem_s.at[2], lsem_r.at[2], to_c)
+    lay_own = pltpu.make_async_copy(layer, lay_rows(me), loc_sem.at[0])
+    lay_x.start()
+    lay_c.start()
+    lay_own.start()
+
+    order = tuple(p for k in range(ratio) for p in (4 + ratio + k, 4 + k)) + (3, 0, 1, 2)
     for s in range(2 * cap):
-        pick[s] = 0
+        slot_pick[s] = 0
     for j, p in enumerate(order):
         mine = owners[p]
         place_of = jnp.int32(0)
         for q in range(p):
             place_of += jnp.where(owners[q] == mine, 1, 0).astype(jnp.int32)
-        who[j] = mine // 2
         slot = (mine % 2) * cap + jnp.minimum(place_of, cap - 1)
         for s in range(2 * cap):
-            pick[s] = jnp.where((mine // 2 == z) & (slot == s), j, pick[s])
-
-    def rows(start, size):
-        return pl.ds(pl.multiple_of(start, 16), size)
-
-    def core_copy(j):
-        return rcopy(grads.at[j, rows((1 - c) * share, share), :], cin.at[j], cs.at[j], cr.at[j], to_c)
-
-    def y_copy(j):
-        return rcopy(yo.at[j], yi.at[j], ysd.at[j], yr.at[j], to_y)
-
-    def right(j):
-        return rcopy(to.at[0, j], fr.at[j], sr.at[j], rl.at[j], device(z + 1, y, x, c))
-
-    def left(j):
-        return rcopy(to.at[1, j], fl.at[j], sl.at[j], rr.at[j], device(z - 1, y, x, c))
-
-    def stage0(j):
-        core_copy(j).start()
-
-    def stage1(j):
-        core_copy(j).wait_recv()
-        for part in range(2):
-            at = y if part == 0 else 1 - y
-            total = (grads[j, rows(c * share + at * quarter, quarter), :].astype(f32)
-                     + cin[j, rows(at * quarter, quarter), :].astype(f32))
-            if part == 0:
-                hold[j] = total
+            slot_pick[s] = jnp.where((mine // 2 == z) & (slot == s), j, slot_pick[s])
+
+    def core_copy(j, src):
+        return rcopy(src.at[rows((1 - c) * share, share), :], cin.at[j], cs.at[j], cr.at[j], to_c)
+
+    def grad_of(j):
+        if isinstance(j, int) and j >= 2 * ratio + 1:
+            return gqkv.at[j - 2 * ratio - 1]
+        if isinstance(j, int) and j == 2 * ratio:
+            return full.at[3]
+        return full.at[4 + j + 1 - 2 * (j % 2), pl.ds(0, 2 * share), :]
+
+    def part(at, h):
+        return rows(at * quarter + h * half, half)
+
+    def y_copy(r):
+        return rcopy(cin.at[r // 2, part(1 - y, r % 2), :], yi.at[r], ysd.at[r], yr.at[r], to_y)
+
+    def right(r):
+        return rcopy(yi.at[r], fr.at[r], sr.at[r], rl.at[r], device(z + 1, y, x, c))
+
+    def left(r):
+        return rcopy(cin.at[r // 2, part(y, r % 2), :], fl.at[r], sl.at[r], rr.at[r], device(z - 1, y, x, c))
+
+    def stage1(r):
+        j, h = r // 2, r % 2
+
+        @pl.when(h == 0)
+        def _():
+            core_copy(j, gqkv.at[0]).wait_recv()
+
+        def add(src):
+            for at in (1 - y, y):
+                value = (src[rows(c * share + at * quarter + h * half, half), :].astype(F32)
+                         + cin[j, part(at, h), :].astype(F32))
+                if at is y:
+                    hold[r] = value
+                else:
+                    cin[j, part(at, h), :] = value.astype(BF16)
+
+        @pl.when(j < 2 * ratio)
+        def _():
+            add(full.at[4 + j + 1 - 2 * (j % 2)])
+
+        @pl.when(j == 2 * ratio)
+        def _():
+            add(full.at[3])
+
+        @pl.when(j > 2 * ratio)
+        def _():
+            add(gqkv.at[j - 2 * ratio - 1])
+
+        y_copy(r).start()
+
+    def stage2(r):
+        y_copy(r).wait_recv()
+        hold[r] = hold[r] + yi[r].astype(F32)
+
+    def flow_right(r):
+        @pl.when(z == 0)
+        def _():
+            yi[r] = hold[r].astype(BF16)
+
+        @pl.when(z > 0)
+        def _():
+            right(r).wait_recv()
+            yi[r] = (hold[r] + fr[r].astype(F32)).astype(BF16)
+
+        @pl.when(z < line - 1)
+        def _():
+            right(r).start()
+
+    def flow_left(r):
+        at = part(y, r % 2)
+
+        @pl.when(z == line - 1)
+        def _():
+            cin[r // 2, at, :] = hold[r].astype(BF16)
+
+        @pl.when(z < line - 1)
+        def _():
+            left(r).wait_recv()
+            cin[r // 2, at, :] = (hold[r] + fl[r].astype(F32)).astype(BF16)
+
+        @pl.when(z > 0)
+        def _():
+            left(r).start()
+
+    def ranged(r, do_it):
+        pl.when((r >= 0) & (r < nchunk))(functools.partial(do_it, r))
+
+    lag = 3
+    ticks = nchunk + lag + 2 * (line - 1)
+
+    def tick(t):
+        ranged(t, stage1)
+        ranged(t - 2, stage2)
+        ranged(t - lag - 2 * z, flow_right)
+        ranged(t - lag - 2 * (line - 1 - z), flow_left)
+
+    def ticking(start, stop):
+        def body(t, carry):
+            tick(t)
+            return carry
+
+        lax.fori_loop(start, stop, body, 0)
+
+    position = lax.broadcasted_iota(jnp.int32, (8, LEN), 1)
+    upper = (lax.broadcasted_iota(jnp.int32, (LEN, LEN), 0)
+             <= lax.broadcasted_iota(jnp.int32, (LEN, LEN), 1)).astype(F32).astype(BF16)
+    row_of = lax.broadcasted_iota(jnp.int32, (SPAN_ROWS, LEN), 0).astype(F32)
+    for copy in loads[:4]:
+        copy.wait()
+
+    def cover(s, carry):
+        seq = (2 * (s // per) + c) * per + s % per
+        seen = jnp.zeros((8, LEN), F32)
+        for n in range(spans.shape[1]):
+            start, size = spans[seq, n, 0], spans[seq, n, 1]
+            seen = jnp.where((position >= start) & (position < start + size), 1.0, seen)
+        rank = dg(seen.astype(BF16), upper, NN)
+        chosen = jnp.where((rank[0:1, :] - 1.0 == row_of) & (seen[0:1, :] > 0.0), 1.0, 0.0).astype(BF16)
+        pick[s] = chosen
+        at, span = rows(s * LEN, LEN), rows(s * SPAN_ROWS, SPAN_ROWS)
+        hm[span, :] = dg(chosen, hid[at, :], NN).astype(BF16)
+        gm[span, :] = dg(chosen, v_ref[at, :], NN).astype(BF16)
+        return carry
+
+    lax.fori_loop(0, nseq, cover, 0)
+
+    for copy in loads[4:]:
+        copy.start()
+
+    for j in range(3):
+        pltpu.make_async_copy(flow.at[j], full.at[j], w_sem.at[j]).wait()
+    for i in range(per):
+        at = rows((1 - x) * own_rows + i * LEN, LEN)
+        k_ref[at, :] = dg(hid[at, :], full[1], NT).astype(BF16)
+        v_ref[at, :] = (dg(hid[at, :], full[2], NT) + vecs[1:2, :]).astype(BF16)
+    qm[...] = (dg(hm[...], full[0], NT) + vecs[0:1, :]).astype(BF16)
+    for copy in loads[4:]:
+        copy.wait()
+    pairs = width // (2 * HDIM)
+    left_half = lax.broadcasted_iota(jnp.int32, (SPAN_ROWS, 2 * HDIM), 1) < HDIM
+    scale = HDIM ** -0.5
+
+    def stacked(value):
+        zero = jnp.zeros_like(value)
+        return jnp.concatenate([jnp.where(left_half, value, zero), jnp.where(left_half, zero, value)], axis=0)
+
+    def merged(value):
+        return jnp.where(left_half, value[:SPAN_ROWS], value[SPAN_ROWS:])
+
+    def places(i):
+        s, pair = i // pairs, i % pairs
+        return (rows(s * LEN, LEN), rows(s * SPAN_ROWS, SPAN_ROWS),
+                pl.ds(pl.multiple_of(pair * (2 * HDIM), 2 * HDIM), 2 * HDIM))
+
+    def attend(i, carry):
+        at, span, lanes = places(i)
+        scores = dg(stacked(qm[span, lanes]), k_ref[at, lanes], NT) * scale
+        raised = jnp.exp(scores - jnp.max(scores, axis=-1, keepdims=True))
+        value = (raised / jnp.sum(raised, axis=-1, keepdims=True)).astype(BF16)
+        probs[i] = value
+        ctx[span, lanes] = merged(dg(value, v_ref[at, lanes], NN)).astype(BF16)
+        return carry
+
+    lax.fori_loop(0, nseq * pairs, attend, 0)
+    for j in range(3, nmat):
+        pltpu.make_async_copy(flow.at[j], full.at[j], w_sem.at[j]).wait()
+    h1 = hm[...].astype(F32) + dg(ctx[...], full[3], NN) + vecs[2:3, :]
+    first, normed, inverse = layer_norm(h1, vecs[4 + ratio:5 + ratio, :], vecs[5 + ratio:6 + ratio, :])
+    n1[...] = normed
+    inv1[...] = inverse
+    low[...] = first.astype(BF16)
+    acc[...] = first + vecs[3 + ratio:4 + ratio, :]
+
+    def feed(k, carry):
+        up = dg(low[...], full[4 + 2 * k], NT) + vecs[pl.ds(3 + k, 1), :]
+        cdf = 0.5 * (1.0 + lax.erf(up * 2.0 ** (-0.5)))
+        active = (up * cdf).astype(BF16)
+        act[k] = active
+        slope[k] = (cdf + up * (jnp.exp(-0.5 * up * up) * (2.0 * jnp.pi) ** (-0.5))).astype(BF16)
+        acc[...] = acc[...] + dg(active, full[5 + 2 * k], NN)
+        return carry
+
+    lax.fori_loop(0, ratio, feed, 0)
+    _, normed, inverse = layer_norm(acc[...], vecs[6 + ratio:7 + ratio, :], vecs[7 + ratio:8 + ratio, :])
+    given = gm[...].astype(F32)
+    gvec[6 + ratio:7 + ratio, :] = column_sum(given * normed)
+    gvec[7 + ratio:8 + ratio, :] = column_sum(given)
+    back = norm_back(given, normed, inverse, vecs[6 + ratio:7 + ratio, :])
+    acc[...] = back
+    df[...] = back.astype(BF16)
+    gvec[3 + ratio:4 + ratio, :] = column_sum(back.astype(BF16).astype(F32))
+    halves = pl.ds(pl.multiple_of(x * 2 * share, 128), 2 * share)
+
+    def feed_back(k, carry):
+        d_up = (dg(df[...], full[5 + 2 * k], NT) * slope[k].astype(F32)).astype(BF16)
+        gvec[pl.ds(3 + k, 1), :] = column_sum(d_up.astype(F32))
+        acc[...] = acc[...] + dg(d_up, full[4 + 2 * k], NN)
+        act_k = act[k, :, halves]
+        act[k] = d_up
+        full[5 + 2 * k, pl.ds(0, 2 * share), :] = dg(act_k, df[...], TN).astype(BF16)
+        core_copy(2 * k, full.at[5 + 2 * k]).start()
+        full[4 + 2 * k, pl.ds(0, 2 * share), :] = dg(act[k, :, halves], low[...], TN).astype(BF16)
+        core_copy(2 * k + 1, full.at[4 + 2 * k]).start()
+        tick(k)
+        return carry
+
+    lax.fori_loop(0, ratio, feed_back, 0)
+    done = ratio
+    gvec[4 + ratio:5 + ratio, :] = column_sum(acc[...] * n1[...])
+    gvec[5 + ratio:6 + ratio, :] = column_sum(acc[...])
+    back = norm_back(acc[...], n1[...], inv1[...], vecs[4 + ratio:5 + ratio, :])
+    acc[...] = back
+    da = back.astype(BF16)
+    gvec[2:3, :] = column_sum(da.astype(F32))
+    df[...] = da
+    low[...] = dg(da, full[3], NT).astype(BF16)
+    full[3, pl.ds(0, 2 * share), :] = dg(ctx[:, halves], da, TN).astype(BF16)
+    core_copy(2 * ratio, full.at[3]).start()
+    tick(done)
+    done += 1
+
+    def attend_back(i, carry):
+        at, span, lanes = places(i)
+        d_two = stacked(low[span, lanes])
+        given = probs[i]
+        value = given.astype(F32)
+        keys = k_ref[at, lanes]
+        d_probs = dg(d_two, v_ref[at, lanes], NT)
+        mean = jnp.sum(value * d_probs, axis=-1, keepdims=True)
+        ds = (value * (d_probs - mean)).astype(BF16)
+        dq[span, lanes] = (merged(dg(ds, keys, NN)) * scale).astype(BF16)
+        k_ref[at, lanes] = (dg(ds, stacked(qm[span, lanes]), TN) * scale).astype(BF16)
+        v_ref[at, lanes] = dg(given, d_two, TN).astype(BF16)
+        return carry
+
+    every = 3
+    for i in range(0, nseq * pairs, every):
+        lax.fori_loop(i, min(i + every, nseq * pairs), attend_back, 0)
+        tick(done)
+        done += 1
+    gvec[0:1, :] = column_sum(dq[...].astype(F32))
+    gqkv[0] = dg(dq[:, halves], hm[...], TN).astype(BF16)
+    core_copy(2 * ratio + 1, gqkv.at[0]).start()
+    for which, src in ((1, k_ref), (2, v_ref)):
+        def some(i, carry, src=src):
+            at = rows(i * LEN, LEN)
+            return carry + dg(src[at, halves], hid[at, :], TN)
+
+        gqkv[which] = lax.fori_loop(0, nseq, some, jnp.zeros((2 * share, width), F32)).astype(BF16)
+        core_copy(2 * ratio + 1 + which, gqkv.at[which]).start()
+        tick(done)
+        done += 1
+
+    def sum_v(i, carry):
+        return carry + column_sum(v_ref[rows(i * LEN, LEN), :].astype(F32))
+
+    gvec[1:2, :] = lax.fori_loop(0, nseq, sum_v, jnp.zeros((1, width), F32))
+
+    def vec_copy(k, who_to):
+        return rcopy(gvec, vin.at[k], vs.at[k], vr.at[k], who_to)
+
+    vec_copy(0, to_c).start()
+    qm[...] = (acc[...] + dg(dq[...], full[0], NN)).astype(BF16)
+    vec_copy(0, to_c).wait()
+    gvec[...] = gvec[...] + vin[0]
+    vec_copy(1, to_y).start()
+
+    def gin_rows(s, core):
+        return gin.at[rows((2 * (s // per) + core) * own_rows + (s % per) * LEN, LEN)]
+
+    def gin_copy(s):
+        return rcopy(hid.at[rows(s * LEN, LEN)], gin_rows(s, c), gsem_s.at[s], gsem_r.at[s], to_c)
+
+    def gin_came(s):
+        return rcopy(hid.at[rows(s * LEN, LEN)], gin_rows(s, 1 - c), gsem_s.at[s], gsem_r.at[s], to_c)
+
+    def gin_own(s):
+        return pltpu.make_async_copy(hid.at[rows(s * LEN, LEN)], gin_rows(s, c), loc_sem.at[1 + s])
+
+    base = done
+
+    def spread(s, carry):
+        at, span = rows(s * LEN, LEN), rows(s * SPAN_ROWS, SPAN_ROWS)
+        total = dg(k_ref[at, :], full[1], NN) + dg(v_ref[at, :], full[2], NN) + dg(pick[s], qm[span, :], TN)
+        hid[at, :] = total.astype(BF16)
+        gin_copy(s).start()
+        gin_own(s).start()
+        tick(base + s)
+        return carry
+
+    lax.fori_loop(0, nseq, spread, 0)
+    done = base + nseq
+    vec_copy(1, to_y).wait()
+    vz[z] = gvec[...] + vin[1]
+
+    def vec_flow(step, send):
+        def one(near, ok_send, ok_recv, direction, slot_out, slot_in):
+            copy = rcopy(vz.at[slot_out], vz.at[slot_out], vzs.at[direction, step], vzr.at[slot_out], near)
+            if send:
+                pl.when(ok_send)(copy.start)
             else:
-                yo[j] = total.astype(bf16)
-        y_copy(j).start()
-
-    def stage2(j):
-        y_copy(j).wait_recv()
-        hold[j] = hold[j] + yi[j].astype(f32)
-
-    def flow_right(j):
-        @pl.when(z == 0)
-        def _():
-            to[0, j] = hold[j].astype(bf16)
-
-        @pl.when(z > 0)
-        def _():
-            right(j).wait_recv()
-            to[0, j] = (hold[j] + fr[j].astype(f32)).astype(bf16)
-
-        @pl.when(z < line - 1)
-        def _():
-            right(j).start()
-
-    def flow_left(j):
-        @pl.when(z == line - 1)
-        def _():
-            to[1, j] = hold[j].astype(bf16)
-
-        @pl.when(z < line - 1)
-        def _():
-            left(j).wait_recv()
-            to[1, j] = (hold[j] + fl[j].astype(f32)).astype(bf16)
-
-        @pl.when(z > 0)
-        def _():
-            left(j).start()
-
-    def total(j):
-        value = hold[j]
-        value = value + jnp.where(z > 0, fr[j].astype(f32), 0.0)
-        return value + jnp.where(z < line - 1, fl[j].astype(f32), 0.0)
-
-    def ranged(j, do_it):
-        pl.when((j >= 0) & (j < nmat))(functools.partial(do_it, j))
-
-    def tick(t):
-        ranged(t, stage0)
-        ranged(t - 1, stage1)
-        ranged(t - 3, stage2)
-        ranged(t - 4 - 2 * z, flow_right)
-        ranged(t - 4 - 2 * (line - 1 - z), flow_left)
-
-    def body(t, carry):
-        tick(t)
-        return carry
-
-    lax.fori_loop(0, nmat + 4 + 2 * (line - 1), body, 0)
-
+                came = rcopy(vz.at[slot_in], vz.at[slot_in], vzs.at[direction, step], vzr.at[slot_in], near)
+                pl.when(ok_send)(copy.wait_send)
+                pl.when(ok_recv)(came.wait_recv)
+
+        one(device(jnp.minimum(z + 1, line - 1), y, x, c), (z < line - 1) & (z - step >= 0), z - step - 1 >= 0, 0,
+            jnp.maximum(z - step, 0), jnp.maximum(z - step - 1, 0))
+        one(device(jnp.maximum(z - 1, 0), y, x, c), (z > 0) & (z + step <= line - 1), z + step + 1 <= line - 1, 1,
+            jnp.minimum(z + step, line - 1), jnp.minimum(z + step + 1, line - 1))
+
+    for step in range(line - 1):
+        vec_flow(step, True)
+        if done < ticks:
+            tick(done)
+            done += 1
+        vec_flow(step, False)
+    ticking(done, ticks)
+    total = vz[0]
+    for k in range(1, line):
+        total = total + vz[k]
+    vec_out[...] = total
+
+    def piece_total(j, h):
+        r = 2 * j + h
+        value = hold[r]
+        value = value + jnp.where(z > 0, fr[r].astype(F32), 0.0)
+        return value + jnp.where(z < line - 1, fl[r].astype(F32), 0.0)
+
+    deliver = rcopy(do, di, dsem.at[0], dsem.at[1], to_y)
     for s in range(cap):
-        do[s] = total(pick[(1 - y) * cap + s]).astype(bf16)
-    deliver = rcopy(do, di, dsem.at[0], dsem.at[1], to_y)
+        for h in range(2):
+            do[s, pl.ds(h * half, half), :] = piece_total(slot_pick[(1 - y) * cap + s], h).astype(BF16)
     deliver.start()
     for s in range(cap):
-        out[s, rows(y * quarter, quarter), :] = total(pick[y * cap + s])
+        for h in range(2):
+            sg[s, part(y, h), :] = piece_total(slot_pick[y * cap + s], h)
+    lay_x_came.wait_recv()
+    lay_d.start()
+
+    def finish(r, carry):
+        y_copy(r).wait_send()
+
+        @pl.when(z < line - 1)
+        def _():
+            right(r).wait_send()
+
+        @pl.when(z > 0)
+        def _():
+            left(r).wait_send()
+
+        return carry
+
+    lax.fori_loop(0, nchunk, finish, 0)
+
+    def last(j, carry):
+        core_copy(j, gqkv.at[0]).wait_send()
+        return carry
+
+    lax.fori_loop(0, nmat, last, 0)
+    for s in range(nseq):
+        gin_copy(s).wait_send()
+        gin_came(s).wait_recv()
+        gin_own(s).wait()
+    lay_x.wait_send()
+    lay_c.wait_send()
+    lay_c_came.wait_recv()
+    lay_own.wait()
+    lay_d.wait_send()
+    lay_d_came.wait_recv()
     deliver.wait_recv()
     for s in range(cap):
-        out[s, rows((1 - y) * quarter, quarter), :] = di[s].astype(f32)
+        sg[s, rows((1 - y) * quarter, quarter), :] = di[s].astype(F32)
     deliver.wait_send()
 
-    def finish(j, carry):
-        core_copy(j).wait_send()
-        y_copy(j).wait_send()
-
-        @pl.when(z < line - 1)
-        def _():
-            right(j).wait_send()
-
-        @pl.when(z > 0)
-        def _():
-            left(j).wait_send()
-
-        return carry
-
-    lax.fori_loop(0, nmat, finish, 0)
-
-
-def reduce_grads(owners, grads, line, order, cap):
-    nmat, both, width = grads.shape
-    share = both // 2
-    quarter = share // 2
-    bf16, f32 = jnp.bfloat16, jnp.float32
+
+def backward(owners, spans, vecs, flow, hidden, incoming, layer, k_own, v_own, line, cap):
+    nmat, width, _ = flow.shape
+    share = width // 4
+    own_rows = layer.shape[0]
+    both = 2 * own_rows
+    nseq = both // LEN
+    span_rows = nseq * SPAN_ROWS
+    ratio = (nmat - 4) // 2
+    quarter, half = share // 2, share // 4
+    n = 2 * nmat
+    pairs = width // (2 * HDIM)
     dma = pltpu.SemaphoreType.DMA
+    vmem = pl.BlockSpec(memory_space=pltpu.VMEM)
+    smem = pl.BlockSpec(memory_space=pltpu.SMEM)
+    hbm = pl.BlockSpec(memory_space=pl.ANY)
+    whole = jax.ShapeDtypeStruct(hidden.shape, BF16)
+
+    def lows(*shape):
+        return pltpu.VMEM(shape, BF16)
+
+    def wide(*shape):
+        return pltpu.VMEM(shape, F32)
+
     return pl.pallas_call(
-        functools.partial(reduce_kernel, line, order, cap),
-        out_shape=jax.ShapeDtypeStruct((cap, share, width), f32),
-        in_specs=[pl.BlockSpec(memory_space=pltpu.SMEM), pl.BlockSpec(memory_space=pltpu.VMEM)],
-        out_specs=pl.BlockSpec(memory_space=pltpu.VMEM),
+        functools.partial(backward_kernel, line, nmat, cap),
+        out_shape=(jax.ShapeDtypeStruct((cap, share, width), F32),
+                   jax.ShapeDtypeStruct(vecs.shape, F32), whole, whole),
+        in_specs=[smem, smem, vmem, hbm, hbm, hbm, hbm, hbm, hbm],
+        out_specs=(vmem, vmem, hbm, hbm),
         scratch_shapes=[
-            pltpu.VMEM((nmat, share, width), bf16),
-            pltpu.VMEM((nmat, quarter, width), f32),
-            pltpu.VMEM((nmat, quarter, width), bf16),
-            pltpu.VMEM((nmat, quarter, width), bf16),
-            pltpu.VMEM((nmat, quarter, width), bf16),
-            pltpu.VMEM((nmat, quarter, width), bf16),
-            pltpu.VMEM((2, nmat, quarter, width), bf16),
-            pltpu.VMEM((cap, quarter, width), bf16),
-            pltpu.VMEM((cap, quarter, width), bf16),
-            pltpu.SMEM((nmat,), jnp.int32),
+            lows(nmat, width, width), lows(both, width), lows(both, width), lows(both, width),
+            lows(nseq, SPAN_ROWS, LEN),
+            lows(nseq * pairs, 2 * SPAN_ROWS, LEN),
+            lows(span_rows, width), lows(span_rows, width), lows(span_rows, width), lows(span_rows, width),
+            wide(span_rows, width), wide(span_rows, 1), lows(span_rows, width), wide(span_rows, width),
+            lows(ratio, span_rows, width), lows(ratio, span_rows, width),
+            lows(span_rows, width), lows(span_rows, width), lows(3, 2 * share, width),
+            wide(*vecs.shape), wide(2, *vecs.shape), wide(line, *vecs.shape),
+            lows(nmat, share, width), wide(n, half, width), lows(n, half, width), lows(n, half, width),
+            lows(n, half, width), lows(cap, quarter, width), lows(cap, quarter, width),
             pltpu.SMEM((2 * cap,), jnp.int32),
-        ] + [dma((nmat,))] * 8 + [dma((2,))],
-        name="reduce_grads",
+            dma((nmat,)), dma((6,)), dma((3,)), dma((3,)), dma((nseq,)), dma((nseq,)), dma((1 + nseq,)),
+            dma((nmat,)), dma((nmat,)),
+        ] + [dma((n,))] * 6 + [dma((2,)), dma((2,)), dma((2,)), dma((2, line)), dma((line,))],
+        name="backward",
         compiler_params=pltpu.CompilerParams(
-            collective_id=2, has_side_effects=True, vmem_limit_bytes=56 * 1024 * 1024),
-    )(owners, grads)
+            collective_id=2, has_side_effects=True, vmem_limit_bytes=62 * 1024 * 1024),
+    )(owners, spans, vecs, flow, hidden, incoming, layer, k_own, v_own)
 
 
 STEP = 10
-SPAN_ROWS = 96
 MATRIX_RATE = 0.03
 VECTOR_RATE = 0.25
 BETA_ONE = 0.5
 BETA_TWO = 0.5
 DECAY = 0.01
 ADAM_EPS = 1e-08
-
-
-def norm_back(grad, normed, inverse, gain):
-    scaled = grad * gain
-    first = jnp.mean(scaled, axis=-1, keepdims=True)
-    second = jnp.mean(scaled * normed, axis=-1, keepdims=True)
-    return inverse * (scaled - first - normed * second)
-
-
-def gelu_slope(value):
-    cdf = 0.5 * (1.0 + lax.erf(value * 2.0 ** (-0.5)))
-    pdf = jnp.exp(-0.5 * value * value) * (2.0 * jnp.pi) ** (-0.5)
-    return cdf + value * pdf
 
 
 def adamw(weight, moment_one, moment_two, grad, step_rate):
@@ -603,129 +929,25 @@
     return (weight - step_rate * (direction + DECAY * weight), new_one, new_two)
 
 
-def dot(eq, a, b):
-    return jnp.einsum(eq, a, b, preferred_element_type=F32)
-
-
 def on_device(line, hidden_in, incoming, spans, owners, vectors, vec_one, vec_two, master_slots, slot_one, slot_two):
     cap, width, share = master_slots.shape
     nmat = owners.shape[0]
     ratio = (nmat - 4) // 2
-    scale = HDIM ** (-0.5)
-    heads = width // HDIM
-    rank_mp = lax.axis_index("mp")
-    rx, rc = rank_mp // 2, rank_mp % 2
-    tokens = hidden_in.shape[0]
-    own = tokens // 4
-    nseq = own // LEN
-    b_up = vectors[3:3 + ratio].reshape(4, ratio, share).transpose(1, 0, 2).reshape(ratio, width)
-    b_q, b_v, b_o, b_down = vectors[0], vectors[1], vectors[2], vectors[3 + ratio]
-    gain_one, shift_one, gain_two, shift_two = (vectors[4 + ratio + i] for i in range(4))
-
-    def split(v):
-        return v.reshape(-1, LEN, heads, HDIM)
-
-    def attend(block):
-        q_blk, k_blk, v_blk = block
-        scores = dot("qhd,khd->hqk", q_blk, k_blk) * scale
-        probs = jax.nn.softmax(scores, axis=-1)
-        return dot("hqk,khd->qhd", probs.astype(BF16), v_blk).astype(BF16)
-
-    vecs = jnp.concatenate([vectors[:3], b_up, vectors[3 + ratio:]], axis=0)
+
+    def regroup(value, first, second):
+        rows = value[3:3 + ratio].reshape(first, second, share).transpose(1, 0, 2).reshape(ratio, width)
+        return jnp.concatenate([value[:3], rows, value[3 + ratio:]], axis=0)
+
+    vecs = regroup(vectors, 4, ratio)
     flow, layer, k_own, v_own = forward(owners, jnp.transpose(master_slots, (0, 2, 1)), hidden_in, vecs, line)
-    layer = lax.all_gather(layer, "mp", axis=0, tiled=True)
-    where = flow_order(nmat)
-    pieces = [flow[where.index(p)] for p in range(nmat)]
-    wq, wk, wv, wo = pieces[:4]
-
-    def ours(v):
-        v = v.reshape((2, 2, v.shape[0] // 4) + v.shape[1:])
-        v = lax.dynamic_index_in_dim(v, rc, 1, keepdims=False)
-        return v.reshape((-1,) + v.shape[2:])
-    hid = ours(hidden_in)
-    inc = ours(incoming)
-    spn = ours(spans)
-    position = jnp.arange(LEN, dtype=jnp.int32)
-    starts = spn[:, :, 0][:, :, None]
-    ends = starts + spn[:, :, 1][:, :, None]
-    covered = jnp.any((position >= starts) & (position < ends), axis=1)
-    rank = jnp.cumsum(covered.astype(jnp.int32), axis=1) - 1
-    pick = ((rank[:, None, :] == jnp.arange(SPAN_ROWS)[None, :, None]) & covered[:, None, :]).astype(BF16)
-    hid_s = hid.reshape(-1, LEN, width)
-    ns = hid_s.shape[0]
-    hm = dot("sit,std->sid", pick, hid_s).astype(BF16).reshape(-1, width)
-    gm = dot("sit,std->sid", pick, inc.reshape(-1, LEN, width)).reshape(-1, width)
-    q = (dot("td,sd->ts", hm, wq) + b_q).astype(BF16)
-    k = dot("td,sd->ts", hid, wk).astype(BF16)
-    v = (dot("td,sd->ts", hid, wv) + b_v).astype(BF16)
-    q_s, k_s, v_s = q.reshape(ns, SPAN_ROWS, heads, HDIM), split(k), split(v)
-    probs = jax.nn.softmax(dot("sqhd,skhd->shqk", q_s, k_s) * scale, axis=-1)
-    pr = probs.astype(BF16)
-    ctx = dot("shqk,skhd->sqhd", pr, v_s).astype(BF16).reshape(-1, width)
-    y1, n1, i1 = layer_norm(hm.astype(F32) + dot("ts,so->to", ctx, wo) + b_o, gain_one, shift_one)
-    low = y1.astype(BF16)
-    second = y1 + b_down
-    acts, ups = [], []
-    for i in range(ratio):
-        up = dot("td,fd->tf", low, pieces[4 + i]) + b_up[i]
-        act = jax.nn.gelu(up, approximate=False).astype(BF16)
-        second = second + dot("tf,fo->to", act, pieces[4 + ratio + i])
-        ups.append(up)
-        acts.append(act)
-    _, n2, i2 = layer_norm(second, gain_two, shift_two)
-    grad_g2 = jnp.sum(gm * n2, axis=0)
-    grad_e2 = jnp.sum(gm, axis=0)
-    dh2 = norm_back(gm, n2, i2, gain_two)
-    df = dh2.astype(BF16)
-    grad_b2 = jnp.sum(df.astype(F32), axis=0)
-
-    def half(v):
-        return lax.dynamic_slice_in_dim(v, rx * 2 * share, 2 * share, 1)
-    grads = [None] * nmat
-    dy1 = dh2
-    b_rows = []
-    for i in range(ratio):
-        du = (dot("to,fo->tf", df, pieces[4 + ratio + i]) * gelu_slope(ups[i])).astype(BF16)
-        dy1 = dy1 + dot("tf,fd->td", du, pieces[4 + i])
-        b_rows.append(jnp.sum(du.astype(F32), axis=0))
-        grads[4 + i] = dot("tf,td->fd", half(du), low)
-        grads[4 + ratio + i] = dot("tf,to->fo", half(acts[i]), df)
-    grad_b1 = jnp.stack(b_rows).reshape(ratio, 4, share).transpose(1, 0, 2).reshape(ratio, width)
-    grad_g1 = jnp.sum(dy1 * n1, axis=0)
-    grad_e1 = jnp.sum(dy1, axis=0)
-    dh1 = norm_back(dy1, n1, i1, gain_one)
-    da = dh1.astype(BF16)
-    grad_bo = jnp.sum(da.astype(F32), axis=0)
-    grads[3] = dot("ts,to->so", half(ctx), da)
-    dctx = dot("to,so->ts", da, wo).astype(BF16).reshape(ns, SPAN_ROWS, heads, HDIM)
-    dp = dot("sqhd,skhd->shqk", dctx, v_s)
-    ds = (probs * (dp - jnp.sum(probs * dp, axis=-1, keepdims=True))).astype(BF16)
-    dq = (dot("shqk,skhd->sqhd", ds, k_s) * scale).astype(BF16).reshape(-1, width)
-    dk = (dot("shqk,sqhd->skhd", ds, q_s) * scale).astype(BF16).reshape(-1, width)
-    dv = dot("shqk,sqhd->skhd", pr, dctx).astype(BF16).reshape(-1, width)
-    grads[0] = dot("ts,td->sd", half(dq), hm)
-    grads[1] = dot("ts,td->sd", half(dk), hid)
-    grads[2] = dot("ts,td->sd", half(dv), hid)
-    grad_bq = jnp.sum(dq.astype(F32), axis=0)
-    grad_bv = jnp.sum(dv.astype(F32), axis=0)
-    back = (dh1 + dot("ts,sd->td", dq, wq)).astype(BF16).reshape(ns, SPAN_ROWS, width)
-    dx = dot("ts,sd->td", dk, wk) + dot("ts,sd->td", dv, wv) + dot("sit,sid->std", pick, back).reshape(-1, width)
-    dx = lax.dynamic_slice_in_dim(dx.astype(BF16), rx * own, own, 0)
-    grad_in = lax.all_gather(dx, "mp", axis=0, tiled=True)
-
-    vec_grad = jnp.concatenate([
-        jnp.stack([grad_bq, grad_bv, grad_bo]), grad_b1,
-        jnp.stack([grad_b2, grad_g1, grad_e1, grad_g2, grad_e2])], axis=0)
-    vec_total = lax.psum(vec_grad, ("dp", "mp")) * 0.5
-    new_vec = adamw(vectors, vec_one, vec_two, vec_total, VECTOR_RATE)
-
-    order = tuple(p for i in range(ratio) for p in (4 + ratio + i, 4 + i)) + (3, 0, 1, 2)
-    slot_grad = reduce_grads(owners, jnp.stack([grads[p] for p in order]).astype(BF16), line, order, cap)
+    slot_grad, vec_grad, layer_out, input_grad = backward(
+        owners, spans, vecs, flow, hidden_in, incoming, layer, k_own, v_own, line, cap)
+    new_vec = adamw(vectors, vec_one, vec_two, regroup(vec_grad, ratio, 4), VECTOR_RATE)
     slot_grad = jnp.transpose(slot_grad, (0, 2, 1))
     held = jnp.sum((owners == lax.axis_index("dp")).astype(jnp.int32))
     occupied = (jnp.arange(cap) < held).astype(F32)[:, None, None]
     new_slots = adamw(master_slots, slot_one, slot_two, slot_grad, MATRIX_RATE)
-    return (layer, grad_in) + new_vec + tuple(v * occupied for v in new_slots)
+    return (layer_out, input_grad) + new_vec + tuple(v * occupied for v in new_slots)
 
 
 def solution(mesh):

time: 454 us -> 249 us (0.55); the launches traced: 446 us -> 248 us
  matrix products: 120 us -> 0 us
  local copies, waits for them, and re-layouts: 65.6 us -> 11.1 us
  Pallas kernels: 184 us -> 224 us
  blocking collectives: 37.8 us -> 0 us
  between operations: 15 us -> 0.71 us
  other arithmetic: 23.2 us -> 12 us
    dot_general x45 -> x0, matrix products: 120 us -> none  [dot(): return jnp.einsum(eq, a, b, preferred_element_type=F32)]
    pallas_call x1, Pallas kernels: 83.5 us -> 123 us  [backward(): pl.pallas_call(functools.partial(backward_kernel, line, nmat, cap), out_s...]
    psum x1 -> x0, blocking collectives: 37.8 us -> none  [on_device(): vec_total = lax.psum(vec_grad, ('dp', 'mp')) * 0.5]
    reshape x12 -> x6, local copies, waits for them, and re-layouts: 18.5 us -> 0.37 us  [regroup(): value[3:3 + ratio].reshape(first, second, share).transpose(1, 0, 2)]
    unnamed x115 -> x19, local copies, waits for them, and re-layouts: 24.1 us -> 6.2 us
    convert_element_type x7 -> x0, local copies, waits for them, and re-layouts: 15.6 us -> none  [the longest x1 4.33 us: on_device(): dv = dot('shqk,sqhd->skhd', pr, dctx).astype(BF16).reshape(-1, width)]
    sub x1 -> x0, other arithmetic: 4.61 us -> none  [on_device(): probs = jax.nn.softmax(dot('sqhd,skhd->shqk', q_s, k_s) * scale, axis=-1)]
  transfers between devices with their start and end apart: 2 -> 0, of which waited for: 0 -> 0; matrix products, arithmetic and copies ran while one was open for 42% -> 0% of each run, Pallas kernels for 19% -> 0%
where the time goes in v3:
time: 249 us; the launch traced here: 248 us
  Pallas kernels  224 us (90%)
  other arithmetic  12 us (5%)
  local copies, waits for them, and re-layouts  11.1 us (4%)
    pallas_call x1, Pallas kernels, backward(): pl.pallas_call(functools.partial(backward_kernel, line, nmat, cap), out_s...  123 us
    pallas_call x1, Pallas kernels, forward(): pl.pallas_call(functools.partial(forward_kernel, line, nmat, cap), out_sh...  101 us
    mul x1, other arithmetic, on_device(): v * occupied  9.44 us
    unnamed x19, local copies, waits for them, and re-layouts  6.2 us

profile of v3, /device:TPU:0, one launch (start us, length us, event | category | flops | bytes accessed | tf_op | source)
XLA Modules:
  0.0 248.1 jit_solution(17436894539776977754)
XLA Ops:
  0.6 0.7 slice.19
  1.4 0.1 reshape.33
  1.5 0.1 reshape.34
  1.6 0.8 slice.20
  2.4 0.7 slice.18
  3.1 0.6 pad_maximum_fusion.vecs
  3.7 0.0 copy-start.4
  3.7 101.0 %forward.1 = (bf16[12,768,768]{2,1,0:T(8,128)(2,1)}, bf16[1024,768]{1,0:T(8,128)(2,1)}, bf16[1024,768]{1,0:T(8,128)(2,1)}, bf16[1024,768]{1,0:T(8,128)(2,1)}) custom-call(s32[12]{0:T(128)} %owners.3, f32[4,192,768]{2,1,0:T(8,128)} %bitcast.18, bf16[4096,768]{1,0:T(8,128)(2,1)} %hidden.3, f32[12,768]{1,0:T(8,128)} %pad_maximum_fusion.vecs), custom_call_target="tpu_custom_call" | custom-call | tf_op jit(solution)/shard_map/forward/pallas_call | solution.py:383
  104.8 0.0 copy-done.4
  104.8 0.8 copy.19.spans
  105.6 0.0 copy-start.1
  105.6 0.0 copy-start.2
  105.6 0.0 copy-start.3
  105.6 0.0 copy-start.5
  105.6 123.2 %backward.1 = (f32[4,192,768]{2,1,0:T(8,128)}, f32[12,768]{1,0:T(8,128)}, bf16[4096,768]{1,0:T(8,128)(2,1)}, bf16[4096,768]{1,0:T(8,128)(2,1)}) custom-call(s32[12]{0:T(128)} %owners.3, s32[8,24,2]{2,1,0:T(8,128)} %copy.19.spans, f32[12,768]{1,0:T(8,128)} %pad_maximum_fusion.vecs, bf16[12,768,768]{2,1,0:T(8,128)(2,1)} %get-tuple-element.16.flow, ...), custom_call_target="tpu_custom_call" | custom-call | tf_op jit(solution)/shard_map/backward/pallas_call | solution.py:887
  228.7 0.7 slice.22
  229.5 0.1 reshape.35
  229.6 0.1 reshape.36
  229.7 0.8 slice.23
  230.5 0.7 slice.21
  231.2 0.0 copy-done.1
  231.2 0.0 copy-done.2
  231.2 0.0 copy-done.3
  231.2 0.0 slice-start
  231.2 0.7 multiply_subtract_fusion
  231.9 0.0 copy-done.5
  231.9 0.6 fusion.2
  232.5 0.6 compare_convert_fusion
  233.2 0.0 copy-start
  233.2 0.0 slice-start.1
  233.2 9.4 %broadcast_multiply_fusion = (f32[4,768,192]{1,2,0:T(8,128)}, f32[4,768,192]{1,2,0:T(8,128)}, f32[4,768,192]{1,2,0:T(8,128)}) fusion(f32[4]{0:T(128)S(1)} %compare_convert_fusion, f32[4,192,768]{2,1,0:T(8,128)} %get-tuple-element.23, f32[4,768,192]{1,2,0:T(8,128)} %param.19, f32[4,768,192]{1,2,0:T(8,128)} %param.17, f32[4,768,192]{1,2,0:T(8,128)} %param.18), kind=kLoop, calls=%fused_computation.4 | loop fusion | flops 10027008 | bytes 16515088 | tf_op jit(solution)/shard_map/mul | solution.py:950
  242.7 0.0 copy-done
  242.7 2.7 %copy.27 = bf16[4096,768]{1,0:T(8,128)(2,1)} copy(bf16[4096,768]{1,0:T(8,128)(2,1)S(1)} %copy-done) | data formatting | bytes 12582912
  245.4 0.0 slice-done
  245.4 0.0 slice-done.1
  245.4 2.7 %copy.28 = bf16[4096,768]{1,0:T(8,128)(2,1)} copy(bf16[4096,768]{1,0:T(8,128)(2,1)S(1)} %bitcast.20) | data formatting | bytes 12582912
  (3 shorter events, 0.0 us)
Async XLA Ops:
  3.7 101.0 %copy-start.4 = (s32[8,24,2]{1,2,0:T(2,128)S(1)}, s32[8,24,2]{1,2,0:T(2,128)}, u32[]{:S(2)}) copy-start(s32[8,24,2]{1,2,0:T(2,128)} %param.12) | copy-start | bytes 4612
  105.6 125.6 %copy-start.1 = (f32[12,768]{1,0:T(8,128)S(1)}, f32[12,768]{1,0:T(8,128)}, u32[]{:S(2)}) copy-start(f32[12,768]{1,0:T(8,128)} %param.14) | copy-start | bytes 110596
  105.6 125.6 %copy-start.2 = (f32[12,768]{1,0:T(8,128)S(1)}, f32[12,768]{1,0:T(8,128)}, u32[]{:S(2)}) copy-start(f32[12,768]{1,0:T(8,128)} %param.15) | copy-start | bytes 110596
  105.6 125.6 %copy-start.3 = (f32[12,768]{1,0:T(8,128)S(1)}, f32[12,768]{1,0:T(8,128)}, u32[]{:S(2)}) copy-start(f32[12,768]{1,0:T(8,128)} %param.16) | copy-start | bytes 110596
  105.6 126.3 %copy-start.5 = (s32[12]{0:T(128)S(1)}, s32[12]{0:T(128)}, u32[]{:S(2)}) copy-start(s32[12]{0:T(128)} %owners.3) | copy-start | bytes 148
  231.2 14.2 %slice-start = ((s8[6291456]{0:T(1024)(128)(4,1)}), s8[2097152]{0:T(1024)(128)(4,1)S(1)}, s32[]{:S(2)}) async-start(s8[6291456]{0:T(1024)(128)(4,1)} %bitcast.19), calls=%async_computation | async-start | bytes 4194304
  233.2 9.5 %copy-start = (bf16[4096,768]{1,0:T(8,128)(2,1)S(1)}, bf16[4096,768]{1,0:T(8,128)(2,1)}, u32[]{:S(2)}) copy-start(bf16[4096,768]{1,0:T(8,128)(2,1)} %get-tuple-element.38) | copy-start | bytes 18874372
  233.2 12.2 %slice-start.1 = ((s8[6291456]{0:T(1024)(128)(4,1)}), s8[4194304]{0:T(1024)(128)(4,1)S(1)}, s32[]{:S(2)}) async-start(s8[6291456]{0:T(1024)(128)(4,1)} %bitcast.19), calls=%async_computation.1 | async-start | bytes 8388608

commit v4 on v3

v4 whole, which is shorter than its diff:
```python
import functools
import jax
import jax.numpy as jnp
from jax import lax
from jax.sharding import PartitionSpec as P
from jax.experimental import pallas as pl
from jax.experimental.pallas import tpu as pltpu

MESH = pl.DeviceIdType.MESH
BF16 = jnp.bfloat16
F32 = jnp.float32
LN_EPS = 1e-12
HDIM = 64
LEN = 512
NT = (((1,), (1,)), ((), ()))
NN = (((1,), (0,)), ((), ()))
TN = (((0,), (0,)), ((), ()))


def dg(left, right, dims):
    return lax.dot_general(left, right, dims, preferred_element_type=F32)


def flow_order(nmat):
    ratio = (nmat - 4) // 2
    return (0, 1, 2, 3) + tuple(p for k in range(ratio) for p in (4 + k, 4 + ratio + k))


def layer_norm(value, gain, shift):
    center = value - jnp.mean(value, axis=-1, keepdims=True)
    inverse = lax.rsqrt(jnp.mean(center * center, axis=-1, keepdims=True) + LN_EPS)
    normed = center * inverse
    return normed * gain + shift, normed, inverse


def gelu(value):
    return 0.5 * value * (1.0 + lax.erf(value * 2.0 ** (-0.5)))


def place():
    dp, mp = lax.axis_index("dp"), lax.axis_index("mp")
    return dp // 2, dp % 2, mp // 2, mp % 2


def device(z, y, x, c):
    return (z * 2 + y, x * 2 + c)


def greet(line):
    z, y, x, c = place()
    bar = pltpu.get_barrier_semaphore()
    for who in (device(z, 1 - y, x, c), device(z, y, 1 - x, c), device(z, y, x, 1 - c)):
        pl.semaphore_signal(bar, inc=1, device_id=who, device_id_type=MESH)

    @pl.when(z > 0)
    def _():
        pl.semaphore_signal(bar, inc=1, device_id=device(z - 1, y, x, c), device_id_type=MESH)

    @pl.when(z < line - 1)
    def _():
        pl.semaphore_signal(bar, inc=1, device_id=device(z + 1, y, x, c), device_id_type=MESH)

    peers = 3 + jnp.where(z > 0, 1, 0) + jnp.where(z < line - 1, 1, 0)
    pl.semaphore_wait(bar, peers.astype(jnp.int32))


def rcopy(src, dst, send, recv, who):
    return pltpu.make_async_remote_copy(
        src_ref=src, dst_ref=dst, send_sem=send, recv_sem=recv, device_id=who, device_id_type=MESH
    )


SPAN_ROWS = 96


def rows(start, size):
    return pl.ds(pl.multiple_of(start, 16), size)


def column_sum(value):
    return jnp.sum(value, axis=0, keepdims=True)


def regroup(src, dst, ratio, share):
    dst[...] = src[...]
    for j in range(ratio):
        for k in range(ratio):
            dst[3 + k:4 + k, j * share:(j + 1) * share] = src[3 + j:4 + j, k * share:(k + 1) * share]


def norm_back(grad, normed, inverse, gain):
    scaled = grad * gain
    first = jnp.mean(scaled, axis=-1, keepdims=True)
    second = jnp.mean(scaled * normed, axis=-1, keepdims=True)
    return inverse * (scaled - first - normed * second)


def stacked(value, left_half):
    zero = jnp.zeros_like(value)
    return jnp.concatenate([jnp.where(left_half, value, zero), jnp.where(left_half, zero, value)], axis=0)


def merged(value, left_half):
    size = left_half.shape[0]
    return jnp.where(left_half, value[:size], value[size:])


def forward_kernel(line, nmat, cap, owners, spans, slots_in, hidden, incoming, vectors,
                   out, layer_out, k_out, v_out, pick_out, probs_out, hm_out, qm_out, ctx_out, low_out,
                   act_out, slope_out, n1_out, inv_out, df_out, dh_out, gvec,
                   vecs, full, slots, ys, stage, fr, fl, hid, q_ref, k_ref, v_ref, ctx, low, acc,
                   pick, probs, hm, gm, qm, act, slope, n1, inv1, df, zo, idx,
                   in_sem, out_sem, slot_send, slot_recv, sr, rl, sl, rr, xs, xr, ysd, yr, ds, dr, cs, cr, loc):
    share = slots.shape[1]
    quarter = share // 2
    half = quarter // 2
    nchunk = 2 * nmat
    z, y, x, c = place()
    me = 2 * x + c
    over = 2 * (1 - x) + c
    to_y, to_x, to_c = device(z, 1 - y, x, c), device(z, y, 1 - x, c), device(z, y, x, 1 - c)
    greet(line)
    ratio = (nmat - 4) // 2
    order = flow_order(nmat)
    own_rows = q_ref.shape[0]
    width = vecs.shape[1]
    regroup(vectors, vecs, ratio, share)
    per = own_rows // LEN
    nseq = 2 * per

    def block_copy(src, dst, b, sem):
        return pltpu.make_async_copy(
            src.at[rows((2 * b + c) * own_rows, own_rows)], dst.at[pl.ds(b * own_rows, own_rows)], sem)

    slot_loads = [pltpu.make_async_copy(slots_in.at[s], acc.at[pl.ds(s * share, share)], in_sem.at[4 + s])
                  for s in range(cap)]
    loads = [block_copy(hidden, hid, b, in_sem.at[b]) for b in range(2)]
    loads += [block_copy(incoming, v_ref, b, in_sem.at[2 + b]) for b in range(2)]
    for copy in slot_loads + loads:
        copy.start()

    def slot_copy(s):
        return rcopy(
            slots.at[s, pl.ds(pl.multiple_of((1 - y) * quarter, 16), quarter), :],
            ys[s].at[y], slot_send.at[s], slot_recv.at[s], to_y)

    for s in range(cap):
        slot_loads[s].wait()
        slots[s] = acc[pl.ds(s * share, share), :].astype(BF16)
        slot_copy(s).start()
        ys[s][y] = slots[s, pl.ds(pl.multiple_of(y * quarter, 16), quarter), :]
    for j, p in enumerate(order):
        mine = owners[p]
        place_of = jnp.int32(0)
        for q in range(p):
            place_of += jnp.where(owners[q] == mine, 1, 0).astype(jnp.int32)
        zo[j] = mine // 2
        idx[j] = (mine % 2) * cap + jnp.minimum(place_of, cap - 1)

    def piece_rows(block, yy, h):
        return pl.ds(pl.multiple_of(block * share + yy * quarter + h * half, 16), half)

    def own(r):
        at = pl.ds(pl.multiple_of((r % 2) * half, 16), half)
        slot, half_of = idx[r // 2] % cap, idx[r // 2] // cap
        stage[...] = ys[0][half_of, at, :]
        for s in range(1, cap):
            @pl.when(r // 2 >= s)
            def _():
                stage[...] = jnp.where(slot == s, ys[s][half_of, at, :], stage[...])

        return stage[...]

    def right(r):
        return rcopy(fr.at[r], fr.at[r], sr.at[r], rl.at[r], device(z + 1, y, x, c))

    def left(r):
        return rcopy(fl.at[r], fl.at[r], sl.at[r], rr.at[r], device(z - 1, y, x, c))

    def x_copy(f):
        at = full.at[f // 2, piece_rows(me, y, f % 2), :]
        return rcopy(at, at, xs.at[f], xr.at[f], to_x)

    def x_came(f):
        at = full.at[f // 2, piece_rows(over, y, f % 2), :]
        return rcopy(at, at, xs.at[f], xr.at[f], to_x)

    def y_copy(f):
        at = full.at[f // 2, piece_rows(me, y, f % 2), :]
        return rcopy(at, at, ysd.at[f], yr.at[f], to_y)

    def y_came(f):
        at = full.at[f // 2, piece_rows(me, 1 - y, f % 2), :]
        return rcopy(at, at, ysd.at[f], yr.at[f], to_y)

    def diag_x(f):
        at = full.at[f // 2, piece_rows(me, 1 - y, f % 2), :]
        return rcopy(at, at, ds.at[f], dr.at[f], to_x)

    def diag_y(f):
        at = full.at[f // 2, piece_rows(over, y, f % 2), :]
        return rcopy(at, at, ds.at[f], dr.at[f], to_y)

    def diag_came(f):
        at = full.at[f // 2, piece_rows(over, 1 - y, f % 2), :]
        return rcopy(at, at, ds.at[f], dr.at[f], to_x)

    def core_copy(p, k):
        block = jnp.where(k == 0, me, over) if not isinstance(k, int) else (me, over)[k]
        at = full.at[p, pl.ds(pl.multiple_of(block * share, 16), share), :]
        return rcopy(at, at, cs.at[p, k], cr.at[p, k], to_c)

    def core_came(p, k):
        block = (2 * x + 1 - c, 2 * (1 - x) + 1 - c)[k]
        at = full.at[p, pl.ds(pl.multiple_of(block * share, 16), share), :]
        return rcopy(at, at, cs.at[p, k], cr.at[p, k], to_c)

    def keep(p):
        return pltpu.make_async_copy(full.at[p], out.at[p], loc.at[p])

    lag0 = 2 * (line - 1)
    lag1 = lag0 + 3
    lag2 = lag1 + 3
    lag3 = lag2 + 1

    def slot_came(s):
        rcopy(slots.at[s, pl.ds(pl.multiple_of((1 - y) * quarter, 16), quarter), :],
              ys[s].at[1 - y], slot_send.at[s], slot_recv.at[s], to_y).wait_recv()

    def tick(t):
        for s in range(cap):
            pl.when(t == 2 * s)(functools.partial(slot_came, s))

        r = t - 2 * z

        @pl.when((r >= 0) & (r < nchunk))
        def _():
            @pl.when(z == 0)
            def _():
                fr[r] = own(r)

            @pl.when(z > 0)
            def _():
                right(r).wait_recv()
                fr[r] = jnp.where(zo[r // 2] == z, own(r), fr[r])

            @pl.when(z < line - 1)
            def _():
                right(r).start()

        l = t - 2 * (line - 1 - z)

        @pl.when((l >= 0) & (l < nchunk))
        def _():
            @pl.when(z == line - 1)
            def _():
                fl[l] = own(l)

            @pl.when(z < line - 1)
            def _():
                left(l).wait_recv()
                fl[l] = jnp.where(zo[l // 2] == z, own(l), fl[l])

            @pl.when(z > 0)
            def _():
                left(l).start()

        f = t - lag0

        @pl.when((f >= 0) & (f < nchunk))
        def _():
            full[f // 2, piece_rows(me, y, f % 2), :] = jnp.where(zo[f // 2] <= z, fr[f], fl[f])
            x_copy(f).start()
            y_copy(f).start()

        g = t - lag1

        @pl.when((g >= 0) & (g < nchunk))
        def _():
            x_came(g).wait_recv()
            y_came(g).wait_recv()

            @pl.when(g % 2 == 0)
            def _():
                diag_x(g).start()

            @pl.when(g % 2 == 1)
            def _():
                diag_y(g).start()

        e = t - lag2

        @pl.when((e >= 0) & (e < nchunk))
        def _():
            diag_came(e).wait_recv()

            @pl.when(e % 2 == 1)
            def _():
                for k in range(2):
                    core_copy(e // 2, k).start()

        w = t - lag3

        @pl.when((w >= 0) & (w < nchunk) & (w % 2 == 1))
        def _():
            for k in range(2):
                core_came(w // 2, k).wait_recv()
            keep(w // 2).start()

    ticks = nchunk + lag3

    def ticking(start, count):
        def body(i, carry):
            tick(start + i)
            return carry

        if count > 0:
            lax.fori_loop(0, count, body, 0)

    position = lax.broadcasted_iota(jnp.int32, (8, LEN), 1)
    row_of = lax.broadcasted_iota(jnp.int32, (SPAN_ROWS, LEN), 0).astype(F32)

    def cover(s, carry):
        seq = (2 * (s // per) + c) * per + s % per
        seen = jnp.zeros((8, LEN), F32)
        for n in range(spans.shape[2]):
            start, size = spans[0, seq, n], spans[1, seq, n]
            seen = jnp.where((position >= start) & (position < start + size), 1.0, seen)
        upper = (lax.broadcasted_iota(jnp.int32, (LEN, LEN), 0)
                 <= lax.broadcasted_iota(jnp.int32, (LEN, LEN), 1)).astype(F32).astype(BF16)
        rank = dg(seen.astype(BF16), upper, NN)
        chosen = jnp.where((rank[0:1, :] - 1.0 == row_of) & (seen[0:1, :] > 0.0), 1.0, 0.0).astype(BF16)
        pick[s] = chosen
        at, span = rows(s * LEN, LEN), rows(s * SPAN_ROWS, SPAN_ROWS)
        hm[span, :] = dg(chosen, hid[at, :], NN).astype(BF16)
        gm[span, :] = dg(chosen, v_ref[at, :], NN).astype(BF16)
        tick(nseq + s)
        return carry

    ticking(0, nseq)
    for copy in loads:
        copy.wait()
    lax.fori_loop(0, nseq, cover, 0)
    kept = []

    def keep_out(src, dst):
        copy = pltpu.make_async_copy(src, dst, out_sem.at[len(kept)])
        copy.start()
        kept.append(copy)

    keep_out(pick, pick_out)
    keep_out(hm, hm_out)

    now = lag3 + 2
    ticking(2 * nseq, now - 2 * nseq)
    for i in range(per):
        block = hid[rows(x * own_rows + i * LEN, LEN), :]
        q_ref[pl.ds(i * LEN, LEN), :] = (
            (dg(block, full[0], NT) + vecs[0:1, :]).astype(BF16) * jnp.asarray(HDIM ** -0.5, BF16))
    tick(now)
    qm[...] = (dg(hm[...], full[0], NT) + vecs[0:1, :]).astype(BF16)
    keep_out(qm, qm_out)
    tick(now + 1)
    now += 2

    def project_k(s, carry):
        at = rows(s * LEN, LEN)
        k_ref[at, :] = dg(hid[at, :], full[1], NT).astype(BF16)
        pl.when(s % 2 == 1)(lambda: tick(now_k + s // 2))
        return carry

    def project_v(s, carry):
        at = rows(s * LEN, LEN)
        v_ref[at, :] = (dg(hid[at, :], full[2], NT) + vecs[1:2, :]).astype(BF16)
        pl.when(s % 2 == 1)(lambda: tick(now_v + s // 2))
        return carry

    now_k = now
    lax.fori_loop(0, nseq, project_k, 0)
    keep_out(k_ref, k_out)
    now_v = now_k + nseq // 2
    lax.fori_loop(0, nseq, project_v, 0)
    keep_out(v_ref, v_out)
    now = now_v + nseq // 2

    pairs = width // (2 * HDIM)
    left_half = lax.broadcasted_iota(jnp.int32, (LEN, 2 * HDIM), 1) < HDIM
    ones = jnp.ones((LEN, 2 * HDIM), BF16)

    def lanes_of(pair):
        return pl.ds(pl.multiple_of(pair * (2 * HDIM), 2 * HDIM), 2 * HDIM)

    def attend(i):
        at, lanes = rows((i // pairs) * LEN, LEN), lanes_of(i % pairs)
        both = rows(x * own_rows + (i // pairs) * LEN, LEN)
        q_blk, k_blk = q_ref[at, lanes], k_ref[both, lanes]
        v_blk = jnp.concatenate([v_ref[both, lanes], ones], axis=1)
        mixed = []
        for h in range(2):
            q_one = jnp.where(left_half if h == 0 else ~left_half, q_blk, jnp.zeros_like(q_blk))
            scores = dg(q_one, k_blk, NT)
            raised = jnp.exp(scores - jnp.max(scores, axis=-1, keepdims=True)).astype(BF16)
            sums = dg(raised, v_blk, NN)
            mixed.append(sums[:, :2 * HDIM] / sums[:, 2 * HDIM:])
        ctx[at, lanes] = jnp.where(left_half, mixed[0], mixed[1]).astype(BF16)

    group = 3

    def attend_step(i, carry):
        for j in range(group):
            attend(i * group + j)
        tick(now + i)
        return carry

    count = per * pairs // group
    lax.fori_loop(0, count, attend_step, 0)
    now += count

    left_span = lax.broadcasted_iota(jnp.int32, (SPAN_ROWS, 2 * HDIM), 1) < HDIM
    scale = HDIM ** -0.5

    def attend_span(i):
        s, lanes = i // pairs, lanes_of(i % pairs)
        at, span = rows(s * LEN, LEN), rows(s * SPAN_ROWS, SPAN_ROWS)
        scores = dg(stacked(qm[span, lanes], left_span), k_ref[at, lanes], NT) * scale
        raised = jnp.exp(scores - jnp.max(scores, axis=-1, keepdims=True))
        value = (raised / jnp.sum(raised, axis=-1, keepdims=True)).astype(BF16)
        probs[i] = value
        ctx[rows(own_rows + s * SPAN_ROWS, SPAN_ROWS), lanes] = merged(
            dg(value, v_ref[at, lanes], NN), left_span).astype(BF16)

    span_group = pairs

    def span_step(i, carry):
        for j in range(span_group):
            attend_span(i * span_group + j)
        tick(now + i)
        return carry

    lax.fori_loop(0, nseq, span_step, 0)
    now += nseq
    keep_out(probs, probs_out)
    span_rows = nseq * SPAN_ROWS
    all_rows = own_rows + span_rows
    spanned = pl.ds(own_rows, span_rows)
    keep_out(ctx.at[spanned], ctx_out)

    def mix(residual, at):
        h1 = residual.astype(F32) + dg(ctx[at, :], full[3], NN) + vecs[2:3, :]
        value, normed, inverse = layer_norm(h1, vecs[4 + ratio:5 + ratio, :], vecs[5 + ratio:6 + ratio, :])
        low[at, :] = value.astype(BF16)
        acc[at, :] = value + vecs[3 + ratio:4 + ratio, :]
        return normed, inverse

    for i in range(per):
        mix(hid[rows(x * own_rows + i * LEN, LEN), :], pl.ds(i * LEN, LEN))
    normed, inverse = mix(hm[...], spanned)
    n1[...] = normed
    inv1[...] = jnp.broadcast_to(inverse, inv1.shape)
    keep_out(n1, n1_out)
    keep_out(inv1, inv_out)
    keep_out(low.at[spanned], low_out)
    tick(now)
    now += 1

    tile = all_rows // 2
    ready = [lag3 + 2 * (5 + 2 * k) + 2 for k in range(ratio)]
    for k in range(ratio):
        for i in range(2):
            if i == 0:
                ticking(now, max(0, ready[k] - now))
                now = max(now, ready[k])
            at = pl.ds(i * tile, tile)
            up = dg(low[at, :], full[4 + 2 * k], NT) + vecs[3 + k:4 + k, :]
            cdf = 0.5 * (1.0 + lax.erf(up * 2.0 ** (-0.5)))
            active = (up * cdf).astype(BF16)
            acc[at, :] = acc[at, :] + dg(active, full[5 + 2 * k], NN)
            if i == 1:
                up, cdf = up[tile - span_rows:], cdf[tile - span_rows:]
                act[k] = active[tile - span_rows:]
                slope[k] = (cdf + up * (jnp.exp(-0.5 * up * up) * (2.0 * jnp.pi) ** (-0.5))).astype(BF16)
            if now < ticks:
                tick(now)
                now += 1
    ticking(now, max(0, ticks - now))
    keep_out(act, act_out)
    keep_out(slope, slope_out)

    _, normed, inverse = layer_norm(
        acc[spanned, :], vecs[6 + ratio:7 + ratio, :], vecs[7 + ratio:8 + ratio, :])
    given = gm[...].astype(F32)
    gvec[...] = jnp.zeros_like(gvec)
    gvec[6 + ratio:7 + ratio, :] = column_sum(given * normed)
    gvec[7 + ratio:8 + ratio, :] = column_sum(given)
    back = norm_back(given, normed, inverse, vecs[6 + ratio:7 + ratio, :])
    df[...] = back.astype(BF16)
    gvec[3 + ratio:4 + ratio, :] = column_sum(back.astype(BF16).astype(F32))
    acc[spanned, :] = back
    keep_out(df, df_out)
    keep_out(acc.at[spanned], dh_out)
    for i in range(per):
        at = pl.ds(i * LEN, LEN)
        q_ref[at, :] = layer_norm(
            acc[at, :], vecs[6 + ratio:7 + ratio, :], vecs[7 + ratio:8 + ratio, :])[0].astype(BF16)
    keep_out(q_ref, layer_out)
    for copy in kept:
        copy.wait()

    def finish(r, carry):
        @pl.when(z < line - 1)
        def _():
            right(r).wait_send()

        @pl.when(z > 0)
        def _():
            left(r).wait_send()

        x_copy(r).wait_send()
        y_copy(r).wait_send()
        diag_came(r).wait_send()
        return carry

    lax.fori_loop(0, nchunk, finish, 0)

    def last(p, carry):
        for k in range(2):
            core_copy(p, k).wait_send()
        keep(p).wait()
        return carry

    lax.fori_loop(0, nmat, last, 0)
    for s in range(cap):
        slot_copy(s).wait_send()


def forward(owners, spans, slots, hidden, incoming, vecs, line):
    cap, share, width = slots.shape
    nmat = owners.shape[0]
    ratio = (nmat - 4) // 2
    own_rows = hidden.shape[0] // 4
    quarter, half = share // 2, share // 4
    n = 2 * nmat
    nseq = 2 * own_rows // LEN
    span_rows = nseq * SPAN_ROWS
    pairs = width // (2 * HDIM)
    dma = pltpu.SemaphoreType.DMA
    vmem = pl.BlockSpec(memory_space=pltpu.VMEM)
    smem = pl.BlockSpec(memory_space=pltpu.SMEM)
    hbm = pl.BlockSpec(memory_space=pl.ANY)

    def lows(*shape):
        return jax.ShapeDtypeStruct(shape, BF16)

    def wide(*shape):
        return jax.ShapeDtypeStruct(shape, F32)

    own, both, span = lows(own_rows, width), lows(2 * own_rows, width), lows(span_rows, width)
    outs = (lows(nmat, 4 * share, width), own, both, both, lows(nseq, SPAN_ROWS, LEN),
            lows(nseq * pairs, 2 * SPAN_ROWS, LEN), span, span, span, span,
            lows(ratio, span_rows, width), lows(ratio, span_rows, width),
            wide(span_rows, width), wide(span_rows, 128), span, wide(span_rows, width), wide(*vecs.shape))
    held = (outs[0], lows(cap, share, width)) + (lows(2, quarter, width),) * cap + (
        lows(half, width), lows(n, half, width), lows(n, half, width), both, own, both, both,
        lows(own_rows + span_rows, width), lows(own_rows + span_rows, width), wide(own_rows + span_rows, width),
        outs[4], outs[5], span, span, span, outs[10], outs[11], outs[12], outs[13], span)
    scratch = [pltpu.VMEM(h.shape, h.dtype) for h in held]
    scratch = [pltpu.VMEM(vecs.shape, F32)] + scratch[:2] + [scratch[2:2 + cap]] + scratch[2 + cap:]
    return pl.pallas_call(
        functools.partial(forward_kernel, line, nmat, cap),
        out_shape=outs,
        in_specs=[smem, smem, hbm, hbm, hbm, vmem],
        out_specs=(hbm,) * (len(outs) - 1) + (vmem,),
        scratch_shapes=scratch + [
            pltpu.SMEM((nmat,), jnp.int32), pltpu.SMEM((nmat,), jnp.int32),
            dma((4 + cap,)), dma((16,)), dma((cap,)), dma((cap,)),
        ] + [dma((n,))] * 10 + [dma((nmat, 2)), dma((nmat, 2)), dma((nmat,))],
        name="forward",
        compiler_params=pltpu.CompilerParams(
            collective_id=1, has_side_effects=True, vmem_limit_bytes=60 * 1024 * 1024),
    )(owners, spans, slots, hidden, incoming, vecs)


def backward_kernel(line, nmat, cap, owners, vectors, flow, hidden, layer, k_in, v_in, pick_in, probs_in,
                    hm_in, qm_in, ctx_in, low_in, act_in, slope_in, n1_in, inv_in, df_in, dh_in, gvec_in,
                    sg, vec_out, lay, gin,
                    vecs, full, hid, k_ref, v_ref, pick, probs, hm, qm, ctx, low, act, slope, n1, inv1, df, acc,
                    dq, gqkv, gvec, vin, vz, cin, hold, yi, fr, fl, do, di, slot_pick, far_pick, far_at,
                    w_sem, act_sem, in_sem, lsem_s, lsem_r, gsem_s, gsem_r, loc_sem,
                    cs, cr, ysd, yr, sr, rl, sl, rr, dss, dsr, vs, vr, vzs, vzr):
    ratio = (nmat - 4) // 2
    width = vecs.shape[1]
    share = cin.shape[1]
    quarter, half = share // 2, share // 4
    nchunk = 2 * nmat
    z, y, x, c = place()
    me, over = 2 * x + c, 2 * (1 - x) + c
    to_y, to_x, to_c = device(z, 1 - y, x, c), device(z, y, 1 - x, c), device(z, y, x, 1 - c)
    own_rows = layer.shape[0]
    nseq = 2 * own_rows // LEN
    per = own_rows // LEN
    greet(line)
    regroup(vectors, vecs, ratio, share)

    def load(src, dst, sem):
        return pltpu.make_async_copy(src, dst, in_sem.at[sem])

    def weight(j):
        return pltpu.make_async_copy(flow.at[j], full.at[j], w_sem.at[j])

    def block_copy(b):
        return load(hidden.at[rows((2 * b + c) * own_rows, own_rows)],
                    hid.at[pl.ds(b * own_rows, own_rows)], 14 + b)

    first_loads = [load(src, dst, i) for i, (src, dst) in enumerate(((df_in, df), (low_in, low), (dh_in, acc)))]
    next_loads = [load(src, dst, 5 + i) for i, (src, dst) in enumerate(
        ((n1_in, n1), (inv_in, inv1), (ctx_in, ctx)))]
    late_loads = [load(src, dst, 8 + i) for i, (src, dst) in enumerate(
        ((probs_in, probs), (k_in, k_ref), (v_in, v_ref), (qm_in, qm), (hm_in, hm), (pick_in, pick)))]
    late_loads += [block_copy(b) for b in range(2)]
    def chunk_loads(k):
        return [weight(5 + 2 * k), pltpu.make_async_copy(slope_in.at[k], slope.at[k], act_sem.at[0, k]),
                weight(4 + 2 * k), pltpu.make_async_copy(act_in.at[k], act.at[k], act_sem.at[1, k])]

    for copy in first_loads:
        copy.start()
    for k in range(ratio):
        for copy in chunk_loads(k):
            copy.start()

    def lay_rows(b):
        return lay.at[rows(b * own_rows, own_rows)]

    lay_x = rcopy(layer, lay_rows(me), lsem_s.at[0], lsem_r.at[0], to_x)
    lay_x_came = rcopy(layer, lay_rows(over), lsem_s.at[0], lsem_r.at[0], to_x)
    lay_c = rcopy(layer, lay_rows(me), lsem_s.at[1], lsem_r.at[1], to_c)
    lay_c_came = rcopy(layer, lay_rows(2 * x + 1 - c), lsem_s.at[1], lsem_r.at[1], to_c)
    lay_d = rcopy(lay_rows(over), lay_rows(over), lsem_s.at[2], lsem_r.at[2], to_c)
    lay_d_came = rcopy(layer, lay_rows(2 * (1 - x) + 1 - c), lsem_s.at[2], lsem_r.at[2], to_c)
    own_block = k_ref.at[pl.ds(0, own_rows)]
    lay_in = pltpu.make_async_copy(layer, own_block, loc_sem.at[1 + nseq])
    lay_own = pltpu.make_async_copy(own_block, lay_rows(me), loc_sem.at[0])
    lay_x.start()
    lay_c.start()

    order = tuple(p for k in range(ratio) for p in (4 + ratio + k, 4 + k)) + (3, 0, 1, 2)
    for s in range(2 * cap):
        slot_pick[s] = -1
        far_pick[s] = -1
        far_at[s] = 0
    for j, p in enumerate(order):
        mine = owners[p]
        place_of, later = jnp.int32(0), jnp.int32(0)
        for q in range(p):
            place_of += jnp.where(owners[q] == mine, 1, 0).astype(jnp.int32)
        for q in order[j + 1:]:
            later += jnp.where(owners[q] == mine, 1, 0).astype(jnp.int32)
        slot = (mine % 2) * cap + jnp.minimum(place_of, cap - 1)
        when = cap - 1 - jnp.minimum(later, cap - 1)
        for s in range(2 * cap):
            slot_pick[s] = jnp.where((mine // 2 == z) & (slot == s), j, slot_pick[s])
            far_at[s] = jnp.where((mine // 2 == z) & (slot == s), when, far_at[s])
            far_pick[s] = jnp.where((mine // 2 == z) & ((mine % 2) * cap + when == s), j, far_pick[s])

    def core_copy(j, src):
        return rcopy(src.at[rows((1 - c) * share, share), :], cin.at[j], cs.at[j], cr.at[j], to_c)

    def grad_of(j):
        if isinstance(j, int) and j >= 2 * ratio + 1:
            return gqkv.at[j - 2 * ratio - 1]
        if isinstance(j, int) and j == 2 * ratio:
            return full.at[3]
        return full.at[4 + j + 1 - 2 * (j % 2), pl.ds(0, 2 * share), :]

    def part(at, h):
        return rows(at * quarter + h * half, half)

    def y_copy(r):
        return rcopy(cin.at[r // 2, part(1 - y, r % 2), :], yi.at[r], ysd.at[r], yr.at[r], to_y)

    def right(r):
        return rcopy(yi.at[r], fr.at[r], sr.at[r], rl.at[r], device(z + 1, y, x, c))

    def left(r):
        return rcopy(cin.at[r // 2, part(y, r % 2), :], fl.at[r], sl.at[r], rr.at[r], device(z - 1, y, x, c))

    def stage1(r):
        j, h = r // 2, r % 2

        @pl.when(h == 0)
        def _():
            core_copy(j, gqkv.at[0]).wait_recv()

        def add(src):
            for at in (1 - y, y):
                value = (src[rows(c * share + at * quarter + h * half, half), :].astype(F32)
                         + cin[j, part(at, h), :].astype(F32))
                if at is y:
                    hold[r] = value
                else:
                    cin[j, part(at, h), :] = value.astype(BF16)

        @pl.when(j < 2 * ratio)
        def _():
            add(full.at[4 + j + 1 - 2 * (j % 2)])

        @pl.when(j == 2 * ratio)
        def _():
            add(full.at[3])

        @pl.when(j > 2 * ratio)
        def _():
            add(gqkv.at[j - 2 * ratio - 1])

        y_copy(r).start()

    def stage2(r):
        y_copy(r).wait_recv()
        hold[r] = hold[r] + yi[r].astype(F32)

    def flow_right(r):
        @pl.when(z == 0)
        def _():
            yi[r] = hold[r].astype(BF16)

        @pl.when(z > 0)
        def _():
            right(r).wait_recv()
            yi[r] = (hold[r] + fr[r].astype(F32)).astype(BF16)

        @pl.when(z < line - 1)
        def _():
            right(r).start()

    def flow_left(r):
        at = part(y, r % 2)

        @pl.when(z == line - 1)
        def _():
            cin[r // 2, at, :] = hold[r].astype(BF16)

        @pl.when(z < line - 1)
        def _():
            left(r).wait_recv()
            cin[r // 2, at, :] = (hold[r] + fl[r].astype(F32)).astype(BF16)

        @pl.when(z > 0)
        def _():
            left(r).start()

    def ranged(r, do_it):
        pl.when((r >= 0) & (r < nchunk))(functools.partial(do_it, r))

    lag, skew = 5, 3
    flown = lag + skew * (line - 1)
    ticks = nchunk + flown

    def piece_total(j, h):
        r = 2 * j + h
        value = hold[r]
        value = value + jnp.where(z > 0, fr[r].astype(F32), 0.0)
        return value + jnp.where(z < line - 1, fl[r].astype(F32), 0.0)

    def deliver(s):
        return rcopy(do.at[s], di.at[s], dss.at[s], dsr.at[s], to_y)

    def settle(j):
        for h in range(2):
            value = piece_total(j, h)
            for s in range(cap):
                sg[s, part(y, h), :] = jnp.where(slot_pick[y * cap + s] == j, value, sg[s, part(y, h), :])

                @pl.when(j <= nmat - cap + s)
                def _():
                    at = pl.ds(h * half, half)
                    do[s, at, :] = jnp.where(far_pick[(1 - y) * cap + s] == j, value.astype(BF16), do[s, at, :])

        for s in range(cap):
            pl.when(j == nmat - cap + s)(lambda s=s: deliver(s).start())

    def tick(t):
        ranged(t, stage1)
        ranged(t - 4, stage2)
        ranged(t - lag - skew * z, flow_right)
        ranged(t - lag - skew * (line - 1 - z), flow_left)
        late = t - flown
        pl.when((late >= 0) & (late < nchunk) & (late % 2 == 1))(lambda: settle(late // 2))

    def ticking(start, stop):
        def body(t, carry):
            tick(t)
            return carry

        lax.fori_loop(start, stop, body, 0)

    gvec[...] = gvec_in[...]
    sg[...] = jnp.zeros_like(sg)
    do[...] = jnp.zeros_like(do)
    for copy in first_loads:
        copy.wait()
    lay_in.start()
    halves = pl.ds(pl.multiple_of(x * 2 * share, 128), 2 * share)

    def feed_back(k, carry):
        for copy in chunk_loads(k):
            copy.wait()

        @pl.when(k == 0)
        def _():
            for j in (3, 0, 1, 2):
                weight(j).start()
            lay_in.wait()
            lay_own.start()
            lay_own.wait()
            for copy in next_loads + late_loads:
                copy.start()

        d_up = (dg(df[...], full[5 + 2 * k], NT) * slope[k].astype(F32)).astype(BF16)
        gvec[pl.ds(3 + k, 1), :] = column_sum(d_up.astype(F32))
        acc[...] = acc[...] + dg(d_up, full[4 + 2 * k], NN)
        act_k = act[k, :, halves]
        act[k] = d_up
        full[5 + 2 * k, pl.ds(0, 2 * share), :] = dg(act_k, df[...], TN).astype(BF16)
        core_copy(2 * k, full.at[5 + 2 * k]).start()
        full[4 + 2 * k, pl.ds(0, 2 * share), :] = dg(act[k, :, halves], low[...], TN).astype(BF16)
        core_copy(2 * k + 1, full.at[4 + 2 * k]).start()
        tick(2 * k)
        tick(2 * k + 1)
        return carry

    lax.fori_loop(0, ratio, feed_back, 0)
    done = 2 * ratio
    weight(3).wait()
    for copy in next_loads:
        copy.wait()
    gvec[4 + ratio:5 + ratio, :] = column_sum(acc[...] * n1[...])
    gvec[5 + ratio:6 + ratio, :] = column_sum(acc[...])
    back = norm_back(acc[...], n1[...], inv1[:, 0:1], vecs[4 + ratio:5 + ratio, :])
    acc[...] = back
    da = back.astype(BF16)
    gvec[2:3, :] = column_sum(da.astype(F32))
    df[...] = da
    low[...] = dg(da, full[3], NT).astype(BF16)
    full[3, pl.ds(0, 2 * share), :] = dg(ctx[:, halves], da, TN).astype(BF16)
    core_copy(2 * ratio, full.at[3]).start()
    ticking(done, done + 2)
    done += 2

    for copy in late_loads:
        copy.wait()
    pairs = width // (2 * HDIM)
    left_half = lax.broadcasted_iota(jnp.int32, (SPAN_ROWS, 2 * HDIM), 1) < HDIM
    scale = HDIM ** -0.5

    def attend_back(i):
        s, pair = i // pairs, i % pairs
        at, span = rows(s * LEN, LEN), rows(s * SPAN_ROWS, SPAN_ROWS)
        lanes = pl.ds(pl.multiple_of(pair * (2 * HDIM), 2 * HDIM), 2 * HDIM)
        d_two = stacked(low[span, lanes], left_half)
        given = probs[i]
        value = given.astype(F32)
        keys = k_ref[at, lanes]
        d_probs = dg(d_two, v_ref[at, lanes], NT)
        mean = jnp.sum(value * d_probs, axis=-1, keepdims=True)
        ds = (value * (d_probs - mean)).astype(BF16)
        dq[span, lanes] = (merged(dg(ds, keys, NN), left_half) * scale).astype(BF16)
        k_ref[at, lanes] = (dg(ds, stacked(qm[span, lanes], left_half), TN) * scale).astype(BF16)
        v_ref[at, lanes] = dg(given, d_two, TN).astype(BF16)

    base_back = done

    def back_step(i, carry):
        for j in range(pairs // 2):
            attend_back(i * (pairs // 2) + j)
        tick(base_back + i)
        return carry

    lax.fori_loop(0, 2 * nseq, back_step, 0)
    done += 2 * nseq
    gvec[0:1, :] = column_sum(dq[...].astype(F32))
    gqkv[0] = dg(dq[:, halves], hm[...], TN).astype(BF16)
    core_copy(2 * ratio + 1, gqkv.at[0]).start()
    for which, src in ((1, k_ref), (2, v_ref)):
        def some(i, carry, src=src):
            at = rows(i * LEN, LEN)
            return carry + dg(src[at, halves], hid[at, :], TN)

        gqkv[which] = lax.fori_loop(0, nseq, some, jnp.zeros((2 * share, width), F32)).astype(BF16)
        core_copy(2 * ratio + 1 + which, gqkv.at[which]).start()
        stop = min(2 * (2 * ratio + 2 + which), done + 3)
        ticking(done, stop)
        done = stop

    def sum_v(i, carry):
        return carry + column_sum(v_ref[rows(i * LEN, LEN), :].astype(F32))

    gvec[1:2, :] = lax.fori_loop(0, nseq, sum_v, jnp.zeros((1, width), F32))

    def vec_copy(k, who_to):
        return rcopy(gvec, vin.at[k], vs.at[k], vr.at[k], who_to)

    vec_copy(0, to_c).start()
    for j in range(3):
        weight(j).wait()
    qm[...] = (acc[...] + dg(dq[...], full[0], NN)).astype(BF16)
    def gin_rows(s, core):
        return gin.at[rows((2 * (s // per) + core) * own_rows + (s % per) * LEN, LEN)]

    def gin_copy(s):
        return rcopy(hid.at[rows(s * LEN, LEN)], gin_rows(s, c), gsem_s.at[s], gsem_r.at[s], to_c)

    def gin_came(s):
        return rcopy(hid.at[rows(s * LEN, LEN)], gin_rows(s, 1 - c), gsem_s.at[s], gsem_r.at[s], to_c)

    def gin_own(s):
        return pltpu.make_async_copy(hid.at[rows(s * LEN, LEN)], gin_rows(s, c), loc_sem.at[1 + s])

    def vec_flow(step, send):
        def one(near, ok_send, ok_recv, direction, slot_out, slot_in):
            copy = rcopy(vz.at[slot_out], vz.at[slot_out], vzs.at[direction, step], vzr.at[slot_out], near)
            if send:
                pl.when(ok_send)(copy.start)
            else:
                came = rcopy(vz.at[slot_in], vz.at[slot_in], vzs.at[direction, step], vzr.at[slot_in], near)
                pl.when(ok_send)(copy.wait_send)
                pl.when(ok_recv)(came.wait_recv)

        one(device(jnp.minimum(z + 1, line - 1), y, x, c), (z < line - 1) & (z - step >= 0), z - step - 1 >= 0, 0,
            jnp.maximum(z - step, 0), jnp.maximum(z - step - 1, 0))
        one(device(jnp.maximum(z - 1, 0), y, x, c), (z > 0) & (z + step <= line - 1), z + step + 1 <= line - 1, 1,
            jnp.minimum(z + step, line - 1), jnp.minimum(z + step + 1, line - 1))

    def vec_step(i):
        if i == 0:
            vec_copy(0, to_c).wait()
            gvec[...] = gvec[...] + vin[0]
            vec_copy(1, to_y).start()
        elif i == 1:
            vec_copy(1, to_y).wait()
            vz[z] = gvec[...] + vin[1]
        if 2 <= i <= line:
            vec_flow(i - 2, False)
        if 1 <= i <= line - 1:
            vec_flow(i - 1, True)

    for s in range(nseq):
        at, span = pl.ds(s * LEN, LEN), pl.ds(s * SPAN_ROWS, SPAN_ROWS)
        total = dg(k_ref[at, :], full[1], NN) + dg(v_ref[at, :], full[2], NN) + dg(pick[s], qm[span, :], TN)
        hid[at, :] = total.astype(BF16)
        gin_copy(s).start()
        gin_own(s).start()
        vec_step(s)
        stop = min(ticks, done + 2)
        ticking(done, stop)
        done = stop
    for i in range(nseq, line + 1):
        vec_step(i)
        stop = min(ticks, done + 1)
        ticking(done, stop)
        done = stop
    ticking(done, ticks)
    total = vz[0]
    for k in range(1, line):
        total = total + vz[k]
    gvec[...] = total
    regroup(gvec, vec_out, ratio, share)

    lay_x_came.wait_recv()
    lay_d.start()

    def finish(r, carry):
        y_copy(r).wait_send()

        @pl.when(z < line - 1)
        def _():
            right(r).wait_send()

        @pl.when(z > 0)
        def _():
            left(r).wait_send()

        return carry

    lax.fori_loop(0, nchunk, finish, 0)

    def last(j, carry):
        core_copy(j, gqkv.at[0]).wait_send()
        return carry

    lax.fori_loop(0, nmat, last, 0)
    for s in range(nseq):
        gin_copy(s).wait_send()
        gin_came(s).wait_recv()
        gin_own(s).wait()
    lay_x.wait_send()
    lay_c.wait_send()
    lay_c_came.wait_recv()
    lay_d.wait_send()
    lay_d_came.wait_recv()
    for s in range(cap):
        deliver(s).wait()
    for s in range(cap):
        sg[s, rows((1 - y) * quarter, quarter), :] = di[far_at[y * cap + s]].astype(F32)


def backward(owners, vecs, saved, hidden, line, cap):
    flow, layer, *kept, gvec = saved
    nmat, width, _ = flow.shape
    share = width // 4
    nseq = 2 * layer.shape[0] // LEN
    span_rows = nseq * SPAN_ROWS
    quarter, half = share // 2, share // 4
    n = 2 * nmat
    dma = pltpu.SemaphoreType.DMA
    vmem = pl.BlockSpec(memory_space=pltpu.VMEM)
    smem = pl.BlockSpec(memory_space=pltpu.SMEM)
    hbm = pl.BlockSpec(memory_space=pl.ANY)
    whole = jax.ShapeDtypeStruct(hidden.shape, BF16)

    def lows(*shape):
        return pltpu.VMEM(shape, BF16)

    def wide(*shape):
        return pltpu.VMEM(shape, F32)

    k, v, pick, probs, hm, qm, ctx, low, act, slope, n1, inv1, df, dh = (
        pltpu.VMEM(value.shape, value.dtype) for value in kept)
    return pl.pallas_call(
        functools.partial(backward_kernel, line, nmat, cap),
        out_shape=(jax.ShapeDtypeStruct((cap, share, width), F32),
                   jax.ShapeDtypeStruct(vecs.shape, F32), whole, whole),
        in_specs=[smem, vmem, hbm, hbm] + [hbm] * (1 + len(kept)) + [vmem],
        out_specs=(vmem, vmem, hbm, hbm),
        scratch_shapes=[
            wide(*vecs.shape), lows(nmat, width, width), lows(2 * layer.shape[0], width), k, v, pick, probs, hm, qm, ctx, low,
            act, slope, n1, inv1, df, dh,
            lows(span_rows, width), lows(3, 2 * share, width),
            wide(*vecs.shape), wide(2, *vecs.shape), wide(line, *vecs.shape),
            lows(nmat, share, width), wide(n, half, width), lows(n, half, width), lows(n, half, width),
            lows(n, half, width), lows(cap, quarter, width), lows(cap, quarter, width),
            pltpu.SMEM((2 * cap,), jnp.int32), pltpu.SMEM((2 * cap,), jnp.int32), pltpu.SMEM((2 * cap,), jnp.int32),
            dma((nmat,)), dma((2, (nmat - 4) // 2)), dma((16,)), dma((3,)), dma((3,)), dma((nseq,)), dma((nseq,)), dma((2 + nseq,)),
            dma((nmat,)), dma((nmat,)),
        ] + [dma((n,))] * 6 + [dma((cap,)), dma((cap,)), dma((2,)), dma((2,)), dma((2, line)), dma((line,))],
        name="backward",
        compiler_params=pltpu.CompilerParams(
            collective_id=2, has_side_effects=True, vmem_limit_bytes=60 * 1024 * 1024),
    )(owners, vecs, flow, hidden, layer, *kept, gvec)


STEP = 10
MATRIX_RATE = 0.03
VECTOR_RATE = 0.25
BETA_ONE = 0.5
BETA_TWO = 0.5
DECAY = 0.01
ADAM_EPS = 1e-08


def adamw(weight, moment_one, moment_two, grad, step_rate):
    new_one = BETA_ONE * moment_one + (1.0 - BETA_ONE) * grad
    new_two = BETA_TWO * moment_two + (1.0 - BETA_TWO) * grad * grad
    corr_one = 1.0 - BETA_ONE**STEP
    corr_two = 1.0 - BETA_TWO**STEP
    direction = new_one / corr_one / (jnp.sqrt(new_two / corr_two) + ADAM_EPS)
    return (weight - step_rate * (direction + DECAY * weight), new_one, new_two)


def on_device(line, hidden_in, incoming, spans, owners, vectors, vec_one, vec_two, master_slots, slot_one, slot_two):
    cap, width, share = master_slots.shape
    nmat = owners.shape[0]
    saved = forward(
        owners, jnp.transpose(spans, (2, 0, 1)), jnp.transpose(master_slots, (0, 2, 1)), hidden_in, incoming, vectors, line)
    slot_grad, vec_grad, layer_out, input_grad = backward(owners, vectors, saved, hidden_in, line, cap)
    new_vec = adamw(vectors, vec_one, vec_two, vec_grad, VECTOR_RATE)
    slot_grad = jnp.transpose(slot_grad, (0, 2, 1))
    held = jnp.sum((owners == lax.axis_index("dp")).astype(jnp.int32))
    occupied = (jnp.arange(cap) < held).astype(F32)[:, None, None]
    new_slots = adamw(master_slots, slot_one, slot_two, slot_grad, MATRIX_RATE)
    return (layer_out, input_grad) + new_vec + tuple(v * occupied for v in new_slots)


def solution(mesh):
    line = mesh.shape["dp"] // 2
    rows, slots = P("dp", None), P("dp", None, "mp")
    return jax.shard_map(
        functools.partial(on_device, line),
        mesh=mesh,
        in_specs=(rows, rows, P("dp", None, None), P(), P(), P(), P(), slots, slots, slots),
        out_specs=(rows, rows, P(), P(), P(), slots, slots, slots),
        check_vma=False,
    )
```

time: 249 us -> 212 us (0.85); the launches traced: 248 us -> 208 us
  Pallas kernels: 224 us -> 187 us
    pallas_call x1, Pallas kernels: 123 us -> 87.2 us  [backward(): pl.pallas_call(functools.partial(backward_kernel, line, nmat, cap), out_s...]
    slice x6 -> x0, local copies, waits for them, and re-layouts: 4.57 us -> none  [the longest x4 3.08 us: regroup(): return jnp.concatenate([value[:3], rows, value[3 + ratio:]], axis=0)]
    unnamed x19 -> x23, local copies, waits for them, and re-layouts: 6.2 us -> 8.71 us
where the time goes in v4:
time: 212 us; the launch traced here: 208 us
  Pallas kernels  187 us (88%)
  other arithmetic  11.2 us (5%)
  local copies, waits for them, and re-layouts  8.71 us (4%)
    pallas_call x1, Pallas kernels, forward(): pl.pallas_call(functools.partial(forward_kernel, line, nmat, cap), out_sh...  100 us
    pallas_call x1, Pallas kernels, backward(): pl.pallas_call(functools.partial(backward_kernel, line, nmat, cap), out_s...  87.2 us
    mul x1, other arithmetic, on_device(): v * occupied  9.09 us
    unnamed x23, local copies, waits for them, and re-layouts  8.71 us

profile of v4, /device:TPU:0, one launch (start us, length us, event | category | flops | bytes accessed | tf_op | source)
XLA Modules:
  0.0 208.3 jit_solution(7273686512318509571)
XLA Ops:
  0.6 1.3 copy.20
  1.9 100.2 %forward.1 = (bf16[12,768,768]{2,1,0:T(8,128)(2,1)}, bf16[1024,768]{1,0:T(8,128)(2,1)}, bf16[2048,768]{1,0:T(8,128)(2,1)}, bf16[2048,768]{1,0:T(8,128)(2,1)}, bf...) custom-call(s32[12]{0:T(128)} %owners.3, ...), custom_call_target="tpu_custom_call" | custom-call | tf_op jit(solution)/shard_map/forward/pallas_call | solution.py:568
  102.2 0.0 copy-start.5
  102.2 0.0 copy-start
  102.2 87.2 %backward.1 = (f32[4,192,768]{2,1,0:T(8,128)}, f32[12,768]{1,0:T(8,128)}, bf16[4096,768]{1,0:T(8,128)(2,1)}, bf16[4096,768]{1,0:T(8,128)(2,1)}) custom-call(s32[12]{0:T(128)} %owners.3, f32[12,768]{1,0:T(8,128)} %vectors.3, bf16[12,768,768]{2,1,0:T(8,128)(2,1)} %get-tuple-element.29.flow, bf16[4096,768]{1,0:T(8,128)(2,1)} %hidden.3, ...), custom_call_target="tpu_custom_call" | custom-call | tf_op jit(solution)/shard_map/backward/pallas_call | solution.py:1027
  189.4 0.0 copy-done.5
  189.4 0.6 fusion.2
  190.1 0.0 slice-start.2
  190.1 0.8 compare_convert_fusion
  190.9 0.0 copy-done
  190.9 0.0 copy-start.1
  190.9 0.0 copy-start.2
  190.9 0.0 copy-start.3
  190.9 0.0 copy-start.4
  190.9 0.0 slice-start.3
  190.9 9.1 %broadcast_multiply_fusion = (f32[4,768,192]{1,2,0:T(8,128)}, f32[4,768,192]{1,2,0:T(8,128)}, f32[4,768,192]{1,2,0:T(8,128)}) fusion(f32[4]{0:T(128)S(1)} %compare_convert_fusion, f32[4,192,768]{2,1,0:T(8,128)} %get-tuple-element.49, f32[4,768,192]{1,2,0:T(8,128)} %param.19, f32[4,768,192]{1,2,0:T(8,128)S(1)} %copy-done, f32[4,768,192]{1,2,0:T(8,128)} %param.18), kind=kLoop, calls=%fused_computation.4 | loop fusion | flops 10027008 | bytes 16515088 | tf_op jit(solution)/shard_map/mul | solution.py:1079
  200.0 0.0 copy-done.1
  200.0 0.0 copy-done.2
  200.0 0.0 copy-done.3
  200.0 0.0 copy-done.4
  200.0 0.0 slice-start
  200.1 0.7 multiply_subtract_fusion
  200.7 0.0 slice-done.2
  200.7 0.0 slice-done.3
  200.7 0.0 slice-start.1
  200.7 3.2 %copy.23 = bf16[4096,768]{1,0:T(8,128)(2,1)} copy(bf16[4096,768]{1,0:T(8,128)(2,1)S(1)} %bitcast.19) | data formatting | bytes 12582912
  203.9 0.0 slice-done
  203.9 1.5 slice-done.1
  205.4 2.7 %copy.24 = bf16[4096,768]{1,0:T(8,128)(2,1)} copy(bf16[4096,768]{1,0:T(8,128)(2,1)S(1)} %bitcast.17) | data formatting | bytes 12582912
  (2 shorter events, 0.0 us)
Async XLA Ops:
  102.2 87.2 %copy-start.5 = (s32[12]{0:T(128)S(1)}, s32[12]{0:T(128)}, u32[]{:S(2)}) copy-start(s32[12]{0:T(128)} %owners.3) | copy-start | bytes 148
  102.2 88.7 %copy-start = (f32[4,768,192]{1,2,0:T(8,128)S(1)}, f32[4,768,192]{1,2,0:T(8,128)}, u32[]{:S(2)}) copy-start(f32[4,768,192]{1,2,0:T(8,128)} %param.17) | copy-start | bytes 7077892
  190.1 10.7 %slice-start.2 = ((s8[6291456]{0:T(1024)(128)(4,1)}), s8[4194304]{0:T(1024)(128)(4,1)S(1)}, s32[]{:S(2)}) async-start(s8[6291456]{0:T(1024)(128)(4,1)} %bitcast.18), calls=%async_computation.2 | async-start | bytes 8388608
  190.9 9.2 %copy-start.1 = (f32[12,768]{1,0:T(8,128)S(1)}, f32[12,768]{1,0:T(8,128)}, u32[]{:S(2)}) copy-start(f32[12,768]{1,0:T(8,128)} %vectors.3) | copy-start | bytes 110596
  190.9 9.1 %copy-start.2 = (f32[12,768]{1,0:T(8,128)S(1)}, f32[12,768]{1,0:T(8,128)}, u32[]{:S(2)}) copy-start(f32[12,768]{1,0:T(8,128)} %param.15) | copy-start | bytes 110596
  190.9 9.1 %copy-start.3 = (f32[12,768]{1,0:T(8,128)S(1)}, f32[12,768]{1,0:T(8,128)}, u32[]{:S(2)}) copy-start(f32[12,768]{1,0:T(8,128)} %param.16) | copy-start | bytes 110596
  190.9 9.1 %copy-start.4 = (f32[12,768]{1,0:T(8,128)S(1)}, f32[12,768]{1,0:T(8,128)}, u32[]{:S(2)}) copy-start(f32[12,768]{1,0:T(8,128)} %get-tuple-element.48) | copy-start | bytes 110596
  190.9 9.8 %slice-start.3 = ((s8[6291456]{0:T(1024)(128)(4,1)}), s8[2097152]{0:T(1024)(128)(4,1)S(1)}, s32[]{:S(2)}) async-start(s8[6291456]{0:T(1024)(128)(4,1)} %bitcast.18), calls=%async_computation.3 | async-start | bytes 4194304
  200.0 3.9 %slice-start = ((s8[6291456]{0:T(1024)(128)(4,1)}), s8[4194304]{0:T(1024)(128)(4,1)S(1)}, s32[]{:S(2)}) async-start(s8[6291456]{0:T(1024)(128)(4,1)} %bitcast.16), calls=%async_computation | async-start | bytes 8388608
  200.7 4.7 %slice-start.1 = ((s8[6291456]{0:T(1024)(128)(4,1)}), s8[2097152]{0:T(1024)(128)(4,1)S(1)}, s32[]{:S(2)}) async-start(s8[6291456]{0:T(1024)(128)(4,1)} %bitcast.16), calls=%async_computation.1 | async-start | bytes 4194304

commit v5 on v4

--- a/solution.py
+++ b/solution.py
@@ -479,12 +479,13 @@
                 up, cdf = up[tile - span_rows:], cdf[tile - span_rows:]
                 act[k] = active[tile - span_rows:]
                 slope[k] = (cdf + up * (jnp.exp(-0.5 * up * up) * (2.0 * jnp.pi) ** (-0.5))).astype(BF16)
+            if i == 1:
+                keep_out(act.at[k], act_out.at[k])
+                keep_out(slope.at[k], slope_out.at[k])
             if now < ticks:
                 tick(now)
                 now += 1
     ticking(now, max(0, ticks - now))
-    keep_out(act, act_out)
-    keep_out(slope, slope_out)
 
     _, normed, inverse = layer_norm(
         acc[spanned, :], vecs[6 + ratio:7 + ratio, :], vecs[7 + ratio:8 + ratio, :])
@@ -572,7 +573,7 @@
         out_specs=(hbm,) * (len(outs) - 1) + (vmem,),
         scratch_shapes=scratch + [
             pltpu.SMEM((nmat,), jnp.int32), pltpu.SMEM((nmat,), jnp.int32),
-            dma((4 + cap,)), dma((16,)), dma((cap,)), dma((cap,)),
+            dma((4 + cap,)), dma((13 + 2 * ratio,)), dma((cap,)), dma((cap,)),
         ] + [dma((n,))] * 10 + [dma((nmat, 2)), dma((nmat, 2)), dma((nmat,))],
         name="forward",
         compiler_params=pltpu.CompilerParams(
@@ -952,6 +953,8 @@
         stop = min(ticks, done + 2)
         ticking(done, stop)
         done = stop
+    lay_x_came.wait_recv()
+    lay_d.start()
     for i in range(nseq, line + 1):
         vec_step(i)
         stop = min(ticks, done + 1)
@@ -964,8 +967,6 @@
     gvec[...] = total
     regroup(gvec, vec_out, ratio, share)
 
-    lay_x_came.wait_recv()
-    lay_d.start()
 
     def finish(r, carry):
         y_copy(r).wait_send()

time: 212 us -> 212 us (level)
  no operation moved by 1% of the time
where the time goes in v5:
time: 212 us; the launch traced here: 208 us
  Pallas kernels  187 us (88%)
  other arithmetic  11.2 us (5%)
  local copies, waits for them, and re-layouts  8.71 us (4%)
    pallas_call x1, Pallas kernels, forward(): pl.pallas_call(functools.partial(forward_kernel, line, nmat, cap), out_sh...  100 us
    pallas_call x1, Pallas kernels, backward(): pl.pallas_call(functools.partial(backward_kernel, line, nmat, cap), out_s...  87.2 us
    mul x1, other arithmetic, on_device(): v * occupied  9.09 us
    unnamed x23, local copies, waits for them, and re-layouts  8.71 us

profile of v5, /device:TPU:0, one launch (start us, length us, event | category | flops | bytes accessed | tf_op | source)
XLA Modules:
  0.0 208.4 jit_solution(759290361134737147)
XLA Ops:
  0.6 1.3 copy.20
  1.9 100.3 %forward.1 = (bf16[12,768,768]{2,1,0:T(8,128)(2,1)}, bf16[1024,768]{1,0:T(8,128)(2,1)}, bf16[2048,768]{1,0:T(8,128)(2,1)}, bf16[2048,768]{1,0:T(8,128)(2,1)}, bf...) custom-call(s32[12]{0:T(128)} %owners.3, ...), custom_call_target="tpu_custom_call" | custom-call | tf_op jit(solution)/shard_map/forward/pallas_call | solution.py:569
  102.2 0.0 copy-start.5
  102.2 0.0 copy-start
  102.3 87.2 %backward.1 = (f32[4,192,768]{2,1,0:T(8,128)}, f32[12,768]{1,0:T(8,128)}, bf16[4096,768]{1,0:T(8,128)(2,1)}, bf16[4096,768]{1,0:T(8,128)(2,1)}) custom-call(s32[12]{0:T(128)} %owners.3, f32[12,768]{1,0:T(8,128)} %vectors.3, bf16[12,768,768]{2,1,0:T(8,128)(2,1)} %get-tuple-element.29.flow, bf16[4096,768]{1,0:T(8,128)(2,1)} %hidden.3, ...), custom_call_target="tpu_custom_call" | custom-call | tf_op jit(solution)/shard_map/backward/pallas_call | solution.py:1028
  189.5 0.0 copy-done.5
  189.5 0.6 fusion.2
  190.1 0.0 slice-start.2
  190.1 0.8 compare_convert_fusion
  190.9 0.0 copy-done
  190.9 0.0 copy-start.1
  190.9 0.0 copy-start.2
  190.9 0.0 copy-start.3
  191.0 0.0 copy-start.4
  191.0 0.0 slice-start.3
  191.0 9.1 %broadcast_multiply_fusion = (f32[4,768,192]{1,2,0:T(8,128)}, f32[4,768,192]{1,2,0:T(8,128)}, f32[4,768,192]{1,2,0:T(8,128)}) fusion(f32[4]{0:T(128)S(1)} %compare_convert_fusion, f32[4,192,768]{2,1,0:T(8,128)} %get-tuple-element.49, f32[4,768,192]{1,2,0:T(8,128)} %param.19, f32[4,768,192]{1,2,0:T(8,128)S(1)} %copy-done, f32[4,768,192]{1,2,0:T(8,128)} %param.18), kind=kLoop, calls=%fused_computation.4 | loop fusion | flops 10027008 | bytes 16515088 | tf_op jit(solution)/shard_map/mul | solution.py:1080
  200.1 0.0 copy-done.1
  200.1 0.0 copy-done.2
  200.1 0.0 copy-done.3
  200.1 0.0 copy-done.4
  200.1 0.0 slice-start
  200.1 0.7 multiply_subtract_fusion
  200.8 0.0 slice-done.2
  200.8 0.0 slice-done.3
  200.8 0.0 slice-start.1
  200.8 3.2 %copy.23 = bf16[4096,768]{1,0:T(8,128)(2,1)} copy(bf16[4096,768]{1,0:T(8,128)(2,1)S(1)} %bitcast.19) | data formatting | bytes 12582912
  204.0 0.0 slice-done
  204.0 1.5 slice-done.1
  205.4 2.7 %copy.24 = bf16[4096,768]{1,0:T(8,128)(2,1)} copy(bf16[4096,768]{1,0:T(8,128)(2,1)S(1)} %bitcast.17) | data formatting | bytes 12582912
  (2 shorter events, 0.0 us)
Async XLA Ops:
  102.2 87.2 %copy-start.5 = (s32[12]{0:T(128)S(1)}, s32[12]{0:T(128)}, u32[]{:S(2)}) copy-start(s32[12]{0:T(128)} %owners.3) | copy-start | bytes 148
  102.2 88.7 %copy-start = (f32[4,768,192]{1,2,0:T(8,128)S(1)}, f32[4,768,192]{1,2,0:T(8,128)}, u32[]{:S(2)}) copy-start(f32[4,768,192]{1,2,0:T(8,128)} %param.17) | copy-start | bytes 7077892
  190.1 10.7 %slice-start.2 = ((s8[6291456]{0:T(1024)(128)(4,1)}), s8[4194304]{0:T(1024)(128)(4,1)S(1)}, s32[]{:S(2)}) async-start(s8[6291456]{0:T(1024)(128)(4,1)} %bitcast.18), calls=%async_computation.2 | async-start | bytes 8388608
  190.9 9.2 %copy-start.1 = (f32[12,768]{1,0:T(8,128)S(1)}, f32[12,768]{1,0:T(8,128)}, u32[]{:S(2)}) copy-start(f32[12,768]{1,0:T(8,128)} %vectors.3) | copy-start | bytes 110596
  190.9 9.1 %copy-start.2 = (f32[12,768]{1,0:T(8,128)S(1)}, f32[12,768]{1,0:T(8,128)}, u32[]{:S(2)}) copy-start(f32[12,768]{1,0:T(8,128)} %param.15) | copy-start | bytes 110596
  190.9 9.1 %copy-start.3 = (f32[12,768]{1,0:T(8,128)S(1)}, f32[12,768]{1,0:T(8,128)}, u32[]{:S(2)}) copy-start(f32[12,768]{1,0:T(8,128)} %param.16) | copy-start | bytes 110596
  191.0 9.1 %copy-start.4 = (f32[12,768]{1,0:T(8,128)S(1)}, f32[12,768]{1,0:T(8,128)}, u32[]{:S(2)}) copy-start(f32[12,768]{1,0:T(8,128)} %get-tuple-element.48) | copy-start | bytes 110596
  191.0 9.8 %slice-start.3 = ((s8[6291456]{0:T(1024)(128)(4,1)}), s8[2097152]{0:T(1024)(128)(4,1)S(1)}, s32[]{:S(2)}) async-start(s8[6291456]{0:T(1024)(128)(4,1)} %bitcast.18), calls=%async_computation.3 | async-start | bytes 4194304
  200.1 3.9 %slice-start = ((s8[6291456]{0:T(1024)(128)(4,1)}), s8[4194304]{0:T(1024)(128)(4,1)S(1)}, s32[]{:S(2)}) async-start(s8[6291456]{0:T(1024)(128)(4,1)} %bitcast.16), calls=%async_computation | async-start | bytes 8388608
  200.8 4.7 %slice-start.1 = ((s8[6291456]{0:T(1024)(128)(4,1)}), s8[2097152]{0:T(1024)(128)(4,1)S(1)}, s32[]{:S(2)}) async-start(s8[6291456]{0:T(1024)(128)(4,1)} %bitcast.16), calls=%async_computation.1 | async-start | bytes 4194304
